TPU v7x, 128 devices: a whole 4x4x4 slice. The times are simulated.
128 devices in a mesh: sample: 4 (over z_hi, core), expert: 32 (over y, x, z_lo).
Axes of the slice: x: 4, y: 4, z: 4 (z_hi: 2, z_lo: 2; z = z_hi * 2 + z_lo), core: 2. Of those that a mesh axis runs over, the one named last changes fastest.
Arguments:
- tokens: bfloat16 [4, 4096, 2048], P('sample', 'expert'), may hold values from -6 to 6
- routes: int32 [4, 4096, 8], P('sample', 'expert'), may hold values from 0 to 31, all different within a row; in each aligned block of 128 rows (0 to 127, 128 to 255, ..., all dimensions but the last counted through in order) at most 33 rows name the same one
- probs: bfloat16 [4, 4096, 8], P('sample', 'expert'), may hold values from 0.049804688 to 1
- cotangent: bfloat16 [4, 4096, 2048], P('sample', 'expert'), may hold values from -6 to 6
- w_gate_up: bfloat16 [32, 2048, 1536], P('expert'), may hold values from -0.125 to 0.125
- w_down: bfloat16 [32, 768, 2048], P('expert'), may hold values from -0.21875 to 0.21875
- gu_noise: float32 [4, 32, 8, 6], P('sample', 'expert'), may hold values from 0.5 to 1.5
- down_noise: float32 [4, 32, 3, 8], P('sample', 'expert'), may hold values from 0.5 to 1.5
Outputs:
- layer_out: bfloat16 [4, 4096, 2048], P('sample', 'expert')
- input_grad: bfloat16 [4, 4096, 2048], P('sample', 'expert')
- prob_grad: float32 [4, 4096, 8], P('sample', 'expert')
- grad_gate_up: float32 [32, 2048, 1536], P('expert', 'sample')
- grad_down: float32 [32, 768, 2048], P('expert', None, 'sample')
Inputs may be any that keep to these rules, and one draw needn't show every extreme that they name: `routes`: each row names 8 different experts. In each aligned block of 128 rows of a group (the tokens of one device) no expert is named more than 33 times, a bound that some block reaches.
All inputs are finite; a program needn't handle non-finite values.
Results may differ from a plain program's by a relative error of at most 0.0083.
Values may be sent and summed in bfloat16 or wider, within the bound.
No kernel may reach another device: no remote copies, remote signals or barrier semaphores. Data moves between devices by JAX's collectives and lax.ppermute only.
A program may use at most 192 MiB of HBM per device.

v0:
```python
import jax
import jax.numpy as jnp
from jax import lax
from jax.sharding import PartitionSpec as P


def tile_scale(weight, noise):
    batch, height, breadth = weight.shape
    tiles_down = noise.shape[1]
    tiles_across = noise.shape[2]
    blocks = weight.astype(jnp.float32).reshape(
        batch, tiles_down, height // tiles_down, tiles_across, breadth // tiles_across
    )
    return (blocks * noise[:, :, None, :, None]).reshape(batch, height, breadth)


def slot_table(routes, probs, capacity, experts):
    count, chosen = routes.shape
    flattened = routes.reshape(-1)
    onehot = (flattened[:, None] == jnp.arange(experts, dtype=jnp.int32)[None, :]).astype(jnp.int32)
    before = jnp.cumsum(onehot, axis=0) - onehot
    slots = jnp.sum(before * onehot, axis=1)
    position = flattened * capacity + slots
    owner = jnp.arange(count * chosen, dtype=jnp.int32) // chosen
    source = jnp.full((experts * capacity,), count, jnp.int32).at[position].set(owner)
    weights = jnp.zeros((experts * capacity,), probs.dtype).at[position].set(probs.reshape(-1))
    return (position.reshape(count, chosen), source, weights)


def forward_rows(inputs, weight_in, weight_out):
    gate_up = jnp.einsum("sjnd,jdf->sjnf", inputs, weight_in, preferred_element_type=jnp.float32)
    half_width = gate_up.shape[-1] // 2
    hidden = (jax.nn.silu(gate_up[..., :half_width]) * gate_up[..., half_width:]).astype(
        jnp.bfloat16
    )
    output = jnp.einsum(
        "sjnf,jfd->sjnd", hidden, weight_out, preferred_element_type=jnp.float32
    ).astype(jnp.bfloat16)
    return (output, hidden, gate_up)


def backward_rows(gate_up, upstream, weight_in, weight_out):
    half_width = gate_up.shape[-1] // 2
    gate = gate_up[..., :half_width]
    upward = gate_up[..., half_width:]
    grad_hidden = jnp.einsum(
        "sjnd,jfd->sjnf", upstream, weight_out, preferred_element_type=jnp.float32
    )
    sigma = jax.nn.sigmoid(gate)
    slope = sigma * (1.0 + gate * (1.0 - sigma))
    grad_mix = jnp.concatenate(
        [grad_hidden * upward * slope, grad_hidden * gate * sigma], axis=-1
    ).astype(jnp.bfloat16)
    grad_input = jnp.einsum(
        "sjnf,jdf->sjnd", grad_mix, weight_in, preferred_element_type=jnp.float32
    ).astype(jnp.bfloat16)
    return (grad_mix, grad_input)


def shards(tokens, routes, probs, cotangent, w_gate_up, w_down, gu_noise, down_noise):
    local_tokens = tokens[0]
    count, model_width = local_tokens.shape
    chosen = routes.shape[2]
    per_device = w_gate_up.shape[0]
    experts = per_device * lax.axis_size("expert")
    capacity = min(count, count * chosen // experts + max(1, count * chosen // (32 * experts)))
    position, source, slot_prob = slot_table(routes[0], probs[0], capacity, experts)
    empty_row = jnp.zeros((1, model_width), jnp.bfloat16)
    send_x = jnp.concatenate([local_tokens, empty_row], axis=0)[source].reshape(
        experts, capacity, model_width
    )
    send_out = jnp.concatenate([cotangent[0], empty_row], axis=0)[source].reshape(
        experts, capacity, model_width
    )
    send_prob = slot_prob.reshape(experts, capacity)
    weight_in = tile_scale(w_gate_up, gu_noise[0]).astype(jnp.bfloat16)
    weight_out = tile_scale(w_down, down_noise[0]).astype(jnp.bfloat16)

    def split_rows(block):
        return block.reshape((-1, per_device) + block.shape[1:])

    def merge_rows(block):
        return block.reshape((-1,) + block.shape[2:])

    inputs = lax.all_to_all(send_x, "expert", split_axis=0, concat_axis=0, tiled=True)
    output, hidden, gate_up = forward_rows(split_rows(inputs), weight_in, weight_out)
    returned = lax.all_to_all(merge_rows(output), "expert", split_axis=0, concat_axis=0, tiled=True)
    hidden_rows = merge_rows(hidden)
    gate_up_rows = merge_rows(gate_up)
    recv_out, recv_prob = (
        lax.all_to_all(send_out, "expert", split_axis=0, concat_axis=0, tiled=True),
        lax.all_to_all(send_prob, "expert", split_axis=0, concat_axis=0, tiled=True),
    )
    scaled_up = (
        split_rows(recv_prob)[..., None].astype(jnp.float32)
        * split_rows(recv_out).astype(jnp.float32)
    ).astype(jnp.bfloat16)
    grad_mix, grad_input = backward_rows(split_rows(gate_up_rows), scaled_up, weight_in, weight_out)
    dx_back = lax.all_to_all(
        merge_rows(grad_input), "expert", split_axis=0, concat_axis=0, tiled=True
    )
    recv_dy = merge_rows(scaled_up)
    grad_rows = merge_rows(grad_mix)
    inputs_all = split_rows(inputs)
    upstream_all = split_rows(recv_dy)
    hidden_all = split_rows(hidden_rows)
    mixes_all = split_rows(grad_rows)
    shares = lax.axis_size("sample")
    raw_in = jnp.einsum("sjnd,sjnf->jdf", inputs_all, mixes_all, preferred_element_type=jnp.float32)
    raw_out = jnp.einsum(
        "sjnf,sjnd->jfd", hidden_all, upstream_all, preferred_element_type=jnp.float32
    )
    sum_in, sum_out = (
        lax.psum_scatter(
            tile_scale(raw_in, gu_noise[0]), "sample", scatter_dimension=1, tiled=True
        ),
        lax.psum_scatter(
            tile_scale(raw_out, down_noise[0]), "sample", scatter_dimension=2, tiled=True
        ),
    )
    routed_y = returned.reshape(experts * capacity, model_width)[position].astype(jnp.float32)
    routed_dx = dx_back.reshape(experts * capacity, model_width)[position].astype(jnp.float32)
    weights = probs[0].astype(jnp.float32)
    layer_out = jnp.sum(weights[:, :, None] * routed_y, axis=1).astype(jnp.bfloat16)
    prob_grad = jnp.sum(cotangent[0].astype(jnp.float32)[:, None, :] * routed_y, axis=2)
    input_grad = jnp.sum(routed_dx, axis=1).astype(jnp.bfloat16)
    return (layer_out[None], input_grad[None], prob_grad[None], sum_in / shares, sum_out / shares)


def solution(mesh):
    in_specs = (
        P("sample", "expert", None),
        P("sample", "expert", None),
        P("sample", "expert", None),
        P("sample", "expert", None),
        P("expert", None, None),
        P("expert", None, None),
        P("sample", "expert", None, None),
        P("sample", "expert", None, None),
    )
    out_specs = (
        P("sample", "expert", None),
        P("sample", "expert", None),
        P("sample", "expert", None),
        P("expert", "sample", None),
        P("expert", None, "sample"),
    )
    return jax.shard_map(shards, mesh=mesh, in_specs=in_specs, out_specs=out_specs, check_vma=False)
```

profile of v0, /device:TPU:1, one launch (start us, length us, event | category | flops | bytes accessed | tf_op | source)
XLA Modules:
  0.0 536.9 jit_solution(15773869347576954893)
XLA Ops:
  8.3 9.0 %reduce-window.6 = s32[32,8,128]{2,1,0:T(8,128)S(1)} reduce-window(s32[32,8,128]{2,1,0:T(8,128)S(1)} %fusion.29, s32[]{:T(128)} %constant.40.clone.1), window={size=1x1x128 pad=0_0x0_0x127_0}, to_apply=%region_0.0 | reduce-window | flops 4161536 | bytes 262148 | tf_op jit(solution)/shard_map/reduce-window
  18.7 7.6 %scatter_custom_fusion.1 = bf16[1056]{0:T(1024)(128)(2,1)S(1)} fusion(s32[1024]{0:T(1024)S(1)} %bitcast.167, bf16[1024]{0:T(1024)(128)(2,1)S(1)} %reshape.296, bf16[]{:T(256)} %constant.18.clone.1), kind=kCustom, calls=%fused_computation.75 | custom fusion | bytes 2114 | tf_op jit(solution)/shard_map/scatter | solution.py:26
  27.0 9.2 %all-to-all-start.2 = ((bf16[32,1,33]{2,1,0:T(2,128)(2,1)}), bf16[32,1,33]{2,1,0:T(2,128)(2,1)S(1)}, u32[]{:S(2)}, u32[]{:S(2)}) async-start(bf16[32,1,33]{2,1,0:T(2,128)(2,1)} %all_to_all.24), calls=%async_computation.2 | async-start | bytes 32768 | tf_op jit(solution)/shard_map/all_to_all | solution.py:92
  53.2 8.0 %all-to-all-start.3 = ((bf16[32,33,2048]{2,1,0:T(8,128)(2,1)}), bf16[32,33,2048]{2,1,0:T(8,128)(2,1)}, u32[]{:S(2)}, u32[]{:S(2)}) async-start(bf16[32,33,2048]{2,1,0:T(8,128)(2,1)} %reshape.245), calls=%async_computation.3 | async-start | bytes 10485760 | tf_op jit(solution)/shard_map/all_to_all | solution.py:91
  72.6 59.5 %all-to-all-done.3 = bf16[32,33,2048]{2,1,0:T(8,128)(2,1)} async-done(((bf16[32,33,2048]{2,1,0:T(8,128)(2,1)}), bf16[32,33,2048]{2,1,0:T(8,128)(2,1)}, u32[]{:S(2)}, u32[]{:S(2)}) %all-to-all-start.3) | async-done | bytes 4325408 | tf_op jit(solution)/shard_map/all_to_all | solution.py:91
  132.2 7.3 %all-to-all-start = ((bf16[32,33,2048]{2,1,0:T(8,128)(2,1)}), bf16[32,33,2048]{2,1,0:T(8,128)(2,1)}, u32[]{:S(2)}, u32[]{:S(2)}) async-start(bf16[32,33,2048]{2,1,0:T(8,128)(2,1)} %reshape.241), calls=%async_computation | async-start | bytes 10485760 | tf_op jit(solution)/shard_map/all_to_all | solution.py:85
  145.1 13.6 %mul.133 = f32[1,2048,1536]{1,2,0:T(8,128)} reshape(f32[8,256,6,256]{1,0,3,2:T(8,128)} %mul.132.clone) | data formatting | bytes 25165824 | tf_op jit(solution)/shard_map/mul | solution.py:14
  158.7 8.7 %copy.69 = bf16[1,2048,1536]{1,2,0:T(8,128)(2,1)} copy(bf16[1,2048,1536]{2,1,0:T(8,128)(2,1)} %param.12) | data formatting | bytes 12582912 | tf_op args[4]
  183.2 7.7 %reshape.317 = bf16[8,256,33,32]{1,0,2,3:T(8,128)(2,1)} reshape(bf16[2048,33,32]{0,1,2:T(8,128)(2,1)} %fusion.8) | data formatting | bytes 8650752 | tf_op jit(solution)/shard_map/sjnf,sjnd->jfd/dot_general | solution.py:110
  191.0 18.7 %all-to-all-done = bf16[32,33,2048]{2,1,0:T(8,128)(2,1)} async-done(((bf16[32,33,2048]{2,1,0:T(8,128)(2,1)}), bf16[32,33,2048]{2,1,0:T(8,128)(2,1)}, u32[]{:S(2)}, u32[]{:S(2)}) %all-to-all-start) | async-done | bytes 4325408 | tf_op jit(solution)/shard_map/all_to_all | solution.py:85
  209.7 13.7 %convolution_bitcast_fusion = f32[32,1,33,1536]{3,2,0,1:T(8,128)S(1)} fusion(bf16[32,33,2048]{2,1,0:T(8,128)(2,1)} %all-to-all-done, f32[1,2048,1536]{1,2,0:T(8,128)} %mul.133, bf16[1,2048,1536]{1,2,0:T(8,128)(2,1)} %copy.69), kind=kOutput, calls=%fused_computation.23 | convolution fusion | flops 6653214720 | bytes 29687808 | tf_op jit(solution)/shard_map/sjnd,jdf->sjnf/dot_general | solution.py:31
  223.4 12.0 %fusion.25 = (bf16[32,33,768]{2,1,0:T(8,128)(2,1)}, bf16[32,33,768]{2,1,0:T(8,128)(2,1)}, bf16[32,1,33,768]{3,2,0,1:T(8,128)(2,1)}) fusion(f32[32,1,33,1536]{3,2,0,1:T(8,128)S(1)} %convolution_bitcast_fusion, bf16[32,33,2048]{2,1,0:T(8,128)(2,1)} %all-to-all-done.3, f32[32,33]{1,0:T(8,128)S(1)} %bitcast.162, f32[1,768,2048]{2,1,0:T(8,128)} %mul.129, ...), kind=kOutput, calls=%fused_computation.43 | convolution fusion | flops 3346071552 | bytes 25120896 | tf_op jit(solution)/shard_map/sjnd,jfd->sjnf/dot_general | solution.py:46
  259.8 7.9 %reshape.314 = bf16[8,256,33,32]{1,0,2,3:T(8,128)(2,1)} reshape(bf16[2048,33,32]{0,1,2:T(8,128)(2,1)} %bitcast.36) | data formatting | bytes 8650752 | tf_op jit(solution)/shard_map/sjnd,sjnf->jdf/dot_general | solution.py:109
  271.5 7.8 %reshape.315 = bf16[6,256,33,32]{1,0,2,3:T(8,128)(2,1)} reshape(bf16[1536,33,32]{0,1,2:T(8,128)(2,1)} %fusion.21) | data formatting | bytes 6488064 | tf_op jit(solution)/shard_map/sjnd,sjnf->jdf/dot_general | solution.py:109
  279.3 14.2 %bitcast_multiply_fusion = f32[8,256,6,256]{3,1,2,0:T(8,128)} fusion(f32[8,6]{1,0:T(8,128)S(1)} %bitcast.169, bf16[8,256,33,32,1]{1,0,2,3,4:T(8,128)(2,1)} %bitcast.152, bf16[6,256,33,32]{1,0,2,3:T(8,128)(2,1)} %reshape.315), kind=kOutput, calls=%fused_computation.6 | convolution fusion | flops 6646923264 | bytes 20152512 | tf_op jit(solution)/shard_map/sjnd,sjnf->jdf/dot_general | solution.py:109
  293.5 12.9 %copy.85 = f32[8,256,6,256]{1,0,3,2:T(8,128)} copy(f32[8,256,6,256]{3,1,2,0:T(8,128)} %bitcast_multiply_fusion) | data formatting | bytes 25165824 | tf_op jit(solution)/shard_map/mul | solution.py:14
  306.4 13.7 %reshape.248 = f32[1,2048,1536]{1,2,0:T(8,128)} reshape(f32[8,256,6,256]{1,0,3,2:T(8,128)} %copy.85) | data formatting | bytes 25165824 | tf_op jit(solution)/shard_map/reshape | solution.py:14
  321.7 9.7 %convert_bitcast_fusion.1 = bf16[32,33,2048]{2,1,0:T(8,128)(2,1)} fusion(bf16[32,1,33,768]{3,2,0,1:T(8,128)(2,1)S(1)} %copy-done.1, f32[1,768,2048]{2,1,0:T(8,128)} %mul.129, bf16[1,768,2048]{2,1,0:T(8,128)(2,1)} %param.13), kind=kOutput, calls=%fused_computation.22 | convolution fusion | flops 3328770048 | bytes 15384576 | tf_op jit(solution)/shard_map/sjnf,jfd->sjnd/dot_general | solution.py:36
  331.3 7.9 %all-to-all-start.1 = ((bf16[32,33,2048]{2,1,0:T(8,128)(2,1)}), bf16[32,33,2048]{2,1,0:T(8,128)(2,1)}, u32[]{:S(2)}, u32[]{:S(2)}) async-start(bf16[32,33,2048]{2,1,0:T(8,128)(2,1)} %convert_bitcast_fusion.1), calls=%async_computation.1 | async-start | bytes 10485760 | tf_op jit(solution)/shard_map/all_to_all | solution.py:87
  339.3 21.6 %convert_bitcast_fusion = bf16[32,33,2048]{2,1,0:T(8,128)(2,1)} fusion(bf16[32,33,768]{2,1,0:T(8,128)(2,1)} %get-tuple-element.23, bf16[32,33,768]{2,1,0:T(8,128)(2,1)S(1)} %copy-done.3, f32[1,2048,1536]{1,2,0:T(8,128)} %mul.133, bf16[1,2048,1536]{1,2,0:T(8,128)(2,1)} %copy.69), kind=kOutput, calls=%fused_computation.21 | convolution fusion | flops 6661865472 | bytes 26443776 | tf_op jit(solution)/shard_map/sjnf,jdf->sjnd/dot_general | solution.py:54
  360.9 50.1 %all-to-all-done.1 = bf16[32,33,2048]{2,1,0:T(8,128)(2,1)} async-done(((bf16[32,33,2048]{2,1,0:T(8,128)(2,1)}), bf16[32,33,2048]{2,1,0:T(8,128)(2,1)}, u32[]{:S(2)}, u32[]{:S(2)}) %all-to-all-start.1) | async-done | bytes 4325408 | tf_op jit(solution)/shard_map/all_to_all | solution.py:87
  423.8 11.6 %gather_fusion.1 = bf16[1024,2048]{1,0:T(8,128)(2,1)} fusion(bf16[1056,2048]{1,0:T(8,128)(2,1)} %reshape.244, s32[1024]{0:T(1024)S(1)} %broadcast_clamp_fusion), kind=kCustom, calls=%fused_computation.1 | custom fusion | bytes 8392704 | tf_op jit(solution)/shard_map/gather | solution.py:121
  435.4 51.6 %all-to-all-done.4 = bf16[32,33,2048]{2,1,0:T(8,128)(2,1)} async-done(((bf16[32,33,2048]{2,1,0:T(8,128)(2,1)}), bf16[32,33,2048]{2,1,0:T(8,128)(2,1)}, u32[]{:S(2)}, u32[]{:S(2)}) %all-to-all-start.4) | async-done | bytes 4325408 | tf_op jit(solution)/shard_map/all_to_all | solution.py:99
  492.7 11.6 %gather_fusion.3 = bf16[1024,2048]{1,0:T(8,128)(2,1)} fusion(bf16[1056,2048]{1,0:T(8,128)(2,1)} %reshape.247, s32[1024]{0:T(1024)S(1)} %broadcast_clamp_fusion), kind=kCustom, calls=%fused_computation.3 | custom fusion | bytes 8392704 | tf_op jit(solution)/shard_map/gather | solution.py:122
  (90 shorter events, 126.5 us)
Async XLA Ops:
  8.0 32.7 %copy-start.4 = (s32[1,128,8]{2,1,0:T(8,128)}, s32[1,128,8]{2,1,0:T(8,128)S(1)}, u32[]{:S(2)}) copy-start(s32[1,128,8]{2,1,0:T(8,128)S(1)} %copy.72) | copy-start | bytes 12292
  18.7 22.0 %copy-start.7 = (s32[1024]{0:T(1024)}, s32[1024]{0:T(1024)S(1)}, u32[]{:S(2)}) copy-start(s32[1024]{0:T(1024)S(1)} %fusion.28) | copy-start | bytes 12292
  27.0 26.1 %all-to-all-start.2 = ((bf16[32,1,33]{2,1,0:T(2,128)(2,1)}), bf16[32,1,33]{2,1,0:T(2,128)(2,1)S(1)}, u32[]{:S(2)}, u32[]{:S(2)}) async-start(bf16[32,1,33]{2,1,0:T(2,128)(2,1)} %all_to_all.24), calls=%async_computation.2 | async-start | bytes 32768 | tf_op jit(solution)/shard_map/all_to_all | solution.py:92
  53.2 8.0 %copy-start.6 = (bf16[1,128,2048]{2,1,0:T(8,128)(2,1)S(1)}, bf16[1,128,2048]{2,1,0:T(8,128)(2,1)}, u32[]{:S(2)}) copy-start(bf16[1,128,2048]{2,1,0:T(8,128)(2,1)} %param.8) | copy-start | bytes 1572868
  53.2 79.0 %all-to-all-start.3 = ((bf16[32,33,2048]{2,1,0:T(8,128)(2,1)}), bf16[32,33,2048]{2,1,0:T(8,128)(2,1)}, u32[]{:S(2)}, u32[]{:S(2)}) async-start(bf16[32,33,2048]{2,1,0:T(8,128)(2,1)} %reshape.245), calls=%async_computation.3 | async-start | bytes 10485760 | tf_op jit(solution)/shard_map/all_to_all | solution.py:91
  72.6 67.1 %copy-start.11 = (f32[1,1,3,8]{3,1,2,0:T(1,128)S(1)}, f32[1,1,3,8]{3,1,2,0:T(1,128)}, u32[]{:S(2)}) copy-start(f32[1,1,3,8]{3,1,2,0:T(1,128)} %param.15) | copy-start | bytes 292
  72.6 67.1 %copy-start.9 = (f32[1,1,8,6]{2,1,3,0:T(1,128)S(1)}, f32[1,1,8,6]{2,1,3,0:T(1,128)}, u32[]{:S(2)}) copy-start(f32[1,1,8,6]{2,1,3,0:T(1,128)} %param.14) | copy-start | bytes 580
  132.2 77.5 %all-to-all-start = ((bf16[32,33,2048]{2,1,0:T(8,128)(2,1)}), bf16[32,33,2048]{2,1,0:T(8,128)(2,1)}, u32[]{:S(2)}, u32[]{:S(2)}) async-start(bf16[32,33,2048]{2,1,0:T(8,128)(2,1)} %reshape.241), calls=%async_computation | async-start | bytes 10485760 | tf_op jit(solution)/shard_map/all_to_all | solution.py:85
  139.5 377.1 %reduce-scatter.5.cloned.1.call-start = ((), (), s32[]{:S(2)}) async-start(), calls=%async_computation.8 | async-start | bytes 7864320 | tf_op jit(solution)/shard_map/reduce_scatter | solution.py:117
  209.7 13.7 %copy-start.12 = (bf16[1,768,2048]{2,1,0:T(8,128)(2,1)S(1)}, bf16[1,768,2048]{2,1,0:T(8,128)(2,1)}, u32[]{:S(2)}) copy-start(bf16[1,768,2048]{2,1,0:T(8,128)(2,1)} %param.13) | copy-start | bytes 9437188
  259.7 265.5 %reduce-scatter.3.cloned.1.call-start = ((), (), s32[]{:S(2)}) async-start(), calls=%async_computation.7 | async-start | bytes 15728640 | tf_op jit(solution)/shard_map/reduce_scatter | solution.py:114
  259.8 7.9 %copy-start.2 = (bf16[32,33,768]{2,1,0:T(8,128)(2,1)S(1)}, bf16[32,33,768]{2,1,0:T(8,128)(2,1)}, u32[]{:S(2)}) copy-start(bf16[32,33,768]{2,1,0:T(8,128)(2,1)} %get-tuple-element.22) | copy-start | bytes 4866052
  320.1 1.5 copy-start.1
  331.3 7.9 %copy-start.3 = (bf16[32,33,768]{2,1,0:T(8,128)(2,1)S(1)}, bf16[32,33,768]{2,1,0:T(8,128)(2,1)}, u32[]{:S(2)}) copy-start(bf16[32,33,768]{2,1,0:T(8,128)(2,1)} %get-tuple-element.22) | copy-start | bytes 4866052
  331.3 79.7 %all-to-all-start.1 = ((bf16[32,33,2048]{2,1,0:T(8,128)(2,1)}), bf16[32,33,2048]{2,1,0:T(8,128)(2,1)}, u32[]{:S(2)}, u32[]{:S(2)}) async-start(bf16[32,33,2048]{2,1,0:T(8,128)(2,1)} %convert_bitcast_fusion.1), calls=%async_computation.1 | async-start | bytes 10485760 | tf_op jit(solution)/shard_map/all_to_all | solution.py:87
  360.9 56.6 %copy-start.8 = (s32[1024]{0:T(1024)S(1)}, s32[1024]{0:T(1024)}, u32[]{:S(2)}) copy-start(s32[1024]{0:T(1024)} %copy-done.7) | copy-start | bytes 12292
  360.9 56.7 %copy-start.5 = (s32[1,128,8]{2,1,0:T(8,128)S(1)}, s32[1,128,8]{2,1,0:T(8,128)}, u32[]{:S(2)}) copy-start(s32[1,128,8]{2,1,0:T(8,128)} %copy-done.4) | copy-start | bytes 12292
  360.9 56.8 %copy-start.10 = (bf16[1,128,8]{1,2,0:T(8,128)(2,1)S(1)}, bf16[1,128,8]{1,2,0:T(8,128)(2,1)}, u32[]{:S(2)}) copy-start(bf16[1,128,8]{1,2,0:T(8,128)(2,1)} %param.10) | copy-start | bytes 6148
  360.9 57.0 %copy-start = (bf16[1,128,2048]{2,1,0:T(8,128)(2,1)S(1)}, bf16[1,128,2048]{2,1,0:T(8,128)(2,1)}, u32[]{:S(2)}) copy-start(bf16[1,128,2048]{2,1,0:T(8,128)(2,1)} %param.11) | copy-start | bytes 1572868
  411.0 76.0 %all-to-all-start.4 = ((bf16[32,33,2048]{2,1,0:T(8,128)(2,1)}), bf16[32,33,2048]{2,1,0:T(8,128)(2,1)}, u32[]{:S(2)}, u32[]{:S(2)}) async-start(bf16[32,33,2048]{2,1,0:T(8,128)(2,1)} %convert_bitcast_fusion), calls=%async_computation.4 | async-start | bytes 10485760 | tf_op jit(solution)/shard_map/all_to_all | solution.py:99
Sparse Core Ops, SparseCore 0:
  259.8 66.9 reduce-scatter.4
  329.7 195.4 reduce-scatter.2
where the time goes:
time: 547 us; the launch traced here: 537 us
  waiting for transfers between devices  186 us (34%)
  local copies, waits for them, and re-layouts  184 us (34%)
  matrix products  77.8 us (14%)
  starting transfers between devices  39.2 us (7%)
  other arithmetic  35.4 us (6%)
  between operations  14.6 us (3%)
    all_to_all x1, waiting for transfers between devices, shards(): lax.all_to_all(send_out, 'expert', split_axis=0, concat_axis=0, tiled=True)  59.5 us
    all_to_all x1, waiting for transfers between devices, shards(): lax.all_to_all(merge_rows(grad_input), 'expert', split_axis=0, concat_axi...  51.6 us
    all_to_all x1, waiting for transfers between devices, shards(): lax.all_to_all(merge_rows(output), 'expert', split_axis=0, concat_axis=0,...  50.1 us
    mul x7, local copies, waits for them, and re-layouts, tile_scale(): return (blocks * noise[:, :, None, :, None]).reshape(batch, height, breadth)  48.2 us
    dot_general x1, matrix products, backward_rows(): jnp.einsum('sjnf,jdf->sjnd', grad_mix, weight_in, preferred_element_type=...  21.6 us
    reshape x2, local copies, waits for them, and re-layouts, tile_scale(): return (blocks * noise[:, :, None, :, None]).reshape(batch, height, breadth)  20.8 us
    all_to_all x1, waiting for transfers between devices, shards(): lax.all_to_all(send_x, 'expert', split_axis=0, concat_axis=0, tiled=True)  18.7 us
    dot_general x2, local copies, waits for them, and re-layouts, shards(): jnp.einsum('sjnd,sjnf->jdf', inputs_all, mixes_all, preferred_element_typ...  15.7 us
  transfers between devices with their start and end apart: 7, of which 5 were waited for; matrix products, arithmetic and copies ran while one was open for 41% of the time, Pallas kernels for 0%

commit v1 on v0

v1 whole, which is shorter than its diff:
```python
import functools

import jax
import jax.numpy as jnp
from jax import lax
from jax.experimental import pallas as pl
from jax.experimental.pallas import tpu as pltpu
from jax.sharding import PartitionSpec as P

D = 2048
FF = 768
TOP = 8
TOK = 128
BLOCKS = 32
LANES = 128
COLS = D // LANES
MAIN = 32
PACK = MAIN * COLS + COLS
ROWS = BLOCKS * (MAIN + 1)
BIG = BLOCKS * MAIN
VMEM_LIMIT = 48 * 1024 * 1024

F32 = jnp.float32
BF16 = jnp.bfloat16


def params(**more):
    return pltpu.CompilerParams(vmem_limit_bytes=VMEM_LIMIT, **more)


def cost(flops, moved):
    return pl.CostEstimate(flops=flops, bytes_accessed=moved, transcendentals=0)


def iota(shape, dim):
    return lax.broadcasted_iota(jnp.int32, shape, dim)


def dot(a, b):
    return jnp.dot(a, b, preferred_element_type=F32)


def dot_nt(a, b):
    return lax.dot_general(a, b, (((1,), (1,)), ((), ())), preferred_element_type=F32)


def dot_tn(a, b):
    return lax.dot_general(a, b, (((0,), (0,)), ((), ())), preferred_element_type=F32)


def slot_keys(routes):
    lane = iota((TOK, LANES), 1)
    chosen = jnp.zeros((TOK, LANES), F32)
    for k in range(TOP):
        chosen = jnp.where(routes[:, k : k + 1] == lane, 1.0, chosen)
    earlier = jnp.where(iota((TOK, TOK), 0) > iota((TOK, TOK), 1), 1.0, 0.0).astype(BF16)
    rank = dot(earlier, chosen.astype(BF16))
    return jnp.where(chosen > 0.0, rank, -1.0)


def expert_weights(routes, probs):
    lane = iota((TOK, LANES), 1)
    weight = jnp.zeros((TOK, LANES), F32)
    for k in range(TOP):
        weight = jnp.where(routes[:, k : k + 1] == lane, probs[:, k : k + 1].astype(F32), weight)
    return weight


def last_slot_order(receive):
    count = BLOCKS * COLS
    tile = iota((count, count), 1 if receive else 0)
    row = iota((count, count), 0 if receive else 1)
    same = ((tile // COLS) == (row % BLOCKS)) & ((tile % COLS) == (row // BLOCKS))
    return jnp.where(same, 1.0, 0.0).astype(BF16)


def unpack_last(tile):
    flat = tile.reshape(BLOCKS * COLS, LANES)
    return dot(last_slot_order(True), flat).astype(BF16)


def dispatch_kernel(weighted, routes_ref, probs_ref, value_ref, out_ref, last_ref):
    routes = routes_ref[...]
    key = slot_keys(routes).T
    spread = jnp.where(iota((BIG, LANES), 0) // MAIN == iota((BIG, LANES), 1), 1.0, 0.0).astype(BF16)
    hit = dot(spread, key.astype(BF16)) == (iota((BIG, TOK), 0) % MAIN).astype(F32)
    last_hit = key[:BLOCKS] == float(MAIN)
    if weighted:
        weight = expert_weights(routes, probs_ref[...]).T
        pick = jnp.where(hit, dot(spread, weight.astype(BF16)), 0.0).astype(BF16)
        last_pick = jnp.where(last_hit, weight[:BLOCKS], 0.0).astype(BF16)
    else:
        pick = jnp.where(hit, 1.0, 0.0).astype(BF16)
        last_pick = jnp.where(last_hit, 1.0, 0.0).astype(BF16)
    for j in range(COLS):
        value = value_ref[:, j * LANES : (j + 1) * LANES]
        rows = dot(pick, value).astype(BF16)
        out_ref[:, j * MAIN : (j + 1) * MAIN, :] = rows.reshape(BLOCKS, MAIN, LANES)
        last_ref[j * BLOCKS : (j + 1) * BLOCKS, :] = dot(last_pick, value).astype(BF16)
    tiles = dot(last_slot_order(False), last_ref[...]).astype(BF16)
    out_ref[:, MAIN * COLS :, :] = tiles.reshape(BLOCKS, COLS, LANES)


def dispatch(routes, probs, value, weighted):
    return pl.pallas_call(
        functools.partial(dispatch_kernel, weighted),
        out_shape=jax.ShapeDtypeStruct((BLOCKS, PACK, LANES), BF16),
        scratch_shapes=[pltpu.VMEM((BLOCKS * COLS, LANES), BF16)],
        compiler_params=params(),
        cost_estimate=cost(2 * ROWS * TOK * D, 2 * (ROWS + TOK) * D),
    )(routes, probs, value)


def noisy_kernel(noise_ref, weight_ref, out_ref):
    row = pl.program_id(0)
    for c in range(weight_ref.shape[1] // 256):
        cut = slice(c * 256, (c + 1) * 256)
        out_ref[:, cut] = (weight_ref[:, cut].astype(F32) * noise_ref[row, c]).astype(BF16)


def noisy(weight, noise):
    height, breadth = weight.shape
    return pl.pallas_call(
        noisy_kernel,
        grid=(height // 256,),
        out_shape=jax.ShapeDtypeStruct(weight.shape, BF16),
        in_specs=[
            pl.BlockSpec(memory_space=pltpu.SMEM),
            pl.BlockSpec((256, breadth), lambda i: (i, 0)),
        ],
        out_specs=pl.BlockSpec((256, breadth), lambda i: (i, 0)),
        compiler_params=params(),
        cost_estimate=cost(height * breadth, 4 * height * breadth),
    )(noise, weight)


def unpack_rows(packed_ref, rows_ref):
    last = unpack_last(packed_ref[:, MAIN * COLS :, :])
    for j in range(COLS):
        cut = slice(j * LANES, (j + 1) * LANES)
        rows_ref[:BIG, cut] = packed_ref[:, j * MAIN : (j + 1) * MAIN, :].reshape(BIG, LANES)
        rows_ref[BIG:, cut] = last[j * BLOCKS : (j + 1) * BLOCKS]


def pack_columns(values, first, out_ref, last_ref):
    for i in range(2):
        cut = values[:, i * LANES : (i + 1) * LANES]
        at = pl.multiple_of((first + i) * MAIN, MAIN)
        out_ref[:, pl.ds(at, MAIN), :] = cut[:BIG].reshape(BLOCKS, MAIN, LANES)
        last_ref[pl.ds(at, BLOCKS), :] = cut[BIG:]


def pack_last(out_ref, last_ref):
    tiles = dot(last_slot_order(False), last_ref[...]).astype(BF16)
    out_ref[:, MAIN * COLS :, :] = tiles.reshape(BLOCKS, COLS, LANES)


def gate_up_kernel(packed_ref, gate_w_ref, up_w_ref, rows_ref, gate_ref, up_ref, hidden_ref):
    @pl.when(pl.program_id(0) == 0)
    def _():
        unpack_rows(packed_ref, rows_ref)

    gate = dot(rows_ref[...], gate_w_ref[...])
    gate_ref[...] = gate
    up = dot(rows_ref[...], up_w_ref[...])
    up_ref[...] = up
    hidden_ref[...] = (gate * jax.nn.sigmoid(gate) * up).astype(BF16)


def gate_up(packed, weight_in):
    wide = FF // 256
    part = pl.BlockSpec((ROWS, 256), lambda i: (0, i))
    return pl.pallas_call(
        gate_up_kernel,
        grid=(wide,),
        out_shape=(
            jax.ShapeDtypeStruct((ROWS, D), BF16),
            jax.ShapeDtypeStruct((ROWS, FF), F32),
            jax.ShapeDtypeStruct((ROWS, FF), F32),
            jax.ShapeDtypeStruct((ROWS, FF), BF16),
        ),
        in_specs=[
            pl.BlockSpec((BLOCKS, PACK, LANES), lambda i: (0, 0, 0)),
            pl.BlockSpec((D, 256), lambda i: (0, i)),
            pl.BlockSpec((D, 256), lambda i: (0, i + wide)),
        ],
        out_specs=(pl.BlockSpec((ROWS, D), lambda i: (0, 0)), part, part, part),
        compiler_params=params(),
        cost_estimate=cost(4 * ROWS * D * FF, 4 * ROWS * D + 4 * D * FF + 10 * ROWS * FF),
    )(packed, weight_in, weight_in)


def down_kernel(hidden_ref, weight_ref, out_ref, last_ref):
    step = pl.program_id(0)
    values = dot(hidden_ref[...], weight_ref[...]).astype(BF16)
    pack_columns(values, step * 2, out_ref, last_ref)

    @pl.when(step == pl.num_programs(0) - 1)
    def _():
        pack_last(out_ref, last_ref)


def down(hidden, weight_out):
    return pl.pallas_call(
        down_kernel,
        grid=(D // 256,),
        out_shape=jax.ShapeDtypeStruct((BLOCKS, PACK, LANES), BF16),
        in_specs=[
            pl.BlockSpec((ROWS, FF), lambda i: (0, 0)),
            pl.BlockSpec((FF, 256), lambda i: (0, i)),
        ],
        out_specs=pl.BlockSpec((BLOCKS, PACK, LANES), lambda i: (0, 0, 0)),
        scratch_shapes=[pltpu.VMEM((BLOCKS * COLS, LANES), BF16)],
        compiler_params=params(),
        cost_estimate=cost(2 * ROWS * D * FF, 2 * ROWS * D + 2 * D * FF + 2 * ROWS * FF),
    )(hidden, weight_out)


def mix_kernel(packed_ref, weight_ref, gate_ref, up_ref, rows_ref, gate_grad_ref, up_grad_ref):
    @pl.when(pl.program_id(0) == 0)
    def _():
        unpack_rows(packed_ref, rows_ref)

    grad = dot_nt(rows_ref[...], weight_ref[...])
    gate = gate_ref[...]
    sigma = jax.nn.sigmoid(gate)
    slope = sigma * (1.0 + gate * (1.0 - sigma))
    gate_grad_ref[...] = (grad * up_ref[...] * slope).astype(BF16)
    up_grad_ref[...] = (grad * gate * sigma).astype(BF16)


def mix(packed, weight_out, gate, up):
    part = pl.BlockSpec((ROWS, 256), lambda i: (0, i))
    return pl.pallas_call(
        mix_kernel,
        grid=(FF // 256,),
        out_shape=(
            jax.ShapeDtypeStruct((ROWS, D), BF16),
            jax.ShapeDtypeStruct((ROWS, FF), BF16),
            jax.ShapeDtypeStruct((ROWS, FF), BF16),
        ),
        in_specs=[
            pl.BlockSpec((BLOCKS, PACK, LANES), lambda i: (0, 0, 0)),
            pl.BlockSpec((256, D), lambda i: (i, 0)),
            part,
            part,
        ],
        out_specs=(pl.BlockSpec((ROWS, D), lambda i: (0, 0)), part, part),
        compiler_params=params(),
        cost_estimate=cost(2 * ROWS * D * FF, 4 * ROWS * D + 2 * D * FF + 12 * ROWS * FF),
    )(packed, weight_out, gate, up)


def input_grad_kernel(gate_grad_ref, up_grad_ref, weight_ref, out_ref, last_ref):
    step = pl.program_id(0)
    values = dot_nt(gate_grad_ref[...], weight_ref[:, :FF])
    values = (values + dot_nt(up_grad_ref[...], weight_ref[:, FF:])).astype(BF16)
    pack_columns(values, step * 2, out_ref, last_ref)

    @pl.when(step == pl.num_programs(0) - 1)
    def _():
        pack_last(out_ref, last_ref)


def input_grads(gate_grad, up_grad, weight_in):
    whole = pl.BlockSpec((ROWS, FF), lambda i: (0, 0))
    return pl.pallas_call(
        input_grad_kernel,
        grid=(D // 256,),
        out_shape=jax.ShapeDtypeStruct((BLOCKS, PACK, LANES), BF16),
        in_specs=[whole, whole, pl.BlockSpec((256, 2 * FF), lambda i: (i, 0))],
        out_specs=pl.BlockSpec((BLOCKS, PACK, LANES), lambda i: (0, 0, 0)),
        scratch_shapes=[pltpu.VMEM((BLOCKS * COLS, LANES), BF16)],
        compiler_params=params(),
        cost_estimate=cost(4 * ROWS * D * FF, 2 * ROWS * D + 4 * D * FF + 4 * ROWS * FF),
    )(gate_grad, up_grad, weight_in)


def weight_in_kernel(share_ref, noise_ref, rows_ref, gate_grad_ref, up_grad_ref, out_ref):
    tile = share_ref[pl.program_id(0)] * 2 + pl.program_id(1)
    for half, grad_ref in enumerate((gate_grad_ref, up_grad_ref)):
        raw = dot_tn(rows_ref[...], grad_ref[...])
        for c in range(FF // 256):
            at = half * FF + c * 256
            scaled = raw[:, c * 256 : (c + 1) * 256] * noise_ref[tile, half * (FF // 256) + c]
            out_ref[0, :, at : at + 256] = scaled.astype(out_ref.dtype)


def weight_in_grads(shares, noise, rows, gate_grad, up_grad, dtype):
    whole = pl.BlockSpec((ROWS, FF), lambda j, i, s: (0, 0))
    return pl.pallas_call(
        weight_in_kernel,
        grid_spec=pltpu.PrefetchScalarGridSpec(
            num_scalar_prefetch=1,
            grid=(2, 2),
            in_specs=[
                pl.BlockSpec(memory_space=pltpu.SMEM),
                pl.BlockSpec((ROWS, 256), lambda j, i, s: (0, s[j] * 2 + i)),
                whole,
                whole,
            ],
            out_specs=pl.BlockSpec((1, 256, 2 * FF), lambda j, i, s: (j, i, 0)),
        ),
        out_shape=jax.ShapeDtypeStruct((2, 512, 2 * FF), dtype),
        compiler_params=params(),
        cost_estimate=cost(2 * ROWS * D * FF, ROWS * D + 4 * ROWS * FF + 4 * D * FF),
    )(shares, noise, rows, gate_grad, up_grad)


def weight_out_kernel(share_ref, noise_ref, hidden_ref, rows_ref, out_ref):
    tile = share_ref[pl.program_id(0)] * 2 + pl.program_id(1)
    raw = dot_tn(hidden_ref[...], rows_ref[...])
    for c in range(FF // 256):
        cut = slice(c * 256, (c + 1) * 256)
        out_ref[0, cut, :] = (raw[cut] * noise_ref[c, tile]).astype(out_ref.dtype)


def weight_out_grads(shares, noise, hidden, rows, dtype):
    return pl.pallas_call(
        weight_out_kernel,
        grid_spec=pltpu.PrefetchScalarGridSpec(
            num_scalar_prefetch=1,
            grid=(2, 2),
            in_specs=[
                pl.BlockSpec(memory_space=pltpu.SMEM),
                pl.BlockSpec((ROWS, FF), lambda j, i, s: (0, 0)),
                pl.BlockSpec((ROWS, 256), lambda j, i, s: (0, s[j] * 2 + i)),
            ],
            out_specs=pl.BlockSpec((1, FF, 256), lambda j, i, s: (j, 0, i)),
        ),
        out_shape=jax.ShapeDtypeStruct((2, FF, 512), dtype),
        compiler_params=params(),
        cost_estimate=cost(ROWS * D * FF, ROWS * D + 2 * ROWS * FF + 2 * D * FF),
    )(shares, noise, hidden, rows)


def combine_tables(routes, weight):
    key = slot_keys(routes)
    spread = jnp.where(iota((LANES, BIG), 1) // MAIN == iota((LANES, BIG), 0), 1.0, 0.0).astype(BF16)
    hit = dot(key.astype(BF16), spread) == (iota((TOK, BIG), 1) % MAIN).astype(F32)
    last_hit = key == float(MAIN)
    if weight is None:
        pick = jnp.where(hit, 1.0, 0.0)
        last_pick = jnp.where(last_hit, 1.0, 0.0)
    else:
        pick = jnp.where(hit, dot(weight.astype(BF16), spread), 0.0)
        last_pick = jnp.where(last_hit, weight, 0.0)
    return key, pick.astype(BF16), last_pick[:, :BLOCKS].astype(BF16)


def combine_kernel(routes_ref, packed_ref, out_ref):
    _, pick, last_pick = combine_tables(routes_ref[...], None)
    last = unpack_last(packed_ref[:, MAIN * COLS :, :])
    for j in range(COLS):
        cut = slice(j * LANES, (j + 1) * LANES)
        rows = packed_ref[:, j * MAIN : (j + 1) * MAIN, :].reshape(BIG, LANES)
        total = dot(pick, rows) + dot(last_pick, last[j * BLOCKS : (j + 1) * BLOCKS])
        out_ref[:, cut] = total.astype(BF16)


def combine(routes, packed):
    return pl.pallas_call(
        combine_kernel,
        out_shape=jax.ShapeDtypeStruct((TOK, D), BF16),
        compiler_params=params(),
        cost_estimate=cost(2 * ROWS * TOK * D, 2 * (ROWS + TOK) * D),
    )(routes, packed)


def combine_output_kernel(routes_ref, probs_ref, cotangent_ref, packed_ref, out_ref, grad_ref, rows_ref):
    routes = routes_ref[...]
    unpack_rows(packed_ref, rows_ref)
    key, pick, last_pick = combine_tables(routes, expert_weights(routes, probs_ref[...]))
    for j in range(D // 256):
        cut = slice(j * 256, (j + 1) * 256)
        total = dot(pick, rows_ref[:BIG, cut]) + dot(last_pick, rows_ref[BIG:, cut])
        out_ref[:, cut] = total.astype(BF16)
    main = dot_nt(cotangent_ref[...], rows_ref[:BIG, :])
    last = dot_nt(cotangent_ref[...], rows_ref[BIG:, :])
    lane = iota((TOK, LANES), 1)
    for k in range(TOP):
        expert = routes[:, k : k + 1]
        slot = jnp.sum(jnp.where(expert == lane, key, 0.0), axis=1, keepdims=True).astype(jnp.int32)
        row = jnp.where(slot < MAIN, expert * MAIN + slot, -1)
        value = jnp.sum(jnp.where(iota((TOK, BIG), 1) == row, main, 0.0), axis=1, keepdims=True)
        row = jnp.where(slot < MAIN, -1, expert)
        value += jnp.sum(jnp.where(iota((TOK, BLOCKS), 1) == row, last, 0.0), axis=1, keepdims=True)
        grad_ref[:, k : k + 1] = value


def combine_output(routes, probs, cotangent, packed):
    return pl.pallas_call(
        combine_output_kernel,
        out_shape=(
            jax.ShapeDtypeStruct((TOK, D), BF16),
            jax.ShapeDtypeStruct((TOK, TOP), F32),
        ),
        scratch_shapes=[pltpu.VMEM((ROWS, D), BF16)],
        compiler_params=params(),
        cost_estimate=cost(4 * ROWS * TOK * D, 2 * (ROWS + 2 * TOK) * D),
    )(routes, probs, cotangent, packed)


def exchange(value):
    return lax.all_to_all(value, "expert", split_axis=0, concat_axis=0, tiled=True)


def across(value, flip):
    pairs = [(s * BLOCKS + e, (s ^ flip) * BLOCKS + e) for s in range(4) for e in range(BLOCKS)]
    return lax.ppermute(value, ("sample", "expert"), pairs)


def shards(tokens, routes, probs, cotangent, w_gate_up, w_down, gu_noise, down_noise):
    routes, probs, cotangent = routes[0], probs[0], cotangent[0]
    gu_noise, down_noise = gu_noise[0, 0], down_noise[0, 0]
    sample = lax.axis_index("sample")
    ours = jnp.stack([sample, sample ^ 2]).astype(jnp.int32)
    theirs = ours ^ 1

    recv_x = exchange(dispatch(routes, probs, tokens[0], False))
    send_dy = dispatch(routes, probs, cotangent, True)
    weight_in = noisy(w_gate_up[0], gu_noise)
    weight_out = noisy(w_down[0], down_noise)
    recv_dy = exchange(send_dy)
    rows_x, gate, up, hidden = gate_up(recv_x, weight_in)
    output = down(hidden, weight_out)
    back_y = exchange(output)
    rows_dy, gate_grad, up_grad = mix(recv_dy, weight_out, gate, up)

    sent_in = weight_in_grads(theirs, gu_noise, rows_x, gate_grad, up_grad, BF16)
    got_in = across(sent_in, 1)
    sent_out = weight_out_grads(theirs, down_noise, hidden, rows_dy, BF16)
    got_out = across(sent_out, 1)
    kept_in = weight_in_grads(ours, gu_noise, rows_x, gate_grad, up_grad, F32)
    kept_out = weight_out_grads(ours, down_noise, hidden, rows_dy, F32)
    far_in = across((kept_in[1] + got_in[1].astype(F32)).astype(BF16), 2)
    far_out = across((kept_out[1] + got_out[1].astype(F32)).astype(BF16), 2)
    back_dx = exchange(input_grads(gate_grad, up_grad, weight_in))

    layer_out, prob_grad = combine_output(routes, probs, cotangent, back_y)
    input_grad = combine(routes, back_dx)
    grad_in = (kept_in[0] + got_in[0].astype(F32) + far_in.astype(F32)) * 0.25
    grad_out = (kept_out[0] + got_out[0].astype(F32) + far_out.astype(F32)) * 0.25
    return (layer_out[None], input_grad[None], prob_grad[None], grad_in[None], grad_out[None])


def solution(mesh):
    tokens = P("sample", "expert", None)
    noise = P("sample", "expert", None, None)
    experts = P("expert", None, None)
    in_specs = (tokens, tokens, tokens, tokens, experts, experts, noise, noise)
    out_specs = (tokens, tokens, tokens, P("expert", "sample", None), P("expert", None, "sample"))
    return jax.shard_map(shards, mesh=mesh, in_specs=in_specs, out_specs=out_specs, check_vma=False)
```

time: 547 us -> 336 us (0.61); the launches traced: 537 us -> 334 us
  local copies, waits for them, and re-layouts: 184 us -> 10.3 us
  Pallas kernels: 0 us -> 97.3 us
  matrix products: 77.8 us -> 0 us
  other arithmetic: 35.4 us -> 9.34 us
  between operations: 14.6 us -> 0.81 us
    pallas_call x0 -> x14, Pallas kernels: none -> 97.3 us  [the longest x2 16.1 us: weight_in_grads(): pl.pallas_call(weight_in_kernel, grid_spec=pltpu.PrefetchScalarGridSpec(n...]
    dot_general x6 -> x0, matrix products: 77.8 us -> none  [the longest x1 21.6 us: backward_rows(): jnp.einsum('sjnf,jdf->sjnd', grad_mix, weight_in, preferred_element_type=...]
    ppermute x0 -> x4, waiting for transfers between devices: none -> 76.5 us  [across(): return lax.ppermute(value, ('sample', 'expert'), pairs)]
    all_to_all x5 -> x4, waiting for transfers between devices: 180 us -> 105 us  [exchange(): lax.all_to_all(value, 'expert', split_axis=0, concat_axis=0, tiled=True)]
    mul x8 -> x0, local copies, waits for them, and re-layouts: 48.3 us -> none  [the longest x7 48.2 us: tile_scale(): return (blocks * noise[:, :, None, :, None]).reshape(batch, height, breadth)]
    reshape x6 -> x0, local copies, waits for them, and re-layouts: 43.4 us -> none  [the longest x2 20.8 us: tile_scale(): return (blocks * noise[:, :, None, :, None]).reshape(batch, height, breadth)]
    gather x4 -> x0, local copies, waits for them, and re-layouts: 34.8 us -> none  [the longest x1 11.6 us: shards(): returned.reshape(experts * capacity, model_width)[position]]
    dot_general x4 -> x0, local copies, waits for them, and re-layouts: 27.8 us -> none  [the longest x2 15.7 us: shards(): jnp.einsum('sjnd,sjnf->jdf', inputs_all, mixes_all, preferred_element_typ...]
  transfers between devices with their start and end apart: 7 -> 8, of which waited for: 5 -> 4; matrix products, arithmetic and copies ran while one was open for 41% -> 2% of each run, Pallas kernels for 0% -> 28%
where the time goes in v1:
time: 336 us; the launch traced here: 334 us
  waiting for transfers between devices  181 us (54%)
  Pallas kernels  97.3 us (29%)
  starting transfers between devices  34.9 us (10%)
  local copies, waits for them, and re-layouts  10.3 us (3%)
  other arithmetic  9.34 us (3%)
    all_to_all x4, waiting for transfers between devices, exchange(): lax.all_to_all(value, 'expert', split_axis=0, concat_axis=0, tiled=True)  105 us
    ppermute x4, waiting for transfers between devices, across(): return lax.ppermute(value, ('sample', 'expert'), pairs)  76.5 us
    all_to_all x4, starting transfers between devices, exchange(): lax.all_to_all(value, 'expert', split_axis=0, concat_axis=0, tiled=True)  26.3 us
    pallas_call x2, Pallas kernels, weight_in_grads(): pl.pallas_call(weight_in_kernel, grid_spec=pltpu.PrefetchScalarGridSpec(n...  16.1 us
    pallas_call x1, Pallas kernels, gate_up(): pl.pallas_call(gate_up_kernel, grid=(wide,), out_shape=(jax.ShapeDtypeStr...  13 us
    pallas_call x1, Pallas kernels, input_grads(): pl.pallas_call(input_grad_kernel, grid=(D // 256,), out_shape=jax.ShapeDt...  12.3 us
    pallas_call x2, Pallas kernels, noisy(): pl.pallas_call(noisy_kernel, grid=(height // 256,), out_shape=jax.ShapeDt...  11.3 us
    pallas_call x1, Pallas kernels, mix(): pl.pallas_call(mix_kernel, grid=(FF // 256,), out_shape=(jax.ShapeDtypeSt...  10.5 us
  transfers between devices with their start and end apart: 8, of which 4 were waited for; matrix products, arithmetic and copies ran while one was open for 2% of the time, Pallas kernels for 28%

profile of v1, /device:TPU:1, one launch (start us, length us, event | category | flops | bytes accessed | tf_op | source)
XLA Modules:
  0.0 334.2 jit_solution(3505923827068803109)
XLA Ops:
  7.5 9.5 %all-to-all-start = ((bf16[32,528,128]{2,1,0:T(8,128)(2,1)}), bf16[32,528,128]{2,1,0:T(8,128)(2,1)}, u32[]{:S(2)}, u32[]{:S(2)}) async-start(bf16[32,528,128]{2,1,0:T(8,128)(2,1)} %copy-done.1), calls=%async_computation | async-start | bytes 8650752 | tf_op jit(solution)/shard_map/all_to_all | solution.py:405
  21.5 56.4 %all-to-all-done.packed_ref = bf16[32,528,128]{2,1,0:T(8,128)(2,1)} async-done(((bf16[32,528,128]{2,1,0:T(8,128)(2,1)}), bf16[32,528,128]{2,1,0:T(8,128)(2,1)}, u32[]{:S(2)}, u32[]{:S(2)}) %all-to-all-start) | async-done | bytes 4325408 | tf_op jit(solution)/shard_map/all_to_all | solution.py:405
  77.9 5.1 %all-to-all-start.2 = ((bf16[32,528,128]{2,1,0:T(8,128)(2,1)}), bf16[32,528,128]{2,1,0:T(8,128)(2,1)}, u32[]{:S(2)}, u32[]{:S(2)}) async-start(bf16[32,528,128]{2,1,0:T(8,128)(2,1)} %copy-done), calls=%async_computation.2 | async-start | bytes 8650752 | tf_op jit(solution)/shard_map/all_to_all | solution.py:405
  83.1 2.9 shard_map.122.weight_ref
  86.0 8.4 %shard_map.120.gate_w_ref.up_w_ref.weight_ref = bf16[2048,1536]{1,0:T(8,128)(2,1)} custom-call(f32[8,6]{1,0:T(8,128)S(1)} %bitcast.50, bf16[2048,1536]{1,0:T(8,128)(2,1)} %bitcast.56), custom_call_target="tpu_custom_call" | custom-call | flops 3145728 | bytes 12582912 | tf_op jit(solution)/shard_map/pallas_call | solution.py:123
  94.4 13.0 %shard_map.121 = (bf16[1056,2048]{1,0:T(8,128)(2,1)}, f32[1056,768]{1,0:T(8,128)S(1)}, f32[1056,768]{1,0:T(8,128)}, bf16[1056,768]{1,0:T(8,128)(2,1)S(1)}) custom-call(bf16[32,528,128]{2,1,0:T(8,128)(2,1)} %all-to-all-done.packed_ref, bf16[2048,1536]{1,0:T(8,128)(2,1)} %shard_map.120.gate_w_ref.up_w_ref.weight_ref, ...), custom_call_target="tpu_custom_call" | custom-call | flops 6643777536 | bytes 23052288 | tf_op jit(solution)/shard_map/pallas_call | solution.py:173
  109.1 7.7 %shard_map.123 = bf16[32,528,128]{2,1,0:T(8,128)(2,1)} custom-call(bf16[1056,768]{1,0:T(8,128)(2,1)S(1)} %get-tuple-element.14.hidden_ref, bf16[768,2048]{1,0:T(8,128)(2,1)S(1)} %shard_map.122.weight_ref), custom_call_target="tpu_custom_call" | custom-call | flops 3321888768 | bytes 9093120 | tf_op jit(solution)/shard_map/pallas_call | solution.py:204
  118.0 22.9 %all-to-all-done.2.packed_ref = bf16[32,528,128]{2,1,0:T(8,128)(2,1)} async-done(((bf16[32,528,128]{2,1,0:T(8,128)(2,1)}), bf16[32,528,128]{2,1,0:T(8,128)(2,1)}, u32[]{:S(2)}, u32[]{:S(2)}) %all-to-all-start.2) | async-done | bytes 4325408 | tf_op jit(solution)/shard_map/all_to_all | solution.py:405
  140.9 6.4 %all-to-all-start.1 = ((bf16[32,528,128]{2,1,0:T(8,128)(2,1)}), bf16[32,528,128]{2,1,0:T(8,128)(2,1)}, u32[]{:S(2)}, u32[]{:S(2)}) async-start(bf16[32,528,128]{2,1,0:T(8,128)(2,1)} %shard_map.123), calls=%async_computation.1 | async-start | bytes 8650752 | tf_op jit(solution)/shard_map/all_to_all | solution.py:405
  147.4 10.5 %shard_map.126 = (bf16[1056,2048]{1,0:T(8,128)(2,1)}, bf16[1056,768]{1,0:T(8,128)(2,1)S(1)}, bf16[1056,768]{1,0:T(8,128)(2,1)S(1)}) custom-call(bf16[32,528,128]{2,1,0:T(8,128)(2,1)} %all-to-all-done.2.packed_ref, bf16[768,2048]{1,0:T(8,128)(2,1)} %copy-done.2, f32[1056,768]{1,0:T(8,128)} %copy-done.5, f32[1056,768]{1,0:T(8,128)} %get-tuple-element.17.up_ref), custom_call_target="tpu_custom_call" | custom-call | flops 3321888768 | bytes 21528576 | tf_op jit(solution)/shard_map/pallas_call | solution.py:234
  158.0 8.0 %shard_map.130 = bf16[2,512,1536]{2,1,0:T(8,128)(2,1)} custom-call(s32[2]{0:T(128)S(1)} %get-tuple-element.28.share_ref, f32[8,6]{1,0:T(8,128)S(1)} %bitcast.51, bf16[1056,2048]{1,0:T(8,128)(2,1)} %get-tuple-element.21.rows_ref, bf16[1056,768]{1,0:T(8,128)(2,1)S(1)} %get-tuple-element.18.gate_grad_ref, bf16[1056,768]{1,0:T(8,128)(2,1)S(1)} %get-tuple-element.19.up_grad_ref), custom_call_target="tpu_custom_call" | custom-call | flops 3321888768 | bytes 11698176 | tf_op jit(solution)/shard_map/pallas_call | solution.py:291
  167.9 12.3 %shard_map.127 = bf16[32,528,128]{2,1,0:T(8,128)(2,1)} custom-call(bf16[1056,768]{1,0:T(8,128)(2,1)S(1)} %get-tuple-element.18.gate_grad_ref, bf16[1056,768]{1,0:T(8,128)(2,1)S(1)} %get-tuple-element.19.up_grad_ref, bf16[2048,1536]{1,0:T(8,128)(2,1)} %shard_map.120.gate_w_ref.up_w_ref.weight_ref), custom_call_target="tpu_custom_call" | custom-call | flops 6643777536 | bytes 13860864 | tf_op jit(solution)/shard_map/pallas_call | solution.py:267
  180.2 25.7 %all-to-all-done.1.packed_ref = bf16[32,528,128]{2,1,0:T(8,128)(2,1)} async-done(((bf16[32,528,128]{2,1,0:T(8,128)(2,1)}), bf16[32,528,128]{2,1,0:T(8,128)(2,1)}, u32[]{:S(2)}, u32[]{:S(2)}) %all-to-all-start.1) | async-done | bytes 4325408 | tf_op jit(solution)/shard_map/all_to_all | solution.py:405
  205.9 5.3 %all-to-all-start.3 = ((bf16[32,528,128]{2,1,0:T(8,128)(2,1)}), bf16[32,528,128]{2,1,0:T(8,128)(2,1)}, u32[]{:S(2)}, u32[]{:S(2)}) async-start(bf16[32,528,128]{2,1,0:T(8,128)(2,1)} %shard_map.127), calls=%async_computation.3 | async-start | bytes 8650752 | tf_op jit(solution)/shard_map/all_to_all | solution.py:405
  211.2 5.0 %shard_map.132 = bf16[2,768,512]{2,1,0:T(8,128)(2,1)S(1)} custom-call(s32[2]{0:T(128)S(1)} %get-tuple-element.28.share_ref, f32[3,8]{1,0:T(4,128)S(1)} %bitcast.54, bf16[1056,768]{1,0:T(8,128)(2,1)S(1)} %copy-done.4, bf16[1056,2048]{1,0:T(8,128)(2,1)} %get-tuple-element.22.rows_ref), custom_call_target="tpu_custom_call" | custom-call | flops 1660944384 | bytes 6930432 | tf_op jit(solution)/shard_map/pallas_call | solution.py:319
  216.3 2.6 collective-permute-start.2
  218.9 5.4 %shard_map.131 = f32[2,768,512]{2,1,0:T(8,128)S(1)} custom-call(s32[2]{0:T(128)S(1)} %get-tuple-element.29.share_ref, f32[3,8]{1,0:T(4,128)S(1)} %bitcast.55, bf16[1056,768]{1,0:T(8,128)(2,1)S(1)} %copy-done.4, bf16[1056,2048]{1,0:T(8,128)(2,1)} %get-tuple-element.22.rows_ref), custom_call_target="tpu_custom_call" | custom-call | flops 1660944384 | bytes 6930432 | tf_op jit(solution)/shard_map/pallas_call | solution.py:319
  224.4 8.1 %shard_map.129 = f32[2,512,1536]{2,1,0:T(8,128)} custom-call(s32[2]{0:T(128)S(1)} %get-tuple-element.29.share_ref, f32[8,6]{1,0:T(8,128)S(1)} %bitcast.52, bf16[1056,2048]{1,0:T(8,128)(2,1)} %get-tuple-element.21.rows_ref, bf16[1056,768]{1,0:T(8,128)(2,1)S(1)} %copy-done.9, bf16[1056,768]{1,0:T(8,128)(2,1)S(1)} %copy-done.11), custom_call_target="tpu_custom_call" | custom-call | flops 3321888768 | bytes 11698176 | tf_op jit(solution)/shard_map/pallas_call | solution.py:291
  232.5 2.8 fusion.5
  235.3 3.8 %collective-permute-start.1 = (bf16[512,1536]{1,0:T(8,128)(2,1)S(1)}, bf16[512,1536]{1,0:T(8,128)(2,1)S(1)}, u32[]{:S(2)}, u32[]{:S(2)}) collective-permute-start(bf16[512,1536]{1,0:T(8,128)(2,1)S(1)} %fusion.5), channel_id=1, source_target_pairs={{0,64},{1,65},{2,66},{3,67},{4,68},{5,69},{6,70},{7,71},{8,72},{9,... | collective-permute-start | bytes 4718600 | tf_op jit(solution)/shard_map/ppermute | solution.py:410
  239.6 76.5 %collective-permute-done.3 = bf16[768,512]{1,0:T(8,128)(2,1)S(1)} collective-permute-done((bf16[768,512]{1,0:T(8,128)(2,1)S(1)}, bf16[768,512]{1,0:T(8,128)(2,1)S(1)}, u32[]{:S(2)}, u32[]{:S(2)}) %collective-permute-start.3) | collective-permute-done | bytes 786464 | tf_op jit(solution)/shard_map/ppermute | solution.py:410
  317.6 5.9 %shard_map.124 = (bf16[128,2048]{1,0:T(8,128)(2,1)}, f32[128,8]{1,0:T(8,128)S(1)}) custom-call(s32[128,8]{1,0:T(8,128)S(1)} %bitcast.43, bf16[128,8]{1,0:T(8,128)(2,1)S(1)} %bitcast.47, bf16[128,2048]{1,0:T(8,128)(2,1)S(1)} %bitcast.40, bf16[32,528,128]{2,1,0:T(8,128)(2,1)} %all-to-all-done.1.packed_ref), custom_call_target="tpu_custom_call" | custom-call | flops 1107296256 | bytes 5373952 | tf_op jit(solution)/shard_map/pallas_call | solution.py:392
  324.2 5.3 %shard_map.128 = bf16[128,2048]{1,0:T(8,128)(2,1)} custom-call(s32[128,8]{1,0:T(8,128)S(1)} %bitcast.44, bf16[32,528,128]{2,1,0:T(8,128)(2,1)} %all-to-all-done.3.packed_ref), custom_call_target="tpu_custom_call" | custom-call | flops 553648128 | bytes 4849664 | tf_op jit(solution)/shard_map/pallas_call | solution.py:362
  329.5 4.7 %fusion.4 = f32[1,512,1536]{2,1,0:T(8,128)} fusion(f32[2,512,1536]{2,1,0:T(8,128)} %shard_map.129, bf16[512,1536]{1,0:T(8,128)(2,1)S(1)} %collective-permute-done.1, bf16[2,512,1536]{2,1,0:T(8,128)(2,1)} %collective-permute-done), kind=kLoop, calls=%fused_computation.6 | loop fusion | flops 3932160 | bytes 9437184 | tf_op jit(solution)/shard_map/broadcast_in_dim | solution.py:444
  (46 shorter events, 19.0 us)
Async XLA Ops:
  2.2 1.0 copy-start.12
  5.5 2.0 copy-start.1
  7.5 9.5 %copy-start.6 = (bf16[1,128,2048]{2,1,0:T(8,128)(2,1)S(1)}, bf16[1,128,2048]{2,1,0:T(8,128)(2,1)}, u32[]{:S(2)}) copy-start(bf16[1,128,2048]{2,1,0:T(8,128)(2,1)} %param.11) | copy-start | bytes 1572868
  7.5 70.4 %all-to-all-start = ((bf16[32,528,128]{2,1,0:T(8,128)(2,1)}), bf16[32,528,128]{2,1,0:T(8,128)(2,1)}, u32[]{:S(2)}, u32[]{:S(2)}) async-start(bf16[32,528,128]{2,1,0:T(8,128)(2,1)} %copy-done.1), calls=%async_computation | async-start | bytes 8650752 | tf_op jit(solution)/shard_map/all_to_all | solution.py:405
  19.4 2.1 copy-start
  21.5 61.5 %copy-start.13 = (f32[1,1,8,6]{2,1,3,0:T(1,128)S(1)}, f32[1,1,8,6]{2,1,3,0:T(1,128)}, u32[]{:S(2)}) copy-start(f32[1,1,8,6]{2,1,3,0:T(1,128)} %param.14) | copy-start | bytes 580
  21.5 61.6 %copy-start.14 = (f32[1,1,3,8]{3,1,2,0:T(1,128)S(1)}, f32[1,1,3,8]{3,1,2,0:T(1,128)}, u32[]{:S(2)}) copy-start(f32[1,1,3,8]{3,1,2,0:T(1,128)} %param.15) | copy-start | bytes 292
  77.9 63.0 %all-to-all-start.2 = ((bf16[32,528,128]{2,1,0:T(8,128)(2,1)}), bf16[32,528,128]{2,1,0:T(8,128)(2,1)}, u32[]{:S(2)}, u32[]{:S(2)}) async-start(bf16[32,528,128]{2,1,0:T(8,128)(2,1)} %copy-done), calls=%async_computation.2 | async-start | bytes 8650752 | tf_op jit(solution)/shard_map/all_to_all | solution.py:405
  86.0 23.1 %copy-start.2 = (bf16[768,2048]{1,0:T(8,128)(2,1)}, bf16[768,2048]{1,0:T(8,128)(2,1)S(1)}, u32[]{:S(2)}) copy-start(bf16[768,2048]{1,0:T(8,128)(2,1)S(1)} %shard_map.122.weight_ref) | copy-start | bytes 9437188
  107.4 1.7 copy-start.5
  116.8 1.2 copy-start.3
  140.9 65.0 %all-to-all-start.1 = ((bf16[32,528,128]{2,1,0:T(8,128)(2,1)}), bf16[32,528,128]{2,1,0:T(8,128)(2,1)}, u32[]{:S(2)}, u32[]{:S(2)}) async-start(bf16[32,528,128]{2,1,0:T(8,128)(2,1)} %shard_map.123), calls=%async_computation.1 | async-start | bytes 8650752 | tf_op jit(solution)/shard_map/all_to_all | solution.py:405
  158.0 9.9 %copy-start.8 = (bf16[1056,768]{1,0:T(8,128)(2,1)}, bf16[1056,768]{1,0:T(8,128)(2,1)S(1)}, u32[]{:S(2)}) copy-start(bf16[1056,768]{1,0:T(8,128)(2,1)S(1)} %get-tuple-element.18.gate_grad_ref) | copy-start | bytes 4866052
  158.0 9.9 %copy-start.10 = (bf16[1056,768]{1,0:T(8,128)(2,1)}, bf16[1056,768]{1,0:T(8,128)(2,1)S(1)}, u32[]{:S(2)}) copy-start(bf16[1056,768]{1,0:T(8,128)(2,1)S(1)} %get-tuple-element.19.up_grad_ref) | copy-start | bytes 4866052
  166.0 66.5 %collective-permute-start = (bf16[2,512,1536]{2,1,0:T(8,128)(2,1)}, bf16[2,512,1536]{2,1,0:T(8,128)(2,1)}, u32[]{:S(2)}, u32[]{:S(2)}) collective-permute-start(bf16[2,512,1536]{2,1,0:T(8,128)(2,1)} %shard_map.130), channel_id=1, source_target_pairs={{0,32},{1,33},{2,34},{3,35},{4,36},{5,37},{6,38},{7,39},{8,40},{9,... | collective-permute-start | bytes 9437192 | tf_op jit(solution)/shard_map/ppermute | solution.py:410
  180.2 31.0 %copy-start.4 = (bf16[1056,768]{1,0:T(8,128)(2,1)S(1)}, bf16[1056,768]{1,0:T(8,128)(2,1)}, u32[]{:S(2)}) copy-start(bf16[1056,768]{1,0:T(8,128)(2,1)} %copy-done.3) | copy-start | bytes 4866052
  205.9 118.3 %all-to-all-start.3 = ((bf16[32,528,128]{2,1,0:T(8,128)(2,1)}), bf16[32,528,128]{2,1,0:T(8,128)(2,1)}, u32[]{:S(2)}, u32[]{:S(2)}) async-start(bf16[32,528,128]{2,1,0:T(8,128)(2,1)} %shard_map.127), calls=%async_computation.3 | async-start | bytes 8650752 | tf_op jit(solution)/shard_map/all_to_all | solution.py:405
  216.3 22.8 %collective-permute-start.2 = (bf16[2,768,512]{2,1,0:T(8,128)(2,1)S(1)}, bf16[2,768,512]{2,1,0:T(8,128)(2,1)S(1)}, u32[]{:S(2)}, u32[]{:S(2)}) collective-permute-start(bf16[2,768,512]{2,1,0:T(8,128)(2,1)S(1)} %shard_map.132), channel_id=1, source_target_pairs={{0,32},{1,33},{2,34},{3,35},{4,36},{5,37},{6,38},{7,39},{8,40},{9,... | collective-permute-start | bytes 4718600 | tf_op jit(solution)/shard_map/ppermute | solution.py:410
  218.9 5.4 %copy-start.9 = (bf16[1056,768]{1,0:T(8,128)(2,1)S(1)}, bf16[1056,768]{1,0:T(8,128)(2,1)}, u32[]{:S(2)}) copy-start(bf16[1056,768]{1,0:T(8,128)(2,1)} %copy-done.8) | copy-start | bytes 4866052
  218.9 5.4 %copy-start.11 = (bf16[1056,768]{1,0:T(8,128)(2,1)S(1)}, bf16[1056,768]{1,0:T(8,128)(2,1)}, u32[]{:S(2)}) copy-start(bf16[1056,768]{1,0:T(8,128)(2,1)} %copy-done.10) | copy-start | bytes 4866052
  235.3 94.2 %collective-permute-start.1 = (bf16[512,1536]{1,0:T(8,128)(2,1)S(1)}, bf16[512,1536]{1,0:T(8,128)(2,1)S(1)}, u32[]{:S(2)}, u32[]{:S(2)}) collective-permute-start(bf16[512,1536]{1,0:T(8,128)(2,1)S(1)} %fusion.5), channel_id=1, source_target_pairs={{0,64},{1,65},{2,66},{3,67},{4,68},{5,69},{6,70},{7,71},{8,72},{9,... | collective-permute-start | bytes 4718600 | tf_op jit(solution)/shard_map/ppermute | solution.py:410
  239.3 78.3 %copy-start.7 = (bf16[1,128,2048]{2,1,0:T(8,128)(2,1)S(1)}, bf16[1,128,2048]{2,1,0:T(8,128)(2,1)}, u32[]{:S(2)}) copy-start(bf16[1,128,2048]{2,1,0:T(8,128)(2,1)} %param.11) | copy-start | bytes 1572868
  239.3 76.8 %collective-permute-start.3 = (bf16[768,512]{1,0:T(8,128)(2,1)S(1)}, bf16[768,512]{1,0:T(8,128)(2,1)S(1)}, u32[]{:S(2)}, u32[]{:S(2)}) collective-permute-start(bf16[768,512]{1,0:T(8,128)(2,1)S(1)} %fusion.11), channel_id=1, source_target_pairs={{0,64},{1,65},{2,66},{3,67},{4,68},{5,69},{6,70},{7,71},{8,72},{9,... | collective-permute-start | bytes 2359304 | tf_op jit(solution)/shard_map/ppermute | solution.py:410

commit v2 on v1

--- a/solution.py
+++ b/solution.py
@@ -29,7 +29,7 @@
 
 
 def cost(flops, moved):
-    return pl.CostEstimate(flops=flops, bytes_accessed=moved, transcendentals=0)
+    return pl.CostEstimate(flops=flops // 1000, bytes_accessed=moved // 1000, transcendentals=0)
 
 
 def iota(shape, dim):
@@ -48,21 +48,24 @@
     return lax.dot_general(a, b, (((0,), (0,)), ((), ())), preferred_element_type=F32)
 
 
+AFTER = pl.BlockSpec(memory_space=pl.ANY)
+
+
 def slot_keys(routes):
-    lane = iota((TOK, LANES), 1)
-    chosen = jnp.zeros((TOK, LANES), F32)
+    expert = iota((LANES, TOK), 0)
+    chosen = jnp.zeros((LANES, TOK), F32)
     for k in range(TOP):
-        chosen = jnp.where(routes[:, k : k + 1] == lane, 1.0, chosen)
-    earlier = jnp.where(iota((TOK, TOK), 0) > iota((TOK, TOK), 1), 1.0, 0.0).astype(BF16)
-    rank = dot(earlier, chosen.astype(BF16))
+        chosen = jnp.where(routes[k : k + 1, :] == expert, 1.0, chosen)
+    earlier = jnp.where(iota((TOK, TOK), 0) < iota((TOK, TOK), 1), 1.0, 0.0).astype(BF16)
+    rank = dot(chosen.astype(BF16), earlier)
     return jnp.where(chosen > 0.0, rank, -1.0)
 
 
 def expert_weights(routes, probs):
-    lane = iota((TOK, LANES), 1)
-    weight = jnp.zeros((TOK, LANES), F32)
+    expert = iota((LANES, TOK), 0)
+    weight = jnp.zeros((LANES, TOK), F32)
     for k in range(TOP):
-        weight = jnp.where(routes[:, k : k + 1] == lane, probs[:, k : k + 1].astype(F32), weight)
+        weight = jnp.where(routes[k : k + 1, :] == expert, probs[k : k + 1, :].astype(F32), weight)
     return weight
 
 
@@ -79,46 +82,54 @@
     return dot(last_slot_order(True), flat).astype(BF16)
 
 
-def dispatch_kernel(weighted, routes_ref, probs_ref, value_ref, out_ref, last_ref):
+def dispatch_kernel(
+    routes_ref, probs_ref, tokens_ref, cotangent_ref, after_ref, x_ref, dy_ref, last_x_ref, last_dy_ref
+):
     routes = routes_ref[...]
-    key = slot_keys(routes).T
+    key = slot_keys(routes)
+    weight = expert_weights(routes, probs_ref[...])
     spread = jnp.where(iota((BIG, LANES), 0) // MAIN == iota((BIG, LANES), 1), 1.0, 0.0).astype(BF16)
     hit = dot(spread, key.astype(BF16)) == (iota((BIG, TOK), 0) % MAIN).astype(F32)
     last_hit = key[:BLOCKS] == float(MAIN)
-    if weighted:
-        weight = expert_weights(routes, probs_ref[...]).T
-        pick = jnp.where(hit, dot(spread, weight.astype(BF16)), 0.0).astype(BF16)
-        last_pick = jnp.where(last_hit, weight[:BLOCKS], 0.0).astype(BF16)
-    else:
-        pick = jnp.where(hit, 1.0, 0.0).astype(BF16)
-        last_pick = jnp.where(last_hit, 1.0, 0.0).astype(BF16)
-    for j in range(COLS):
-        value = value_ref[:, j * LANES : (j + 1) * LANES]
-        rows = dot(pick, value).astype(BF16)
-        out_ref[:, j * MAIN : (j + 1) * MAIN, :] = rows.reshape(BLOCKS, MAIN, LANES)
-        last_ref[j * BLOCKS : (j + 1) * BLOCKS, :] = dot(last_pick, value).astype(BF16)
-    tiles = dot(last_slot_order(False), last_ref[...]).astype(BF16)
-    out_ref[:, MAIN * COLS :, :] = tiles.reshape(BLOCKS, COLS, LANES)
-
-
-def dispatch(routes, probs, value, weighted):
-    return pl.pallas_call(
-        functools.partial(dispatch_kernel, weighted),
-        out_shape=jax.ShapeDtypeStruct((BLOCKS, PACK, LANES), BF16),
-        scratch_shapes=[pltpu.VMEM((BLOCKS * COLS, LANES), BF16)],
-        compiler_params=params(),
-        cost_estimate=cost(2 * ROWS * TOK * D, 2 * (ROWS + TOK) * D),
-    )(routes, probs, value)
-
-
-def noisy_kernel(noise_ref, weight_ref, out_ref):
+    order = last_slot_order(False)
+
+    def send(value_ref, pick, last_pick, out_ref, last_ref):
+        for j in range(COLS):
+            value = value_ref[:, j * LANES : (j + 1) * LANES]
+            rows = dot(pick, value).astype(BF16)
+            out_ref[:, j * MAIN : (j + 1) * MAIN, :] = rows.reshape(BLOCKS, MAIN, LANES)
+            last_ref[j * BLOCKS : (j + 1) * BLOCKS, :] = dot(last_pick, value).astype(BF16)
+        tiles = dot(order, last_ref[...]).astype(BF16)
+        out_ref[:, MAIN * COLS :, :] = tiles.reshape(BLOCKS, COLS, LANES)
+
+    pick = jnp.where(hit, 1.0, 0.0).astype(BF16)
+    last_pick = jnp.where(last_hit, 1.0, 0.0).astype(BF16)
+    send(tokens_ref, pick, last_pick, x_ref, last_x_ref)
+    pick = jnp.where(hit, dot(spread, weight.astype(BF16)), 0.0).astype(BF16)
+    last_pick = jnp.where(last_hit, weight[:BLOCKS], 0.0).astype(BF16)
+    send(cotangent_ref, pick, last_pick, dy_ref, last_dy_ref)
+
+
+def dispatch(routes, probs, tokens, cotangent, after):
+    packed = jax.ShapeDtypeStruct((BLOCKS, PACK, LANES), BF16)
+    return pl.pallas_call(
+        dispatch_kernel,
+        out_shape=(packed, packed),
+        in_specs=[pl.BlockSpec(memory_space=pltpu.VMEM)] * 4 + [AFTER],
+        scratch_shapes=[pltpu.VMEM((BLOCKS * COLS, LANES), BF16)] * 2,
+        compiler_params=params(),
+        cost_estimate=cost(4 * ROWS * TOK * D, 4 * (ROWS + TOK) * D),
+    )(routes, probs, tokens, cotangent, after)
+
+
+def noisy_kernel(noise_ref, weight_ref, after_ref, out_ref):
     row = pl.program_id(0)
     for c in range(weight_ref.shape[1] // 256):
         cut = slice(c * 256, (c + 1) * 256)
         out_ref[:, cut] = (weight_ref[:, cut].astype(F32) * noise_ref[row, c]).astype(BF16)
 
 
-def noisy(weight, noise):
+def noisy(weight, noise, after):
     height, breadth = weight.shape
     return pl.pallas_call(
         noisy_kernel,
@@ -127,11 +138,12 @@
         in_specs=[
             pl.BlockSpec(memory_space=pltpu.SMEM),
             pl.BlockSpec((256, breadth), lambda i: (i, 0)),
+            AFTER,
         ],
         out_specs=pl.BlockSpec((256, breadth), lambda i: (i, 0)),
         compiler_params=params(),
         cost_estimate=cost(height * breadth, 4 * height * breadth),
-    )(noise, weight)
+    )(noise, weight, after)
 
 
 def unpack_rows(packed_ref, rows_ref):
@@ -216,7 +228,7 @@
     )(hidden, weight_out)
 
 
-def mix_kernel(packed_ref, weight_ref, gate_ref, up_ref, rows_ref, gate_grad_ref, up_grad_ref):
+def mix_kernel(packed_ref, weight_ref, gate_ref, up_ref, after_ref, rows_ref, gate_grad_ref, up_grad_ref):
     @pl.when(pl.program_id(0) == 0)
     def _():
         unpack_rows(packed_ref, rows_ref)
@@ -229,7 +241,7 @@
     up_grad_ref[...] = (grad * gate * sigma).astype(BF16)
 
 
-def mix(packed, weight_out, gate, up):
+def mix(packed, weight_out, gate, up, after):
     part = pl.BlockSpec((ROWS, 256), lambda i: (0, i))
     return pl.pallas_call(
         mix_kernel,
@@ -244,14 +256,15 @@
             pl.BlockSpec((256, D), lambda i: (i, 0)),
             part,
             part,
+            AFTER,
         ],
         out_specs=(pl.BlockSpec((ROWS, D), lambda i: (0, 0)), part, part),
         compiler_params=params(),
         cost_estimate=cost(2 * ROWS * D * FF, 4 * ROWS * D + 2 * D * FF + 12 * ROWS * FF),
-    )(packed, weight_out, gate, up)
-
-
-def input_grad_kernel(gate_grad_ref, up_grad_ref, weight_ref, out_ref, last_ref):
+    )(packed, weight_out, gate, up, after)
+
+
+def input_grad_kernel(gate_grad_ref, up_grad_ref, weight_ref, after_in, after_out, out_ref, last_ref):
     step = pl.program_id(0)
     values = dot_nt(gate_grad_ref[...], weight_ref[:, :FF])
     values = (values + dot_nt(up_grad_ref[...], weight_ref[:, FF:])).astype(BF16)
@@ -262,21 +275,21 @@
         pack_last(out_ref, last_ref)
 
 
-def input_grads(gate_grad, up_grad, weight_in):
+def input_grads(gate_grad, up_grad, weight_in, after):
     whole = pl.BlockSpec((ROWS, FF), lambda i: (0, 0))
     return pl.pallas_call(
         input_grad_kernel,
         grid=(D // 256,),
         out_shape=jax.ShapeDtypeStruct((BLOCKS, PACK, LANES), BF16),
-        in_specs=[whole, whole, pl.BlockSpec((256, 2 * FF), lambda i: (i, 0))],
+        in_specs=[whole, whole, pl.BlockSpec((256, 2 * FF), lambda i: (i, 0)), AFTER, AFTER],
         out_specs=pl.BlockSpec((BLOCKS, PACK, LANES), lambda i: (0, 0, 0)),
         scratch_shapes=[pltpu.VMEM((BLOCKS * COLS, LANES), BF16)],
         compiler_params=params(),
         cost_estimate=cost(4 * ROWS * D * FF, 2 * ROWS * D + 4 * D * FF + 4 * ROWS * FF),
-    )(gate_grad, up_grad, weight_in)
-
-
-def weight_in_kernel(share_ref, noise_ref, rows_ref, gate_grad_ref, up_grad_ref, out_ref):
+    )(gate_grad, up_grad, weight_in, *after)
+
+
+def weight_in_kernel(share_ref, noise_ref, rows_ref, gate_grad_ref, up_grad_ref, after_ref, out_ref):
     tile = share_ref[pl.program_id(0)] * 2 + pl.program_id(1)
     for half, grad_ref in enumerate((gate_grad_ref, up_grad_ref)):
         raw = dot_tn(rows_ref[...], grad_ref[...])
@@ -286,7 +299,7 @@
             out_ref[0, :, at : at + 256] = scaled.astype(out_ref.dtype)
 
 
-def weight_in_grads(shares, noise, rows, gate_grad, up_grad, dtype):
+def weight_in_grads(shares, noise, rows, gate_grad, up_grad, dtype, after):
     whole = pl.BlockSpec((ROWS, FF), lambda j, i, s: (0, 0))
     return pl.pallas_call(
         weight_in_kernel,
@@ -298,13 +311,14 @@
                 pl.BlockSpec((ROWS, 256), lambda j, i, s: (0, s[j] * 2 + i)),
                 whole,
                 whole,
+                AFTER,
             ],
             out_specs=pl.BlockSpec((1, 256, 2 * FF), lambda j, i, s: (j, i, 0)),
         ),
         out_shape=jax.ShapeDtypeStruct((2, 512, 2 * FF), dtype),
         compiler_params=params(),
         cost_estimate=cost(2 * ROWS * D * FF, ROWS * D + 4 * ROWS * FF + 4 * D * FF),
-    )(shares, noise, rows, gate_grad, up_grad)
+    )(shares, noise, rows, gate_grad, up_grad, after)
 
 
 def weight_out_kernel(share_ref, noise_ref, hidden_ref, rows_ref, out_ref):
@@ -334,8 +348,8 @@
     )(shares, noise, hidden, rows)
 
 
-def combine_tables(routes, weight):
-    key = slot_keys(routes)
+def combine_tables(key, weight):
+    key = key.T
     spread = jnp.where(iota((LANES, BIG), 1) // MAIN == iota((LANES, BIG), 0), 1.0, 0.0).astype(BF16)
     hit = dot(key.astype(BF16), spread) == (iota((TOK, BIG), 1) % MAIN).astype(F32)
     last_hit = key == float(MAIN)
@@ -343,49 +357,98 @@
         pick = jnp.where(hit, 1.0, 0.0)
         last_pick = jnp.where(last_hit, 1.0, 0.0)
     else:
+        weight = weight.T
         pick = jnp.where(hit, dot(weight.astype(BF16), spread), 0.0)
         last_pick = jnp.where(last_hit, weight, 0.0)
-    return key, pick.astype(BF16), last_pick[:, :BLOCKS].astype(BF16)
-
-
-def combine_kernel(routes_ref, packed_ref, out_ref):
-    _, pick, last_pick = combine_tables(routes_ref[...], None)
-    last = unpack_last(packed_ref[:, MAIN * COLS :, :])
+    return pick.astype(BF16), last_pick[:, :BLOCKS].astype(BF16)
+
+
+def combine_kernel(place_ref, routes_ref, packed_ref, *refs):
+    out_ref = refs[-1]
+    experts = BLOCKS // 2
+    key = slot_keys(routes_ref[...]).T + 1.0
+    plane = place_ref[1]
+
+    def spread(shape, width):
+        return jnp.where(iota(shape, 0) == iota(shape, 1) // width * 2 + plane, 1.0, 0.0).astype(BF16)
+
+    main = (TOK, experts * MAIN)
+    hit = dot(key.astype(BF16), spread((LANES, experts * MAIN), MAIN))
+    pick = jnp.where(hit == (iota(main, 1) % MAIN + 1).astype(F32), 1.0, 0.0).astype(BF16)
+    hit = dot(key.astype(BF16), spread((LANES, LANES), 1))
+    last_pick = jnp.where(hit == float(MAIN + 1), 1.0, 0.0).astype(BF16)[:, :experts]
+
+    count = experts * COLS
+    row, tile = iota((count, count), 0), iota((count, count), 1)
+    order = ((tile // COLS) == (row % experts)) & ((tile % COLS) == (row // experts))
+    last = packed_ref[:, 0, MAIN * COLS :, :].reshape(count, LANES)
+    last = dot(jnp.where(order, 1.0, 0.0).astype(BF16), last).astype(BF16)
     for j in range(COLS):
-        cut = slice(j * LANES, (j + 1) * LANES)
-        rows = packed_ref[:, j * MAIN : (j + 1) * MAIN, :].reshape(BIG, LANES)
-        total = dot(pick, rows) + dot(last_pick, last[j * BLOCKS : (j + 1) * BLOCKS])
-        out_ref[:, cut] = total.astype(BF16)
-
-
-def combine(routes, packed):
+        rows = packed_ref[:, 0, j * MAIN : (j + 1) * MAIN, :].reshape(experts * MAIN, LANES)
+        total = dot(pick, rows) + dot(last_pick, last[j * experts : (j + 1) * experts])
+        out_ref[:, j * LANES : (j + 1) * LANES] = total.astype(out_ref.dtype)
+
+
+def combine(place, routes, packed, dtype, after):
+    experts = BLOCKS // 2
     return pl.pallas_call(
         combine_kernel,
-        out_shape=jax.ShapeDtypeStruct((TOK, D), BF16),
-        compiler_params=params(),
-        cost_estimate=cost(2 * ROWS * TOK * D, 2 * (ROWS + TOK) * D),
-    )(routes, packed)
+        grid_spec=pltpu.PrefetchScalarGridSpec(
+            num_scalar_prefetch=1,
+            grid=(1,),
+            in_specs=[
+                pl.BlockSpec((TOP, TOK), lambda i, p: (0, 0)),
+                pl.BlockSpec((experts, 1, PACK, LANES), lambda i, p: (0, p[0], 0, 0)),
+                *[AFTER] * len(after),
+            ],
+            out_specs=pl.BlockSpec((TOK, D), lambda i, p: (0, 0)),
+        ),
+        out_shape=jax.ShapeDtypeStruct((TOK, D), dtype),
+        compiler_params=params(),
+        cost_estimate=cost(ROWS * TOK * D, (ROWS + 2 * TOK) * D),
+    )(place, routes, packed.reshape(experts, 2, PACK, LANES), *after)
+
+
+def finish_kernel(kept_ref, got_ref, far_ref, after_ref, out_ref):
+    total = kept_ref[0] + got_ref[0].astype(F32) + far_ref[...].astype(F32)
+    out_ref[...] = total * 0.25
+
+
+def finish(kept, got, far, after):
+    height, breadth = far.shape
+    first = pl.BlockSpec((1, 128, breadth), lambda i: (0, i, 0))
+    part = pl.BlockSpec((128, breadth), lambda i: (i, 0))
+    return pl.pallas_call(
+        finish_kernel,
+        grid=(height // 128,),
+        out_shape=jax.ShapeDtypeStruct((height, breadth), F32),
+        in_specs=[first, first, part, AFTER],
+        out_specs=part,
+        compiler_params=params(),
+        cost_estimate=cost(3 * height * breadth, 12 * height * breadth),
+    )(kept, got, far, after)
 
 
 def combine_output_kernel(routes_ref, probs_ref, cotangent_ref, packed_ref, out_ref, grad_ref, rows_ref):
     routes = routes_ref[...]
     unpack_rows(packed_ref, rows_ref)
-    key, pick, last_pick = combine_tables(routes, expert_weights(routes, probs_ref[...]))
+    key = slot_keys(routes)
+    pick, last_pick = combine_tables(key, expert_weights(routes, probs_ref[...]))
     for j in range(D // 256):
         cut = slice(j * 256, (j + 1) * 256)
         total = dot(pick, rows_ref[:BIG, cut]) + dot(last_pick, rows_ref[BIG:, cut])
         out_ref[:, cut] = total.astype(BF16)
-    main = dot_nt(cotangent_ref[...], rows_ref[:BIG, :])
-    last = dot_nt(cotangent_ref[...], rows_ref[BIG:, :])
-    lane = iota((TOK, LANES), 1)
+    main = dot_nt(rows_ref[:BIG, :], cotangent_ref[...])
+    last = dot_nt(rows_ref[BIG:, :], cotangent_ref[...])
     for k in range(TOP):
-        expert = routes[:, k : k + 1]
-        slot = jnp.sum(jnp.where(expert == lane, key, 0.0), axis=1, keepdims=True).astype(jnp.int32)
+        expert = routes[k : k + 1, :]
+        slot = jnp.sum(jnp.where(expert == iota((LANES, TOK), 0), key, 0.0), axis=0, keepdims=True)
+        slot = slot.astype(jnp.int32)
         row = jnp.where(slot < MAIN, expert * MAIN + slot, -1)
-        value = jnp.sum(jnp.where(iota((TOK, BIG), 1) == row, main, 0.0), axis=1, keepdims=True)
+        value = jnp.sum(jnp.where(iota((BIG, TOK), 0) == row, main, 0.0), axis=0, keepdims=True)
         row = jnp.where(slot < MAIN, -1, expert)
-        value += jnp.sum(jnp.where(iota((TOK, BLOCKS), 1) == row, last, 0.0), axis=1, keepdims=True)
-        grad_ref[:, k : k + 1] = value
+        value += jnp.sum(jnp.where(iota((BLOCKS, TOK), 0) == row, last, 0.0), axis=0, keepdims=True)
+        grad_ref[k : k + 1, :] = value
 
 
 def combine_output(routes, probs, cotangent, packed):
@@ -393,7 +456,7 @@
         combine_output_kernel,
         out_shape=(
             jax.ShapeDtypeStruct((TOK, D), BF16),
-            jax.ShapeDtypeStruct((TOK, TOP), F32),
+            jax.ShapeDtypeStruct((TOP, TOK), F32),
         ),
         scratch_shapes=[pltpu.VMEM((ROWS, D), BF16)],
         compiler_params=params(),
@@ -403,6 +466,18 @@
 
 def exchange(value):
     return lax.all_to_all(value, "expert", split_axis=0, concat_axis=0, tiled=True)
+
+
+def exchange_in_plane(value):
+    planes = [list(range(z, BLOCKS, 2)) for z in range(2)]
+    value = value.reshape(BLOCKS // 2, 2 * PACK, LANES)
+    return lax.all_to_all(
+        value, "expert", split_axis=0, concat_axis=0, tiled=True, axis_index_groups=planes
+    )
+
+
+def between_planes(value):
+    return lax.ppermute(value, "expert", [(e, e ^ 1) for e in range(BLOCKS)])
 
 
 def across(value, flip):
@@ -411,37 +486,46 @@
 
 
 def shards(tokens, routes, probs, cotangent, w_gate_up, w_down, gu_noise, down_noise):
-    routes, probs, cotangent = routes[0], probs[0], cotangent[0]
+    routes, probs, cotangent = routes[0].T, probs[0].T, cotangent[0]
     gu_noise, down_noise = gu_noise[0, 0], down_noise[0, 0]
     sample = lax.axis_index("sample")
     ours = jnp.stack([sample, sample ^ 2]).astype(jnp.int32)
     theirs = ours ^ 1
 
-    recv_x = exchange(dispatch(routes, probs, tokens[0], False))
-    send_dy = dispatch(routes, probs, cotangent, True)
-    weight_in = noisy(w_gate_up[0], gu_noise)
-    weight_out = noisy(w_down[0], down_noise)
+    far_routes = between_planes(routes)
+    send_x, send_dy = dispatch(routes, probs, tokens[0], cotangent, far_routes)
+    recv_x = exchange(send_x)
+    weight_in = noisy(w_gate_up[0], gu_noise, recv_x)
+    weight_out = noisy(w_down[0], down_noise, recv_x)
     recv_dy = exchange(send_dy)
     rows_x, gate, up, hidden = gate_up(recv_x, weight_in)
     output = down(hidden, weight_out)
     back_y = exchange(output)
-    rows_dy, gate_grad, up_grad = mix(recv_dy, weight_out, gate, up)
-
-    sent_in = weight_in_grads(theirs, gu_noise, rows_x, gate_grad, up_grad, BF16)
+    rows_dy, gate_grad, up_grad = mix(recv_dy, weight_out, gate, up, output)
+
+    sent_in = weight_in_grads(theirs, gu_noise, rows_x, gate_grad, up_grad, BF16, output)
     got_in = across(sent_in, 1)
     sent_out = weight_out_grads(theirs, down_noise, hidden, rows_dy, BF16)
     got_out = across(sent_out, 1)
-    kept_in = weight_in_grads(ours, gu_noise, rows_x, gate_grad, up_grad, F32)
+    kept_in = weight_in_grads(ours, gu_noise, rows_x, gate_grad, up_grad, F32, output)
     kept_out = weight_out_grads(ours, down_noise, hidden, rows_dy, F32)
-    far_in = across((kept_in[1] + got_in[1].astype(F32)).astype(BF16), 2)
-    far_out = across((kept_out[1] + got_out[1].astype(F32)).astype(BF16), 2)
-    back_dx = exchange(input_grads(gate_grad, up_grad, weight_in))
+    half_in = (kept_in[1] + got_in[1].astype(F32)).astype(BF16)
+    half_out = (kept_out[1] + got_out[1].astype(F32)).astype(BF16)
+    far_in = across(half_in, 2)
+    far_out = across(half_out, 2)
+    send_dx = input_grads(gate_grad, up_grad, weight_in, (half_in, half_out))
+    back_dx = exchange_in_plane(send_dx)
 
     layer_out, prob_grad = combine_output(routes, probs, cotangent, back_y)
-    input_grad = combine(routes, back_dx)
-    grad_in = (kept_in[0] + got_in[0].astype(F32) + far_in.astype(F32)) * 0.25
-    grad_out = (kept_out[0] + got_out[0].astype(F32) + far_out.astype(F32)) * 0.25
-    return (layer_out[None], input_grad[None], prob_grad[None], grad_in[None], grad_out[None])
+    plane = lax.axis_index("expert") % 2
+    place = jnp.stack([1 - plane, plane]).astype(jnp.int32)
+    there = combine(place, far_routes, back_dx, BF16, (layer_out,))
+    place = jnp.stack([plane, plane]).astype(jnp.int32)
+    here = combine(place, routes, back_dx, F32, (there,))
+    grad_in = finish(kept_in, got_in, far_in, there)
+    grad_out = finish(kept_out, got_out, far_out, there)
+    input_grad = (here + between_planes(there).astype(F32)).astype(BF16)
+    return (layer_out[None], input_grad[None], prob_grad.T[None], grad_in[None], grad_out[None])
 
 
 def solution(mesh):

time: 336 us -> 289 us (0.86)
  waiting for transfers between devices: 181 us -> 73.1 us
  blocking collectives: 0 us -> 58.9 us
  Pallas kernels: 97.3 us -> 109 us
  starting transfers between devices: 34.9 us -> 30 us
  other arithmetic: 9.34 us -> 4.92 us
    all_to_all x4 -> x2, waiting for transfers between devices: 105 us -> 18.3 us  [exchange(): lax.all_to_all(value, 'expert', split_axis=0, concat_axis=0, tiled=True)]
    ppermute x4, waiting for transfers between devices: 76.5 us -> 0.01 us  [across(): return lax.ppermute(value, ('sample', 'expert'), pairs)]
    all_to_all x0 -> x1, blocking collectives: none -> 58.9 us  [exchange(): lax.all_to_all(value, 'expert', split_axis=0, concat_axis=0, tiled=True)]
    all_to_all x0 -> x1, waiting for transfers between devices: none -> 53.6 us  [exchange_in_plane(): lax.all_to_all(value, 'expert', split_axis=0, concat_axis=0, tiled=True,...]
    all_to_all x4 -> x2, starting transfers between devices: 26.3 us -> 13 us  [exchange(): lax.all_to_all(value, 'expert', split_axis=0, concat_axis=0, tiled=True)]
    pallas_call x3 -> x5, Pallas kernels: 9.9 us -> 21.6 us  [the longest x2 9.24 us: finish(): pl.pallas_call(finish_kernel, grid=(height // 128,), out_shape=jax.ShapeD...]
    all_to_all x0 -> x1, starting transfers between devices: none -> 6.76 us  [exchange_in_plane(): lax.all_to_all(value, 'expert', split_axis=0, concat_axis=0, tiled=True,...]
    broadcast_in_dim x2 -> x1, other arithmetic: 6.19 us -> 0.9 us  [shards(): input_grad[None]]
  transfers between devices with their start and end apart: 8 -> 9, of which waited for: 4 -> 3; matrix products, arithmetic and copies ran while one was open for 2% -> 1% of each run, Pallas kernels for 28% -> 36%
where the time goes in v2:
time: 289 us; the launch traced here: 287 us
  Pallas kernels  109 us (38%)
  waiting for transfers between devices  73.1 us (25%)
  blocking collectives  58.9 us (20%)
  starting transfers between devices  30 us (10%)
  local copies, waits for them, and re-layouts  10.6 us (4%)
  other arithmetic  4.92 us (2%)
    all_to_all x1, blocking collectives, exchange(): lax.all_to_all(value, 'expert', split_axis=0, concat_axis=0, tiled=True)  58.9 us
    all_to_all x1, waiting for transfers between devices, exchange_in_plane(): lax.all_to_all(value, 'expert', split_axis=0, concat_axis=0, tiled=True,...  53.6 us
    all_to_all x2, waiting for transfers between devices, exchange(): lax.all_to_all(value, 'expert', split_axis=0, concat_axis=0, tiled=True)  18.3 us
    pallas_call x2, Pallas kernels, weight_in_grads(): pl.pallas_call(weight_in_kernel, grid_spec=pltpu.PrefetchScalarGridSpec(n...  15.6 us
    all_to_all x2, starting transfers between devices, exchange(): lax.all_to_all(value, 'expert', split_axis=0, concat_axis=0, tiled=True)  13 us
    pallas_call x1, Pallas kernels, gate_up(): pl.pallas_call(gate_up_kernel, grid=(wide,), out_shape=(jax.ShapeDtypeStr...  13 us
    pallas_call x1, Pallas kernels, input_grads(): pl.pallas_call(input_grad_kernel, grid=(D // 256,), out_shape=jax.ShapeDt...  12.2 us
    pallas_call x2, Pallas kernels, noisy(): pl.pallas_call(noisy_kernel, grid=(height // 256,), out_shape=jax.ShapeDt...  11.7 us
  transfers between devices with their start and end apart: 9, of which 3 were waited for; matrix products, arithmetic and copies ran while one was open for 1% of the time, Pallas kernels for 36%

profile of v2, /device:TPU:1, one launch (start us, length us, event | category | flops | bytes accessed | tf_op | source)
XLA Modules:
  0.0 287.1 jit_solution(15328117014797740950)
XLA Ops:
  7.8 5.6 %shard_map.119 = (bf16[32,528,128]{2,1,0:T(8,128)(2,1)S(1)}, bf16[32,528,128]{2,1,0:T(8,128)(2,1)}) custom-call(s32[8,128]{1,0:T(8,128)S(1)} %bitcast.42, bf16[8,128]{1,0:T(8,128)(2,1)S(1)} %bitcast.48, bf16[128,2048]{1,0:T(8,128)(2,1)S(1)} %bitcast.37, bf16[128,2048]{1,0:T(8,128)(2,1)S(1)} %bitcast.34, s32[8,128]{1,0:T(8,128)S(1)} %collective-permute-done.after_ref.routes_ref), custom_call_target="tpu_custom_call" | custom-call | flops 1107296 | bytes 9699 | tf_op jit(solution)/shard_map/pallas_call | solution.py:115
  13.5 58.9 %all_to_all.20.after_ref.packed_ref = bf16[32,528,128]{2,1,0:T(8,128)(2,1)} all-to-all(bf16[32,528,128]{2,1,0:T(8,128)(2,1)S(1)} %get-tuple-element.16), channel_id=1, replica_groups=mesh['sample'=4,'expert'=32] {'expert'}, dimensions={0} | all-to-all | bytes 8650752 | tf_op jit(solution)/shard_map/all_to_all | solution.py:468
  72.4 5.0 %all-to-all-start.2 = ((bf16[32,528,128]{2,1,0:T(8,128)(2,1)}), bf16[32,528,128]{2,1,0:T(8,128)(2,1)}, u32[]{:S(2)}, u32[]{:S(2)}) async-start(bf16[32,528,128]{2,1,0:T(8,128)(2,1)} %get-tuple-element.19), calls=%async_computation.2 | async-start | bytes 8650752 | tf_op jit(solution)/shard_map/all_to_all | solution.py:468
  77.5 3.3 %shard_map.122.weight_ref = bf16[768,2048]{1,0:T(8,128)(2,1)S(1)} custom-call(f32[3,8]{1,0:T(4,128)S(1)} %bitcast.45, bf16[768,2048]{1,0:T(8,128)(2,1)} %bitcast.53, bf16[32,528,128]{2,1,0:T(8,128)(2,1)} %all_to_all.20.after_ref.packed_ref), custom_call_target="tpu_custom_call" | custom-call | flops 1572 | bytes 6291 | tf_op jit(solution)/shard_map/pallas_call | solution.py:134
  80.8 8.4 %shard_map.120.gate_w_ref.up_w_ref.weight_ref = bf16[2048,1536]{1,0:T(8,128)(2,1)} custom-call(f32[8,6]{1,0:T(8,128)S(1)} %bitcast.38, bf16[2048,1536]{1,0:T(8,128)(2,1)} %bitcast.51, bf16[32,528,128]{2,1,0:T(8,128)(2,1)S(1)} %bitcast.33), custom_call_target="tpu_custom_call" | custom-call | flops 3145 | bytes 12582 | tf_op jit(solution)/shard_map/pallas_call | solution.py:134
  89.2 13.0 %shard_map.121 = (bf16[1056,2048]{1,0:T(8,128)(2,1)}, f32[1056,768]{1,0:T(8,128)S(1)}, f32[1056,768]{1,0:T(8,128)}, bf16[1056,768]{1,0:T(8,128)(2,1)S(1)}) custom-call(bf16[32,528,128]{2,1,0:T(8,128)(2,1)} %all_to_all.20.after_ref.packed_ref, bf16[2048,1536]{1,0:T(8,128)(2,1)} %shard_map.120.gate_w_ref.up_w_ref.weight_ref, ...), custom_call_target="tpu_custom_call" | custom-call | flops 6643777 | bytes 23052 | tf_op jit(solution)/shard_map/pallas_call | solution.py:185
  103.8 7.8 %shard_map.123.after_ref = bf16[32,528,128]{2,1,0:T(8,128)(2,1)} custom-call(bf16[1056,768]{1,0:T(8,128)(2,1)S(1)} %get-tuple-element.17.hidden_ref, bf16[768,2048]{1,0:T(8,128)(2,1)S(1)} %shard_map.122.weight_ref), custom_call_target="tpu_custom_call" | custom-call | flops 3321888 | bytes 9093 | tf_op jit(solution)/shard_map/pallas_call | solution.py:216
  112.8 18.3 %all-to-all-done.2.packed_ref = bf16[32,528,128]{2,1,0:T(8,128)(2,1)} async-done(((bf16[32,528,128]{2,1,0:T(8,128)(2,1)}), bf16[32,528,128]{2,1,0:T(8,128)(2,1)}, u32[]{:S(2)}, u32[]{:S(2)}) %all-to-all-start.2) | async-done | bytes 4325408 | tf_op jit(solution)/shard_map/all_to_all | solution.py:468
  131.1 8.0 %all-to-all-start.1 = ((bf16[32,528,128]{2,1,0:T(8,128)(2,1)}), bf16[32,528,128]{2,1,0:T(8,128)(2,1)}, u32[]{:S(2)}, u32[]{:S(2)}) async-start(bf16[32,528,128]{2,1,0:T(8,128)(2,1)} %shard_map.123.after_ref), calls=%async_computation.1 | async-start | bytes 8650752 | tf_op jit(solution)/shard_map/all_to_all | solution.py:468
  139.2 10.5 %shard_map.125 = (bf16[1056,2048]{1,0:T(8,128)(2,1)}, bf16[1056,768]{1,0:T(8,128)(2,1)S(1)}, bf16[1056,768]{1,0:T(8,128)(2,1)S(1)}) custom-call(bf16[32,528,128]{2,1,0:T(8,128)(2,1)} %all-to-all-done.2.packed_ref, bf16[768,2048]{1,0:T(8,128)(2,1)} %copy-done, f32[1056,768]{1,0:T(8,128)} %copy-done.8, f32[1056,768]{1,0:T(8,128)} %get-tuple-element.21.up_ref, ...), custom_call_target="tpu_custom_call" | custom-call | flops 3321888 | bytes 21528 | tf_op jit(solution)/shard_map/pallas_call | solution.py:246
  149.7 7.6 %shard_map.127 = bf16[2,512,1536]{2,1,0:T(8,128)(2,1)} custom-call(s32[2]{0:T(128)S(1)} %get-tuple-element.27.share_ref, f32[8,6]{1,0:T(8,128)S(1)} %bitcast.39, bf16[1056,2048]{1,0:T(8,128)(2,1)} %get-tuple-element.24.rows_ref, bf16[1056,768]{1,0:T(8,128)(2,1)S(1)} %get-tuple-element.22.gate_grad_ref, bf16[1056,768]{1,0:T(8,128)(2,1)S(1)} %get-tuple-element.23.up_grad_ref, ...), custom_call_target="tpu_custom_call" | custom-call | flops 3321888 | bytes 11698 | tf_op jit(solution)/shard_map/pallas_call | solution.py:304
  160.0 5.1 %shard_map.129 = bf16[2,768,512]{2,1,0:T(8,128)(2,1)S(1)} custom-call(s32[2]{0:T(128)S(1)} %get-tuple-element.27.share_ref, f32[3,8]{1,0:T(4,128)S(1)} %bitcast.46, bf16[1056,768]{1,0:T(8,128)(2,1)S(1)} %copy-done.2, bf16[1056,2048]{1,0:T(8,128)(2,1)} %get-tuple-element.25.rows_ref), custom_call_target="tpu_custom_call" | custom-call | flops 1660944 | bytes 6930 | tf_op jit(solution)/shard_map/pallas_call | solution.py:333
  165.1 5.2 %shard_map.128.kept_ref = f32[2,768,512]{2,1,0:T(8,128)S(1)} custom-call(s32[2]{0:T(128)S(1)} %get-tuple-element.28.share_ref, f32[3,8]{1,0:T(4,128)S(1)} %bitcast.47, bf16[1056,768]{1,0:T(8,128)(2,1)S(1)} %copy-done.2, bf16[1056,2048]{1,0:T(8,128)(2,1)} %get-tuple-element.25.rows_ref), custom_call_target="tpu_custom_call" | custom-call | flops 1660944 | bytes 6930 | tf_op jit(solution)/shard_map/pallas_call | solution.py:333
  170.3 8.0 %shard_map.126.kept_ref = f32[2,512,1536]{2,1,0:T(8,128)} custom-call(s32[2]{0:T(128)S(1)} %get-tuple-element.28.share_ref, f32[8,6]{1,0:T(8,128)S(1)} %bitcast.40, bf16[1056,2048]{1,0:T(8,128)(2,1)} %get-tuple-element.24.rows_ref, bf16[1056,768]{1,0:T(8,128)(2,1)S(1)} %get-tuple-element.22.gate_grad_ref, ...), custom_call_target="tpu_custom_call" | custom-call | flops 3321888 | bytes 11698 | tf_op jit(solution)/shard_map/pallas_call | solution.py:304
  179.5 3.5 %fusion.1.after_in = bf16[512,1536]{1,0:T(8,128)(2,1)S(1)} fusion(f32[2,512,1536]{2,1,0:T(8,128)} %shard_map.126.kept_ref, bf16[2,512,1536]{2,1,0:T(8,128)(2,1)S(1)} %collective-permute-done.1.got_ref), kind=kLoop, calls=%fused_computation.2 | loop fusion | flops 2359296 | bytes 6291456 | tf_op jit(solution)/shard_map/convert_element_type | solution.py:512
  183.0 12.2 %shard_map.130 = bf16[32,528,128]{2,1,0:T(8,128)(2,1)} custom-call(bf16[1056,768]{1,0:T(8,128)(2,1)S(1)} %get-tuple-element.22.gate_grad_ref, bf16[1056,768]{1,0:T(8,128)(2,1)S(1)} %get-tuple-element.23.up_grad_ref, bf16[2048,1536]{1,0:T(8,128)(2,1)} %shard_map.120.gate_w_ref.up_w_ref.weight_ref, bf16[512,1536]{1,0:T(8,128)(2,1)S(1)} %fusion.1.after_in, ...), custom_call_target="tpu_custom_call" | custom-call | flops 6643777 | bytes 13860 | tf_op jit(solution)/shard_map/pallas_call | solution.py:280
  196.5 6.8 %all-to-all-start.3 = ((bf16[16,1056,128]{2,1,0:T(8,128)(2,1)}), bf16[16,1056,128]{2,1,0:T(8,128)(2,1)}, u32[]{:S(2)}, u32[]{:S(2)}) async-start(bf16[16,1056,128]{2,1,0:T(8,128)(2,1)} %bitcast.50), calls=%async_computation.3 | async-start | bytes 8650752 | tf_op jit(solution)/shard_map/all_to_all | solution.py:474
  203.2 3.4 %collective-permute-start.4 = (bf16[512,1536]{1,0:T(8,128)(2,1)}, bf16[512,1536]{1,0:T(8,128)(2,1)}, u32[]{:S(2)}, u32[]{:S(2)}) collective-permute-start(bf16[512,1536]{1,0:T(8,128)(2,1)} %copy-done.5), channel_id=1, source_target_pairs={{0,64},{1,65},{2,66},{3,67},{4,68},{5,69},{6,70},{7,71},{8,72},{9,... | collective-permute-start | bytes 4718600 | tf_op jit(solution)/shard_map/ppermute | solution.py:485
  208.0 6.1 %shard_map.124 = (bf16[128,2048]{1,0:T(8,128)(2,1)}, f32[8,128]{1,0:T(8,128)}) custom-call(s32[8,128]{1,0:T(8,128)S(1)} %bitcast.43, bf16[8,128]{1,0:T(8,128)(2,1)S(1)} %bitcast.49, bf16[128,2048]{1,0:T(8,128)(2,1)S(1)} %bitcast.35, bf16[32,528,128]{2,1,0:T(8,128)(2,1)} %all-to-all-done.1.packed_ref), custom_call_target="tpu_custom_call" | custom-call | flops 1107296 | bytes 5373 | tf_op jit(solution)/shard_map/pallas_call | solution.py:455
  214.1 53.6 %all-to-all-done.3 = bf16[16,1056,128]{2,1,0:T(8,128)(2,1)} async-done(((bf16[16,1056,128]{2,1,0:T(8,128)(2,1)}), bf16[16,1056,128]{2,1,0:T(8,128)(2,1)}, u32[]{:S(2)}, u32[]{:S(2)}) %all-to-all-start.3) | async-done | bytes 4325408 | tf_op jit(solution)/shard_map/all_to_all | solution.py:474
  268.8 3.4 %shard_map.131.refs_0_.after_ref = bf16[128,2048]{1,0:T(8,128)(2,1)S(1)} custom-call(s32[2]{0:T(128)S(1)} %pad_add_fusion.2.place_ref, s32[8,128]{1,0:T(8,128)S(1)} %collective-permute-done.after_ref.routes_ref, bf16[16,2,528,128]{3,2,1,0:T(8,128)(2,1)} %bitcast.18.packed_ref, bf16[128,2048]{1,0:T(8,128)(2,1)S(1)} %copy-done.12), custom_call_target="tpu_custom_call" | custom-call | flops 276824 | bytes 2686 | tf_op jit(solution)/shard_map/pallas_call | solution.py:394
  273.5 4.6 %shard_map.134 = f32[768,512]{1,0:T(8,128)} custom-call(f32[2,768,512]{2,1,0:T(8,128)S(1)} %shard_map.128.kept_ref, bf16[2,768,512]{2,1,0:T(8,128)(2,1)S(1)} %copy-done.7, bf16[768,512]{1,0:T(8,128)(2,1)} %collective-permute-done.5.far_ref, bf16[128,2048]{1,0:T(8,128)(2,1)S(1)} %shard_map.131.refs_0_.after_ref), custom_call_target="tpu_custom_call" | custom-call | flops 1179 | bytes 4718 | tf_op jit(solution)/shard_map/pallas_call | solution.py:421
  278.1 4.6 %shard_map.133 = f32[512,1536]{1,0:T(8,128)} custom-call(f32[2,512,1536]{2,1,0:T(8,128)} %shard_map.126.kept_ref, bf16[2,512,1536]{2,1,0:T(8,128)(2,1)S(1)} %copy-done.4, bf16[512,1536]{1,0:T(8,128)(2,1)} %collective-permute-done.4.far_ref, bf16[128,2048]{1,0:T(8,128)(2,1)S(1)} %shard_map.131.refs_0_.after_ref), custom_call_target="tpu_custom_call" | custom-call | flops 2359 | bytes 9437 | tf_op jit(solution)/shard_map/pallas_call | solution.py:421
  282.8 3.4 %shard_map.132 = f32[128,2048]{1,0:T(8,128)S(1)} custom-call(s32[2]{0:T(128)S(1)} %pad_add_fusion.place_ref, s32[8,128]{1,0:T(8,128)S(1)} %bitcast.44, bf16[16,2,528,128]{3,2,1,0:T(8,128)(2,1)} %bitcast.18.packed_ref, bf16[128,2048]{1,0:T(8,128)(2,1)S(1)} %shard_map.131.refs_0_.after_ref), custom_call_target="tpu_custom_call" | custom-call | flops 276824 | bytes 2686 | tf_op jit(solution)/shard_map/pallas_call | solution.py:394
  (64 shorter events, 20.2 us)
Async XLA Ops:
  0.6 3.8 %collective-permute-start = (s32[8,128]{1,0:T(8,128)}, s32[8,128]{1,0:T(8,128)S(1)}, u32[]{:S(2)}, u32[]{:S(2)}) collective-permute-start(s32[8,128]{1,0:T(8,128)} %bitcast.41), channel_id=1, source_target_pairs={{0,1},{1,0},{2,3},{3,2},{4,5},{5,4},{6,7},{7,6},{8,9},{9,8},{10,11... | collective-permute-start | bytes 12296 | tf_op jit(solution)/shard_map/ppermute | solution.py:480
  72.4 5.0 %copy-start.18 = (f32[1,1,8,6]{2,1,3,0:T(1,128)S(1)}, f32[1,1,8,6]{2,1,3,0:T(1,128)}, u32[]{:S(2)}) copy-start(f32[1,1,8,6]{2,1,3,0:T(1,128)} %param.14) | copy-start | bytes 580
  72.4 5.1 %copy-start.19 = (f32[1,1,3,8]{3,1,2,0:T(1,128)S(1)}, f32[1,1,3,8]{3,1,2,0:T(1,128)}, u32[]{:S(2)}) copy-start(f32[1,1,3,8]{3,1,2,0:T(1,128)} %param.15) | copy-start | bytes 292
  72.4 8.4 %slice-start = ((s8[4325376]{0:T(1024)(128)(4,1)}), s8[131072]{0:T(1024)(128)(4,1)S(1)}, s32[]{:S(2)}) async-start(s8[4325376]{0:T(1024)(128)(4,1)} %bitcast.32), calls=%async_computation.4 | async-start | bytes 262144
  72.4 58.7 %all-to-all-start.2 = ((bf16[32,528,128]{2,1,0:T(8,128)(2,1)}), bf16[32,528,128]{2,1,0:T(8,128)(2,1)}, u32[]{:S(2)}, u32[]{:S(2)}) async-start(bf16[32,528,128]{2,1,0:T(8,128)(2,1)} %get-tuple-element.19), calls=%async_computation.2 | async-start | bytes 8650752 | tf_op jit(solution)/shard_map/all_to_all | solution.py:468
  77.5 3.3 %slice-start.1 = ((s8[4325376]{0:T(1024)(128)(4,1)}), s8[4194304]{0:T(1024)(128)(4,1)S(1)}, s32[]{:S(2)}) async-start(s8[4325376]{0:T(1024)(128)(4,1)} %bitcast.32), calls=%async_computation.5 | async-start | bytes 8388608
  80.8 23.1 %copy-start = (bf16[768,2048]{1,0:T(8,128)(2,1)}, bf16[768,2048]{1,0:T(8,128)(2,1)S(1)}, u32[]{:S(2)}) copy-start(bf16[768,2048]{1,0:T(8,128)(2,1)S(1)} %shard_map.122.weight_ref) | copy-start | bytes 9437188
  102.2 1.7 copy-start.8
  111.6 1.2 copy-start.1
  131.1 65.3 %all-to-all-start.1 = ((bf16[32,528,128]{2,1,0:T(8,128)(2,1)}), bf16[32,528,128]{2,1,0:T(8,128)(2,1)}, u32[]{:S(2)}, u32[]{:S(2)}) async-start(bf16[32,528,128]{2,1,0:T(8,128)(2,1)} %shard_map.123.after_ref), calls=%async_computation.1 | async-start | bytes 8650752 | tf_op jit(solution)/shard_map/all_to_all | solution.py:468
  149.7 10.3 %copy-start.2 = (bf16[1056,768]{1,0:T(8,128)(2,1)S(1)}, bf16[1056,768]{1,0:T(8,128)(2,1)}, u32[]{:S(2)}) copy-start(bf16[1056,768]{1,0:T(8,128)(2,1)} %copy-done.1) | copy-start | bytes 4866052
  157.3 21.4 %collective-permute-start.1 = (bf16[2,512,1536]{2,1,0:T(8,128)(2,1)}, bf16[2,512,1536]{2,1,0:T(8,128)(2,1)S(1)}, u32[]{:S(2)}, u32[]{:S(2)}) collective-permute-start(bf16[2,512,1536]{2,1,0:T(8,128)(2,1)} %shard_map.127), channel_id=1, source_target_pairs={{0,32},{1,33},{2,34},{3,35},{4,36},{5,37},{6,38},{7,39},{8,40},{9,... | collective-permute-start | bytes 9437192 | tf_op jit(solution)/shard_map/ppermute | solution.py:485
  165.1 13.3 %collective-permute-start.2 = (bf16[2,768,512]{2,1,0:T(8,128)(2,1)S(1)}, bf16[2,768,512]{2,1,0:T(8,128)(2,1)S(1)}, u32[]{:S(2)}, u32[]{:S(2)}) collective-permute-start(bf16[2,768,512]{2,1,0:T(8,128)(2,1)S(1)} %shard_map.129), channel_id=1, source_target_pairs={{0,32},{1,33},{2,34},{3,35},{4,36},{5,37},{6,38},{7,39},{8,40},{9,... | collective-permute-start | bytes 4718600 | tf_op jit(solution)/shard_map/ppermute | solution.py:485
  178.7 4.3 %copy-start.9 = (bf16[768,512]{1,0:T(8,128)(2,1)}, bf16[768,512]{1,0:T(8,128)(2,1)S(1)}, u32[]{:S(2)}) copy-start(bf16[768,512]{1,0:T(8,128)(2,1)S(1)} %fusion.3.after_out) | copy-start | bytes 2359300
  179.5 3.5 %copy-start.3 = (bf16[2,512,1536]{2,1,0:T(8,128)(2,1)}, bf16[2,512,1536]{2,1,0:T(8,128)(2,1)S(1)}, u32[]{:S(2)}) copy-start(bf16[2,512,1536]{2,1,0:T(8,128)(2,1)S(1)} %collective-permute-done.1.got_ref) | copy-start | bytes 9437188
  195.3 1.2 copy-start.5
  196.4 10.5 %copy-start.15 = (s32[1,128,8]{1,2,0:T(8,128)S(1)}, s32[1,128,8]{1,2,0:T(8,128)}, u32[]{:S(2)}) copy-start(s32[1,128,8]{1,2,0:T(8,128)} %param.9) | copy-start | bytes 12292
  196.5 10.5 %copy-start.17 = (bf16[1,128,8]{1,2,0:T(8,128)(2,1)S(1)}, bf16[1,128,8]{1,2,0:T(8,128)(2,1)}, u32[]{:S(2)}) copy-start(bf16[1,128,8]{1,2,0:T(8,128)(2,1)} %param.10) | copy-start | bytes 6148
  196.5 71.2 %all-to-all-start.3 = ((bf16[16,1056,128]{2,1,0:T(8,128)(2,1)}), bf16[16,1056,128]{2,1,0:T(8,128)(2,1)}, u32[]{:S(2)}, u32[]{:S(2)}) async-start(bf16[16,1056,128]{2,1,0:T(8,128)(2,1)} %bitcast.50), calls=%async_computation.3 | async-start | bytes 8650752 | tf_op jit(solution)/shard_map/all_to_all | solution.py:474
  203.2 74.9 %collective-permute-start.4 = (bf16[512,1536]{1,0:T(8,128)(2,1)}, bf16[512,1536]{1,0:T(8,128)(2,1)}, u32[]{:S(2)}, u32[]{:S(2)}) collective-permute-start(bf16[512,1536]{1,0:T(8,128)(2,1)} %copy-done.5), channel_id=1, source_target_pairs={{0,64},{1,65},{2,66},{3,67},{4,68},{5,69},{6,70},{7,71},{8,72},{9,... | collective-permute-start | bytes 4718600 | tf_op jit(solution)/shard_map/ppermute | solution.py:485
  206.6 67.0 %collective-permute-start.5 = (bf16[768,512]{1,0:T(8,128)(2,1)}, bf16[768,512]{1,0:T(8,128)(2,1)}, u32[]{:S(2)}, u32[]{:S(2)}) collective-permute-start(bf16[768,512]{1,0:T(8,128)(2,1)} %copy-done.9), channel_id=1, source_target_pairs={{0,64},{1,65},{2,66},{3,67},{4,68},{5,69},{6,70},{7,71},{8,72},{9,... | collective-permute-start | bytes 2359304 | tf_op jit(solution)/shard_map/ppermute | solution.py:485
  267.7 5.9 %copy-start.7 = (bf16[2,768,512]{2,1,0:T(8,128)(2,1)S(1)}, bf16[2,768,512]{2,1,0:T(8,128)(2,1)}, u32[]{:S(2)}) copy-start(bf16[2,768,512]{2,1,0:T(8,128)(2,1)} %copy-done.6) | copy-start | bytes 4718596
  272.2 14.0 %collective-permute-start.3 = (bf16[128,2048]{1,0:T(8,128)(2,1)S(1)}, bf16[128,2048]{1,0:T(8,128)(2,1)S(1)}, u32[]{:S(2)}, u32[]{:S(2)}) collective-permute-start(bf16[128,2048]{1,0:T(8,128)(2,1)S(1)} %shard_map.131.refs_0_.after_ref), channel_id=1, source_target_pairs={{0,1},{1,0},{2,3},{3,2},{4,5},{5,4},{6,7},{7,6},{8,9},{9,8},{10,11... | collective-permute-start | bytes 1572872 | tf_op jit(solution)/shard_map/ppermute | solution.py:480
  273.5 4.6 %copy-start.4 = (bf16[2,512,1536]{2,1,0:T(8,128)(2,1)S(1)}, bf16[2,512,1536]{2,1,0:T(8,128)(2,1)}, u32[]{:S(2)}) copy-start(bf16[2,512,1536]{2,1,0:T(8,128)(2,1)} %copy-done.3) | copy-start | bytes 9437188
  (7 other events, 6.8 us)

commit v3 on v2

--- a/solution.py
+++ b/solution.py
@@ -24,8 +24,8 @@
 BF16 = jnp.bfloat16
 
 
-def params(**more):
-    return pltpu.CompilerParams(vmem_limit_bytes=VMEM_LIMIT, **more)
+def params(limit=VMEM_LIMIT):
+    return pltpu.CompilerParams(vmem_limit_bytes=limit)
 
 
 def cost(flops, moved):
@@ -48,7 +48,7 @@
     return lax.dot_general(a, b, (((0,), (0,)), ((), ())), preferred_element_type=F32)
 
 
-AFTER = pl.BlockSpec(memory_space=pl.ANY)
+STAYS = pl.BlockSpec(memory_space=pl.ANY)
 
 
 def slot_keys(routes):
@@ -83,8 +83,19 @@
 
 
 def dispatch_kernel(
-    routes_ref, probs_ref, tokens_ref, cotangent_ref, after_ref, x_ref, dy_ref, last_x_ref, last_dy_ref
+    routes_ref, probs_ref, tokens_hbm, cotangent_hbm, x_hbm, dy_hbm,
+    tokens_ref, cotangent_ref, x_ref, dy_ref, last_ref, load_sem, store_sem,
 ):
+    loads = [
+        pltpu.make_async_copy(tokens_hbm, tokens_ref, load_sem.at[0]),
+        pltpu.make_async_copy(cotangent_hbm, cotangent_ref, load_sem.at[1]),
+    ]
+    stores = [
+        pltpu.make_async_copy(x_ref, x_hbm, store_sem.at[0]),
+        pltpu.make_async_copy(dy_ref, dy_hbm, store_sem.at[1]),
+    ]
+    for load in loads:
+        load.start()
     routes = routes_ref[...]
     key = slot_keys(routes)
     weight = expert_weights(routes, probs_ref[...])
@@ -93,7 +104,7 @@
     last_hit = key[:BLOCKS] == float(MAIN)
     order = last_slot_order(False)
 
-    def send(value_ref, pick, last_pick, out_ref, last_ref):
+    def fill(value_ref, pick, last_pick, out_ref):
         for j in range(COLS):
             value = value_ref[:, j * LANES : (j + 1) * LANES]
             rows = dot(pick, value).astype(BF16)
@@ -104,22 +115,39 @@
 
     pick = jnp.where(hit, 1.0, 0.0).astype(BF16)
     last_pick = jnp.where(last_hit, 1.0, 0.0).astype(BF16)
-    send(tokens_ref, pick, last_pick, x_ref, last_x_ref)
+    loads[0].wait()
+    fill(tokens_ref, pick, last_pick, x_ref)
+    stores[0].start()
     pick = jnp.where(hit, dot(spread, weight.astype(BF16)), 0.0).astype(BF16)
     last_pick = jnp.where(last_hit, weight[:BLOCKS], 0.0).astype(BF16)
-    send(cotangent_ref, pick, last_pick, dy_ref, last_dy_ref)
-
-
-def dispatch(routes, probs, tokens, cotangent, after):
+    loads[1].wait()
+    fill(cotangent_ref, pick, last_pick, dy_ref)
+    stores[1].start()
+    for store in stores:
+        store.wait()
+
+
+def dispatch(routes, probs, tokens, cotangent):
     packed = jax.ShapeDtypeStruct((BLOCKS, PACK, LANES), BF16)
+    choice = pl.BlockSpec((TOP, TOK), lambda i: (0, 0))
     return pl.pallas_call(
         dispatch_kernel,
+        grid=(1,),
         out_shape=(packed, packed),
-        in_specs=[pl.BlockSpec(memory_space=pltpu.VMEM)] * 4 + [AFTER],
-        scratch_shapes=[pltpu.VMEM((BLOCKS * COLS, LANES), BF16)] * 2,
-        compiler_params=params(),
+        in_specs=[choice, choice, STAYS, STAYS],
+        out_specs=(STAYS, STAYS),
+        scratch_shapes=[
+            pltpu.VMEM((TOK, D), BF16),
+            pltpu.VMEM((TOK, D), BF16),
+            pltpu.VMEM((BLOCKS, PACK, LANES), BF16),
+            pltpu.VMEM((BLOCKS, PACK, LANES), BF16),
+            pltpu.VMEM((BLOCKS * COLS, LANES), BF16),
+            pltpu.SemaphoreType.DMA((2,)),
+            pltpu.SemaphoreType.DMA((2,)),
+        ],
+        compiler_params=params(60 * 1024 * 1024),
         cost_estimate=cost(4 * ROWS * TOK * D, 4 * (ROWS + TOK) * D),
-    )(routes, probs, tokens, cotangent, after)
+    )(routes, probs, tokens, cotangent)
 
 
 def noisy_kernel(noise_ref, weight_ref, after_ref, out_ref):
@@ -138,7 +166,7 @@
         in_specs=[
             pl.BlockSpec(memory_space=pltpu.SMEM),
             pl.BlockSpec((256, breadth), lambda i: (i, 0)),
-            AFTER,
+            STAYS,
         ],
         out_specs=pl.BlockSpec((256, breadth), lambda i: (i, 0)),
         compiler_params=params(),
@@ -256,7 +284,7 @@
             pl.BlockSpec((256, D), lambda i: (i, 0)),
             part,
             part,
-            AFTER,
+            STAYS,
         ],
         out_specs=(pl.BlockSpec((ROWS, D), lambda i: (0, 0)), part, part),
         compiler_params=params(),
@@ -281,7 +309,7 @@
         input_grad_kernel,
         grid=(D // 256,),
         out_shape=jax.ShapeDtypeStruct((BLOCKS, PACK, LANES), BF16),
-        in_specs=[whole, whole, pl.BlockSpec((256, 2 * FF), lambda i: (i, 0)), AFTER, AFTER],
+        in_specs=[whole, whole, pl.BlockSpec((256, 2 * FF), lambda i: (i, 0)), STAYS, STAYS],
         out_specs=pl.BlockSpec((BLOCKS, PACK, LANES), lambda i: (0, 0, 0)),
         scratch_shapes=[pltpu.VMEM((BLOCKS * COLS, LANES), BF16)],
         compiler_params=params(),
@@ -311,7 +339,7 @@
                 pl.BlockSpec((ROWS, 256), lambda j, i, s: (0, s[j] * 2 + i)),
                 whole,
                 whole,
-                AFTER,
+                STAYS,
             ],
             out_specs=pl.BlockSpec((1, 256, 2 * FF), lambda j, i, s: (j, i, 0)),
         ),
@@ -363,11 +391,11 @@
     return pick.astype(BF16), last_pick[:, :BLOCKS].astype(BF16)
 
 
-def combine_kernel(place_ref, routes_ref, packed_ref, *refs):
+def combine_kernel(plane_ref, routes_ref, packed_ref, *refs):
     out_ref = refs[-1]
     experts = BLOCKS // 2
     key = slot_keys(routes_ref[...]).T + 1.0
-    plane = place_ref[1]
+    plane = plane_ref[0]
 
     def spread(shape, width):
         return jnp.where(iota(shape, 0) == iota(shape, 1) // width * 2 + plane, 1.0, 0.0).astype(BF16)
@@ -389,7 +417,7 @@
         out_ref[:, j * LANES : (j + 1) * LANES] = total.astype(out_ref.dtype)
 
 
-def combine(place, routes, packed, dtype, after):
+def combine(plane, own, routes, packed, dtype, after):
     experts = BLOCKS // 2
     return pl.pallas_call(
         combine_kernel,
@@ -398,39 +426,59 @@
             grid=(1,),
             in_specs=[
                 pl.BlockSpec((TOP, TOK), lambda i, p: (0, 0)),
-                pl.BlockSpec((experts, 1, PACK, LANES), lambda i, p: (0, p[0], 0, 0)),
-                *[AFTER] * len(after),
+                pl.BlockSpec((experts, 1, PACK, LANES), lambda i, p: (0, p[0] if own else 1 - p[0], 0, 0)),
+                *[STAYS] * len(after),
             ],
             out_specs=pl.BlockSpec((TOK, D), lambda i, p: (0, 0)),
         ),
         out_shape=jax.ShapeDtypeStruct((TOK, D), dtype),
         compiler_params=params(),
         cost_estimate=cost(ROWS * TOK * D, (ROWS + 2 * TOK) * D),
-    )(place, routes, packed.reshape(experts, 2, PACK, LANES), *after)
-
-
-def finish_kernel(kept_ref, got_ref, far_ref, after_ref, out_ref):
-    total = kept_ref[0] + got_ref[0].astype(F32) + far_ref[...].astype(F32)
-    out_ref[...] = total * 0.25
-
-
-def finish(kept, got, far, after):
+    )(plane, routes, packed.reshape(experts, 2, PACK, LANES), *after)
+
+
+def finish_kernel(near_ref, far_ref, after_ref, out_ref):
+    out_ref[...] = (near_ref[...] + far_ref[...].astype(F32)) * 0.25
+
+
+def finish(near, far, rows, after):
     height, breadth = far.shape
-    first = pl.BlockSpec((1, 128, breadth), lambda i: (0, i, 0))
-    part = pl.BlockSpec((128, breadth), lambda i: (i, 0))
+    part = pl.BlockSpec((rows, breadth), lambda i: (i, 0))
     return pl.pallas_call(
         finish_kernel,
-        grid=(height // 128,),
+        grid=(height // rows,),
         out_shape=jax.ShapeDtypeStruct((height, breadth), F32),
-        in_specs=[first, first, part, AFTER],
+        in_specs=[part, part, STAYS],
         out_specs=part,
         compiler_params=params(),
-        cost_estimate=cost(3 * height * breadth, 12 * height * breadth),
-    )(kept, got, far, after)
-
-
-def combine_output_kernel(routes_ref, probs_ref, cotangent_ref, packed_ref, out_ref, grad_ref, rows_ref):
+        cost_estimate=cost(2 * height * breadth, 10 * height * breadth),
+    )(near, far, after)
+
+
+def near_kernel(kept_ref, got_ref, after_ref, out_ref):
+    out_ref[...] = kept_ref[0] + got_ref[0].astype(F32)
+
+
+def near_sum(kept, got, rows, after):
+    _, height, breadth = kept.shape
+    first = pl.BlockSpec((1, rows, breadth), lambda i: (0, i, 0))
+    return pl.pallas_call(
+        near_kernel,
+        grid=(height // rows,),
+        out_shape=jax.ShapeDtypeStruct((height, breadth), F32),
+        in_specs=[first, first, STAYS],
+        out_specs=pl.BlockSpec((rows, breadth), lambda i: (i, 0)),
+        compiler_params=params(),
+        cost_estimate=cost(height * breadth, 10 * height * breadth),
+    )(kept, got, after)
+
+
+def combine_output_kernel(
+    routes_ref, probs_ref, cotangent_ref, packed_ref, after_in, after_out,
+    out_ref, grad_ref, same_routes_ref, rows_ref,
+):
     routes = routes_ref[...]
+    same_routes_ref[...] = routes
     unpack_rows(packed_ref, rows_ref)
     key = slot_keys(routes)
     pick, last_pick = combine_tables(key, expert_weights(routes, probs_ref[...]))
@@ -451,17 +499,19 @@
         grad_ref[k : k + 1, :] = value
 
 
-def combine_output(routes, probs, cotangent, packed):
+def combine_output(routes, probs, cotangent, packed, after):
     return pl.pallas_call(
         combine_output_kernel,
         out_shape=(
             jax.ShapeDtypeStruct((TOK, D), BF16),
             jax.ShapeDtypeStruct((TOP, TOK), F32),
+            jax.ShapeDtypeStruct((TOP, TOK), jnp.int32),
         ),
+        in_specs=[pl.BlockSpec(memory_space=pltpu.VMEM)] * 4 + [STAYS, STAYS],
         scratch_shapes=[pltpu.VMEM((ROWS, D), BF16)],
         compiler_params=params(),
         cost_estimate=cost(4 * ROWS * TOK * D, 2 * (ROWS + 2 * TOK) * D),
-    )(routes, probs, cotangent, packed)
+    )(routes, probs, cotangent, packed, *after)
 
 
 def exchange(value):
@@ -492,8 +542,7 @@
     ours = jnp.stack([sample, sample ^ 2]).astype(jnp.int32)
     theirs = ours ^ 1
 
-    far_routes = between_planes(routes)
-    send_x, send_dy = dispatch(routes, probs, tokens[0], cotangent, far_routes)
+    send_x, send_dy = dispatch(routes, probs, tokens[0], cotangent)
     recv_x = exchange(send_x)
     weight_in = noisy(w_gate_up[0], gu_noise, recv_x)
     weight_out = noisy(w_down[0], down_noise, recv_x)
@@ -516,14 +565,17 @@
     send_dx = input_grads(gate_grad, up_grad, weight_in, (half_in, half_out))
     back_dx = exchange_in_plane(send_dx)
 
-    layer_out, prob_grad = combine_output(routes, probs, cotangent, back_y)
-    plane = lax.axis_index("expert") % 2
-    place = jnp.stack([1 - plane, plane]).astype(jnp.int32)
-    there = combine(place, far_routes, back_dx, BF16, (layer_out,))
-    place = jnp.stack([plane, plane]).astype(jnp.int32)
-    here = combine(place, routes, back_dx, F32, (there,))
-    grad_in = finish(kept_in, got_in, far_in, there)
-    grad_out = finish(kept_out, got_out, far_out, there)
+    near_in = near_sum(kept_in, got_in, 256, back_y)
+    near_out = near_sum(kept_out, got_out, 384, back_y)
+    layer_out, prob_grad, same_routes = combine_output(
+        routes, probs, cotangent, back_y, (near_in, near_out)
+    )
+    far_routes = between_planes(same_routes)
+    plane = (lax.axis_index("expert") % 2).astype(jnp.int32)[None]
+    there = combine(plane, False, far_routes, back_dx, BF16, ())
+    here = combine(plane, True, routes, back_dx, F32, (there,))
+    grad_in = finish(near_in, far_in, 256, there)
+    grad_out = finish(near_out, far_out, 384, there)
     input_grad = (here + between_planes(there).astype(F32)).astype(BF16)
     return (layer_out[None], input_grad[None], prob_grad.T[None], grad_in[None], grad_out[None])
 

time: 289 us -> 284 us (0.983)
  local copies, waits for them, and re-layouts: 10.6 us -> 3.12 us
    all_to_all x1, waiting for transfers between devices: 53.6 us -> 5.58 us  [exchange_in_plane(): lax.all_to_all(value, 'expert', split_axis=0, concat_axis=0, tiled=True,...]
    ppermute x2, waiting for transfers between devices: 1.21 us -> 42.5 us  [between_planes(): return lax.ppermute(value, 'expert', [(e, e ^ 1) for e in range(BLOCKS)])]
    unnamed x46 -> x36, local copies, waits for them, and re-layouts: 10.6 us -> 3.12 us
    all_to_all x2, waiting for transfers between devices: 18.3 us -> 23.9 us  [exchange(): lax.all_to_all(value, 'expert', split_axis=0, concat_axis=0, tiled=True)]
    pallas_call x3 -> x5, Pallas kernels: 14.9 us -> 16.9 us  [the longest x1 7.17 us: dispatch(): pl.pallas_call(dispatch_kernel, grid=(1,), out_shape=(packed, packed), in...]
  transfers between devices with their start and end apart: 9 -> 9, of which waited for: 3 -> 5; matrix products, arithmetic and copies ran while one was open for 1% -> 2% of each run, Pallas kernels for 36% -> 36%
where the time goes in v3:
time: 284 us; the launch traced here: 282 us
  Pallas kernels  110 us (39%)
  waiting for transfers between devices  71.9 us (25%)
  blocking collectives  61.1 us (22%)
  starting transfers between devices  28.3 us (10%)
  other arithmetic  6.99 us (2%)
  local copies, waits for them, and re-layouts  3.12 us (1%)
    all_to_all x1, blocking collectives, exchange(): lax.all_to_all(value, 'expert', split_axis=0, concat_axis=0, tiled=True)  61.1 us
    ppermute x2, waiting for transfers between devices, between_planes(): return lax.ppermute(value, 'expert', [(e, e ^ 1) for e in range(BLOCKS)])  42.5 us
    all_to_all x2, waiting for transfers between devices, exchange(): lax.all_to_all(value, 'expert', split_axis=0, concat_axis=0, tiled=True)  23.9 us
    pallas_call x2, Pallas kernels, weight_in_grads(): pl.pallas_call(weight_in_kernel, grid_spec=pltpu.PrefetchScalarGridSpec(n...  16 us
    pallas_call x1, Pallas kernels, gate_up(): pl.pallas_call(gate_up_kernel, grid=(wide,), out_shape=(jax.ShapeDtypeStr...  13 us
    pallas_call x1, Pallas kernels, input_grads(): pl.pallas_call(input_grad_kernel, grid=(D // 256,), out_shape=jax.ShapeDt...  12.2 us
    pallas_call x2, Pallas kernels, noisy(): pl.pallas_call(noisy_kernel, grid=(height // 256,), out_shape=jax.ShapeDt...  11.7 us
    all_to_all x2, starting transfers between devices, exchange(): lax.all_to_all(value, 'expert', split_axis=0, concat_axis=0, tiled=True)  11.5 us
  transfers between devices with their start and end apart: 9, of which 5 were waited for; matrix products, arithmetic and copies ran while one was open for 2% of the time, Pallas kernels for 36%

profile of v3, /device:TPU:1, one launch (start us, length us, event | category | flops | bytes accessed | tf_op | source)
XLA Modules:
  0.0 282.3 jit_solution(10827782374162964447)
XLA Ops:
  0.6 7.2 %shard_map.119 = (bf16[32,528,128]{2,1,0:T(8,128)(2,1)}, bf16[32,528,128]{2,1,0:T(8,128)(2,1)}) custom-call(s32[8,128]{1,0:T(8,128)} %bitcast.38, bf16[8,128]{1,0:T(8,128)(2,1)} %bitcast.44, bf16[128,2048]{1,0:T(8,128)(2,1)} %bitcast.51, bf16[128,2048]{1,0:T(8,128)(2,1)} %bitcast.33), custom_call_target="tpu_custom_call" | custom-call | flops 1107296 | bytes 9699 | tf_op jit(solution)/shard_map/pallas_call | solution.py:133
  7.8 61.1 %all_to_all.20.after_ref.packed_ref = bf16[32,528,128]{2,1,0:T(8,128)(2,1)} all-to-all(bf16[32,528,128]{2,1,0:T(8,128)(2,1)} %get-tuple-element.17), channel_id=1, replica_groups=mesh['sample'=4,'expert'=32] {'expert'}, dimensions={0} | all-to-all | bytes 8650752 | tf_op jit(solution)/shard_map/all_to_all | solution.py:518
  68.9 5.0 %all-to-all-start.2 = ((bf16[32,528,128]{2,1,0:T(8,128)(2,1)}), bf16[32,528,128]{2,1,0:T(8,128)(2,1)}, u32[]{:S(2)}, u32[]{:S(2)}) async-start(bf16[32,528,128]{2,1,0:T(8,128)(2,1)} %get-tuple-element.20), calls=%async_computation.2 | async-start | bytes 8650752 | tf_op jit(solution)/shard_map/all_to_all | solution.py:518
  74.0 3.3 %shard_map.122.weight_ref = bf16[768,2048]{1,0:T(8,128)(2,1)S(1)} custom-call(f32[3,8]{1,0:T(4,128)S(1)} %bitcast.41, bf16[768,2048]{1,0:T(8,128)(2,1)} %bitcast.48, bf16[32,528,128]{2,1,0:T(8,128)(2,1)} %all_to_all.20.after_ref.packed_ref), custom_call_target="tpu_custom_call" | custom-call | flops 1572 | bytes 6291 | tf_op jit(solution)/shard_map/pallas_call | solution.py:162
  77.3 8.4 %shard_map.120.gate_w_ref.up_w_ref.weight_ref = bf16[2048,1536]{1,0:T(8,128)(2,1)} custom-call(f32[8,6]{1,0:T(8,128)S(1)} %bitcast.35, bf16[2048,1536]{1,0:T(8,128)(2,1)} %bitcast.47, bf16[32,528,128]{2,1,0:T(8,128)(2,1)S(1)} %bitcast.32), custom_call_target="tpu_custom_call" | custom-call | flops 3145 | bytes 12582 | tf_op jit(solution)/shard_map/pallas_call | solution.py:162
  85.7 13.0 %shard_map.121 = (bf16[1056,2048]{1,0:T(8,128)(2,1)}, f32[1056,768]{1,0:T(8,128)S(1)}, f32[1056,768]{1,0:T(8,128)}, bf16[1056,768]{1,0:T(8,128)(2,1)S(1)}) custom-call(bf16[32,528,128]{2,1,0:T(8,128)(2,1)} %all_to_all.20.after_ref.packed_ref, bf16[2048,1536]{1,0:T(8,128)(2,1)} %shard_map.120.gate_w_ref.up_w_ref.weight_ref, ...), custom_call_target="tpu_custom_call" | custom-call | flops 6643777 | bytes 23052 | tf_op jit(solution)/shard_map/pallas_call | solution.py:213
  100.5 7.8 %shard_map.123.after_ref = bf16[32,528,128]{2,1,0:T(8,128)(2,1)} custom-call(bf16[1056,768]{1,0:T(8,128)(2,1)S(1)} %get-tuple-element.18.hidden_ref, bf16[768,2048]{1,0:T(8,128)(2,1)S(1)} %shard_map.122.weight_ref), custom_call_target="tpu_custom_call" | custom-call | flops 3321888 | bytes 9093 | tf_op jit(solution)/shard_map/pallas_call | solution.py:244
  109.5 22.4 %all-to-all-done.2.packed_ref = bf16[32,528,128]{2,1,0:T(8,128)(2,1)} async-done(((bf16[32,528,128]{2,1,0:T(8,128)(2,1)}), bf16[32,528,128]{2,1,0:T(8,128)(2,1)}, u32[]{:S(2)}, u32[]{:S(2)}) %all-to-all-start.2) | async-done | bytes 4325408 | tf_op jit(solution)/shard_map/all_to_all | solution.py:518
  131.8 6.5 %all-to-all-start.1 = ((bf16[32,528,128]{2,1,0:T(8,128)(2,1)}), bf16[32,528,128]{2,1,0:T(8,128)(2,1)}, u32[]{:S(2)}, u32[]{:S(2)}) async-start(bf16[32,528,128]{2,1,0:T(8,128)(2,1)} %shard_map.123.after_ref), calls=%async_computation.1 | async-start | bytes 8650752 | tf_op jit(solution)/shard_map/all_to_all | solution.py:518
  138.4 10.5 %shard_map.124 = (bf16[1056,2048]{1,0:T(8,128)(2,1)}, bf16[1056,768]{1,0:T(8,128)(2,1)S(1)}, bf16[1056,768]{1,0:T(8,128)(2,1)S(1)}) custom-call(bf16[32,528,128]{2,1,0:T(8,128)(2,1)} %all-to-all-done.2.packed_ref, bf16[768,2048]{1,0:T(8,128)(2,1)} %copy-done, f32[1056,768]{1,0:T(8,128)} %copy-done.8, f32[1056,768]{1,0:T(8,128)} %get-tuple-element.22.up_ref, ...), custom_call_target="tpu_custom_call" | custom-call | flops 3321888 | bytes 21528 | tf_op jit(solution)/shard_map/pallas_call | solution.py:274
  148.9 7.5 %shard_map.126 = bf16[2,512,1536]{2,1,0:T(8,128)(2,1)} custom-call(s32[2]{0:T(128)S(1)} %get-tuple-element.29.share_ref, f32[8,6]{1,0:T(8,128)S(1)} %bitcast.36, bf16[1056,2048]{1,0:T(8,128)(2,1)} %get-tuple-element.19.rows_ref, bf16[1056,768]{1,0:T(8,128)(2,1)S(1)} %get-tuple-element.23.gate_grad_ref, bf16[1056,768]{1,0:T(8,128)(2,1)S(1)} %get-tuple-element.24.up_grad_ref, ...), custom_call_target="tpu_custom_call" | custom-call | flops 3321888 | bytes 11698 | tf_op jit(solution)/shard_map/pallas_call | solution.py:332
  158.3 5.1 %shard_map.129 = bf16[2,768,512]{2,1,0:T(8,128)(2,1)S(1)} custom-call(s32[2]{0:T(128)S(1)} %get-tuple-element.29.share_ref, f32[3,8]{1,0:T(4,128)S(1)} %bitcast.42, bf16[1056,768]{1,0:T(8,128)(2,1)S(1)} %copy-done.3, bf16[1056,2048]{1,0:T(8,128)(2,1)} %get-tuple-element.25.rows_ref), custom_call_target="tpu_custom_call" | custom-call | flops 1660944 | bytes 6930 | tf_op jit(solution)/shard_map/pallas_call | solution.py:361
  163.5 5.2 %shard_map.128.kept_ref = f32[2,768,512]{2,1,0:T(8,128)S(1)} custom-call(s32[2]{0:T(128)S(1)} %get-tuple-element.30.share_ref, f32[3,8]{1,0:T(4,128)S(1)} %bitcast.43, bf16[1056,768]{1,0:T(8,128)(2,1)S(1)} %copy-done.3, bf16[1056,2048]{1,0:T(8,128)(2,1)} %get-tuple-element.25.rows_ref), custom_call_target="tpu_custom_call" | custom-call | flops 1660944 | bytes 6930 | tf_op jit(solution)/shard_map/pallas_call | solution.py:361
  168.7 8.5 %shard_map.125.kept_ref = f32[2,512,1536]{2,1,0:T(8,128)} custom-call(s32[2]{0:T(128)S(1)} %get-tuple-element.30.share_ref, f32[8,6]{1,0:T(8,128)S(1)} %bitcast.37, bf16[1056,2048]{1,0:T(8,128)(2,1)} %get-tuple-element.19.rows_ref, bf16[1056,768]{1,0:T(8,128)(2,1)S(1)} %get-tuple-element.23.gate_grad_ref, ...), custom_call_target="tpu_custom_call" | custom-call | flops 3321888 | bytes 11698 | tf_op jit(solution)/shard_map/pallas_call | solution.py:332
  178.6 4.6 %fusion.1.after_in = bf16[512,1536]{1,0:T(8,128)(2,1)} fusion(f32[2,512,1536]{2,1,0:T(8,128)} %shard_map.125.kept_ref, bf16[2,512,1536]{2,1,0:T(8,128)(2,1)S(1)} %collective-permute-done.got_ref), kind=kLoop, calls=%fused_computation.2 | loop fusion | flops 2359296 | bytes 6291456 | tf_op jit(solution)/shard_map/convert_element_type | solution.py:561
  183.2 12.2 %shard_map.132 = bf16[32,528,128]{2,1,0:T(8,128)(2,1)} custom-call(bf16[1056,768]{1,0:T(8,128)(2,1)S(1)} %get-tuple-element.23.gate_grad_ref, bf16[1056,768]{1,0:T(8,128)(2,1)S(1)} %get-tuple-element.24.up_grad_ref, bf16[2048,1536]{1,0:T(8,128)(2,1)} %shard_map.120.gate_w_ref.up_w_ref.weight_ref, bf16[512,1536]{1,0:T(8,128)(2,1)} %fusion.1.after_in, ...), custom_call_target="tpu_custom_call" | custom-call | flops 6643777 | bytes 13860 | tf_op jit(solution)/shard_map/pallas_call | solution.py:308
  196.9 5.3 %all-to-all-start.3 = ((bf16[16,1056,128]{2,1,0:T(8,128)(2,1)}), bf16[16,1056,128]{2,1,0:T(8,128)(2,1)}, u32[]{:S(2)}, u32[]{:S(2)}) async-start(bf16[16,1056,128]{2,1,0:T(8,128)(2,1)} %bitcast.46), calls=%async_computation.3 | async-start | bytes 8650752 | tf_op jit(solution)/shard_map/all_to_all | solution.py:524
  202.1 3.7 %collective-permute-start.4 = (bf16[512,1536]{1,0:T(8,128)(2,1)}, bf16[512,1536]{1,0:T(8,128)(2,1)}, u32[]{:S(2)}, u32[]{:S(2)}) collective-permute-start(bf16[512,1536]{1,0:T(8,128)(2,1)} %fusion.1.after_in), channel_id=1, source_target_pairs={{0,64},{1,65},{2,66},{3,67},{4,68},{5,69},{6,70},{7,71},{8,72},{9,... | collective-permute-start | bytes 4718600 | tf_op jit(solution)/shard_map/ppermute | solution.py:535
  207.4 3.1 %shard_map.127.after_in.near_ref = f32[512,1536]{1,0:T(8,128)S(1)} custom-call(f32[2,512,1536]{2,1,0:T(8,128)} %shard_map.125.kept_ref, bf16[2,512,1536]{2,1,0:T(8,128)(2,1)} %copy-done.12, bf16[32,528,128]{2,1,0:T(8,128)(2,1)} %all-to-all-done.1.after_ref.packed_ref), custom_call_target="tpu_custom_call" | custom-call | flops 786 | bytes 7864 | tf_op jit(solution)/shard_map/pallas_call | solution.py:465
  210.5 6.0 %shard_map.131 = (bf16[128,2048]{1,0:T(8,128)(2,1)}, f32[8,128]{1,0:T(8,128)}, s32[8,128]{1,0:T(8,128)S(1)}) custom-call(s32[8,128]{1,0:T(8,128)S(1)} %bitcast.39, bf16[8,128]{1,0:T(8,128)(2,1)S(1)} %bitcast.45, bf16[128,2048]{1,0:T(8,128)(2,1)S(1)} %bitcast.34, bf16[32,528,128]{2,1,0:T(8,128)(2,1)} %all-to-all-done.1.after_ref.packed_ref, ...), custom_call_target="tpu_custom_call" | custom-call | flops 1107296 | bytes 5373 | tf_op jit(solution)/shard_map/pallas_call | solution.py:503
  217.0 39.9 %collective-permute-done.2.routes_ref = s32[8,128]{1,0:T(8,128)S(1)} collective-permute-done((s32[8,128]{1,0:T(8,128)S(1)}, s32[8,128]{1,0:T(8,128)S(1)}, u32[]{:S(2)}, u32[]{:S(2)}) %collective-permute-start.2) | collective-permute-done | bytes 4128 | tf_op jit(solution)/shard_map/ppermute | solution.py:530
  256.9 5.6 %all-to-all-done.3 = bf16[16,1056,128]{2,1,0:T(8,128)(2,1)} async-done(((bf16[16,1056,128]{2,1,0:T(8,128)(2,1)}), bf16[16,1056,128]{2,1,0:T(8,128)(2,1)}, u32[]{:S(2)}, u32[]{:S(2)}) %all-to-all-start.3) | async-done | bytes 4325408 | tf_op jit(solution)/shard_map/all_to_all | solution.py:524
  262.5 3.0 %shard_map.133.refs_0_.after_ref = bf16[128,2048]{1,0:T(8,128)(2,1)S(1)} custom-call(s32[1]{0:T(128)} %bitcast.14.plane_ref, s32[8,128]{1,0:T(8,128)S(1)} %collective-permute-done.2.routes_ref, bf16[16,2,528,128]{3,2,1,0:T(8,128)(2,1)} %bitcast.18.packed_ref), custom_call_target="tpu_custom_call" | custom-call | flops 276824 | bytes 2686 | tf_op jit(solution)/shard_map/pallas_call | solution.py:422
  265.4 5.4 %collective-permute-start.3 = (bf16[128,2048]{1,0:T(8,128)(2,1)S(1)}, bf16[128,2048]{1,0:T(8,128)(2,1)S(1)}, u32[]{:S(2)}, u32[]{:S(2)}) collective-permute-start(bf16[128,2048]{1,0:T(8,128)(2,1)S(1)} %shard_map.133.refs_0_.after_ref), channel_id=1, source_target_pairs={{0,1},{1,0},{2,3},{3,2},{4,5},{5,4},{6,7},{7,6},{8,9},{9,8},{10,11... | collective-permute-start | bytes 1572872 | tf_op jit(solution)/shard_map/ppermute | solution.py:530
  (54 shorter events, 21.5 us)
Async XLA Ops:
  68.9 5.0 %copy-start.13 = (f32[1,1,8,6]{2,1,3,0:T(1,128)S(1)}, f32[1,1,8,6]{2,1,3,0:T(1,128)}, u32[]{:S(2)}) copy-start(f32[1,1,8,6]{2,1,3,0:T(1,128)} %param.14) | copy-start | bytes 580
  68.9 5.1 %copy-start.14 = (f32[1,1,3,8]{3,1,2,0:T(1,128)S(1)}, f32[1,1,3,8]{3,1,2,0:T(1,128)}, u32[]{:S(2)}) copy-start(f32[1,1,3,8]{3,1,2,0:T(1,128)} %param.15) | copy-start | bytes 292
  68.9 8.4 %slice-start = ((s8[4325376]{0:T(1024)(128)(4,1)}), s8[131072]{0:T(1024)(128)(4,1)S(1)}, s32[]{:S(2)}) async-start(s8[4325376]{0:T(1024)(128)(4,1)} %bitcast.31), calls=%async_computation.4 | async-start | bytes 262144
  68.9 62.9 %all-to-all-start.2 = ((bf16[32,528,128]{2,1,0:T(8,128)(2,1)}), bf16[32,528,128]{2,1,0:T(8,128)(2,1)}, u32[]{:S(2)}, u32[]{:S(2)}) async-start(bf16[32,528,128]{2,1,0:T(8,128)(2,1)} %get-tuple-element.20), calls=%async_computation.2 | async-start | bytes 8650752 | tf_op jit(solution)/shard_map/all_to_all | solution.py:518
  74.0 3.3 %slice-start.1 = ((s8[4325376]{0:T(1024)(128)(4,1)}), s8[4194304]{0:T(1024)(128)(4,1)S(1)}, s32[]{:S(2)}) async-start(s8[4325376]{0:T(1024)(128)(4,1)} %bitcast.31), calls=%async_computation.5 | async-start | bytes 8388608
  77.3 23.3 %copy-start = (bf16[768,2048]{1,0:T(8,128)(2,1)}, bf16[768,2048]{1,0:T(8,128)(2,1)S(1)}, u32[]{:S(2)}) copy-start(bf16[768,2048]{1,0:T(8,128)(2,1)S(1)} %shard_map.122.weight_ref) | copy-start | bytes 9437188
  131.8 65.0 %all-to-all-start.1 = ((bf16[32,528,128]{2,1,0:T(8,128)(2,1)}), bf16[32,528,128]{2,1,0:T(8,128)(2,1)}, u32[]{:S(2)}, u32[]{:S(2)}) async-start(bf16[32,528,128]{2,1,0:T(8,128)(2,1)} %shard_map.123.after_ref), calls=%async_computation.1 | async-start | bytes 8650752 | tf_op jit(solution)/shard_map/all_to_all | solution.py:518
  148.9 9.4 %copy-start.3 = (bf16[1056,768]{1,0:T(8,128)(2,1)S(1)}, bf16[1056,768]{1,0:T(8,128)(2,1)}, u32[]{:S(2)}) copy-start(bf16[1056,768]{1,0:T(8,128)(2,1)} %copy-done.2) | copy-start | bytes 4866052
  156.4 22.1 %collective-permute-start = (bf16[2,512,1536]{2,1,0:T(8,128)(2,1)}, bf16[2,512,1536]{2,1,0:T(8,128)(2,1)S(1)}, u32[]{:S(2)}, u32[]{:S(2)}) collective-permute-start(bf16[2,512,1536]{2,1,0:T(8,128)(2,1)} %shard_map.126), channel_id=1, source_target_pairs={{0,32},{1,33},{2,34},{3,35},{4,36},{5,37},{6,38},{7,39},{8,40},{9,... | collective-permute-start | bytes 9437192 | tf_op jit(solution)/shard_map/ppermute | solution.py:535
  163.4 13.8 %collective-permute-start.1 = (bf16[2,768,512]{2,1,0:T(8,128)(2,1)S(1)}, bf16[2,768,512]{2,1,0:T(8,128)(2,1)S(1)}, u32[]{:S(2)}, u32[]{:S(2)}) collective-permute-start(bf16[2,768,512]{2,1,0:T(8,128)(2,1)S(1)} %shard_map.129), channel_id=1, source_target_pairs={{0,32},{1,33},{2,34},{3,35},{4,36},{5,37},{6,38},{7,39},{8,40},{9,... | collective-permute-start | bytes 4718600 | tf_op jit(solution)/shard_map/ppermute | solution.py:535
  168.6 8.5 %copy-start.1 = (f32[2,768,512]{2,1,0:T(8,128)}, f32[2,768,512]{2,1,0:T(8,128)S(1)}, u32[]{:S(2)}) copy-start(f32[2,768,512]{2,1,0:T(8,128)S(1)} %shard_map.128.kept_ref) | copy-start | bytes 9437188
  177.2 6.0 %copy-start.6 = (bf16[2,768,512]{2,1,0:T(8,128)(2,1)}, bf16[2,768,512]{2,1,0:T(8,128)(2,1)S(1)}, u32[]{:S(2)}) copy-start(bf16[2,768,512]{2,1,0:T(8,128)(2,1)S(1)} %collective-permute-done.1.got_ref) | copy-start | bytes 4718596
  178.6 4.6 %copy-start.12 = (bf16[2,512,1536]{2,1,0:T(8,128)(2,1)}, bf16[2,512,1536]{2,1,0:T(8,128)(2,1)S(1)}, u32[]{:S(2)}) copy-start(bf16[2,512,1536]{2,1,0:T(8,128)(2,1)S(1)} %collective-permute-done.got_ref) | copy-start | bytes 9437188
  196.9 9.1 %copy-start.7 = (bf16[2,768,512]{2,1,0:T(8,128)(2,1)S(1)}, bf16[2,768,512]{2,1,0:T(8,128)(2,1)}, u32[]{:S(2)}) copy-start(bf16[2,768,512]{2,1,0:T(8,128)(2,1)} %copy-done.6) | copy-start | bytes 4718596
  196.9 65.6 %all-to-all-start.3 = ((bf16[16,1056,128]{2,1,0:T(8,128)(2,1)}), bf16[16,1056,128]{2,1,0:T(8,128)(2,1)}, u32[]{:S(2)}, u32[]{:S(2)}) async-start(bf16[16,1056,128]{2,1,0:T(8,128)(2,1)} %bitcast.46), calls=%async_computation.3 | async-start | bytes 8650752 | tf_op jit(solution)/shard_map/all_to_all | solution.py:524
  202.1 70.9 %collective-permute-start.4 = (bf16[512,1536]{1,0:T(8,128)(2,1)}, bf16[512,1536]{1,0:T(8,128)(2,1)}, u32[]{:S(2)}, u32[]{:S(2)}) collective-permute-start(bf16[512,1536]{1,0:T(8,128)(2,1)} %fusion.1.after_in), channel_id=1, source_target_pairs={{0,64},{1,65},{2,66},{3,67},{4,68},{5,69},{6,70},{7,71},{8,72},{9,... | collective-permute-start | bytes 4718600 | tf_op jit(solution)/shard_map/ppermute | solution.py:535
  205.8 65.0 %collective-permute-start.5 = (bf16[768,512]{1,0:T(8,128)(2,1)}, bf16[768,512]{1,0:T(8,128)(2,1)}, u32[]{:S(2)}, u32[]{:S(2)}) collective-permute-start(bf16[768,512]{1,0:T(8,128)(2,1)} %fusion.3.after_out), channel_id=1, source_target_pairs={{0,64},{1,65},{2,66},{3,67},{4,68},{5,69},{6,70},{7,71},{8,72},{9,... | collective-permute-start | bytes 2359304 | tf_op jit(solution)/shard_map/ppermute | solution.py:535
  207.4 3.1 %copy-start.4 = (f32[768,512]{1,0:T(8,128)}, f32[768,512]{1,0:T(8,128)S(1)}, u32[]{:S(2)}) copy-start(f32[768,512]{1,0:T(8,128)S(1)} %shard_map.130.after_out.near_ref) | copy-start | bytes 4718596
  207.4 3.1 %copy-start.9 = (bf16[1,128,2048]{2,1,0:T(8,128)(2,1)S(1)}, bf16[1,128,2048]{2,1,0:T(8,128)(2,1)}, u32[]{:S(2)}) copy-start(bf16[1,128,2048]{2,1,0:T(8,128)(2,1)} %param.11) | copy-start | bytes 1572868
  207.4 3.1 %copy-start.10 = (s32[1,128,8]{1,2,0:T(8,128)S(1)}, s32[1,128,8]{1,2,0:T(8,128)}, u32[]{:S(2)}) copy-start(s32[1,128,8]{1,2,0:T(8,128)} %param.9) | copy-start | bytes 12292
  207.4 3.1 %copy-start.11 = (bf16[1,128,8]{1,2,0:T(8,128)(2,1)S(1)}, bf16[1,128,8]{1,2,0:T(8,128)(2,1)}, u32[]{:S(2)}) copy-start(bf16[1,128,8]{1,2,0:T(8,128)(2,1)} %param.10) | copy-start | bytes 6148
  216.6 40.3 %collective-permute-start.2 = (s32[8,128]{1,0:T(8,128)S(1)}, s32[8,128]{1,0:T(8,128)S(1)}, u32[]{:S(2)}, u32[]{:S(2)}) collective-permute-start(s32[8,128]{1,0:T(8,128)S(1)} %get-tuple-element.27), channel_id=1, source_target_pairs={{0,1},{1,0},{2,3},{3,2},{4,5},{5,4},{6,7},{7,6},{8,9},{9,8},{10,11... | collective-permute-start | bytes 12296 | tf_op jit(solution)/shard_map/ppermute | solution.py:530
  262.5 8.3 %copy-start.5 = (f32[768,512]{1,0:T(8,128)S(1)}, f32[768,512]{1,0:T(8,128)}, u32[]{:S(2)}) copy-start(f32[768,512]{1,0:T(8,128)} %copy-done.4) | copy-start | bytes 4718596
  265.4 16.0 %collective-permute-start.3 = (bf16[128,2048]{1,0:T(8,128)(2,1)S(1)}, bf16[128,2048]{1,0:T(8,128)(2,1)S(1)}, u32[]{:S(2)}, u32[]{:S(2)}) collective-permute-start(bf16[128,2048]{1,0:T(8,128)(2,1)S(1)} %shard_map.133.refs_0_.after_ref), channel_id=1, source_target_pairs={{0,1},{1,0},{2,3},{3,2},{4,5},{5,4},{6,7},{7,6},{8,9},{9,8},{10,11... | collective-permute-start | bytes 1572872 | tf_op jit(solution)/shard_map/ppermute | solution.py:530
  (2 other events, 3.0 us)

commit v4 on v3

--- a/solution.py
+++ b/solution.py
@@ -51,6 +51,13 @@
 STAYS = pl.BlockSpec(memory_space=pl.ANY)
 
 
+def place(expert):
+    return ((((expert >> 3) + (expert >> 1)) & 3) << 3) | (expert & 7)
+
+
+ORDER = sorted(range(BLOCKS), key=place)
+
+
 def slot_keys(routes):
     expert = iota((LANES, TOK), 0)
     chosen = jnp.zeros((LANES, TOK), F32)
@@ -90,13 +97,15 @@
         pltpu.make_async_copy(tokens_hbm, tokens_ref, load_sem.at[0]),
         pltpu.make_async_copy(cotangent_hbm, cotangent_ref, load_sem.at[1]),
     ]
-    stores = [
-        pltpu.make_async_copy(x_ref, x_hbm, store_sem.at[0]),
-        pltpu.make_async_copy(dy_ref, dy_hbm, store_sem.at[1]),
-    ]
+    half = MAIN * COLS // 2
+    stores = []
+    for made_ref, hbm in ((x_ref, x_hbm), (dy_ref, dy_hbm)):
+        for cut in (pl.ds(0, half), pl.ds(half, PACK - half)):
+            sem = store_sem.at[len(stores)]
+            stores.append(pltpu.make_async_copy(made_ref.at[:, cut, :], hbm.at[:, cut, :], sem))
     for load in loads:
         load.start()
-    routes = routes_ref[...]
+    routes = place(routes_ref[...])
     key = slot_keys(routes)
     weight = expert_weights(routes, probs_ref[...])
     spread = jnp.where(iota((BIG, LANES), 0) // MAIN == iota((BIG, LANES), 1), 1.0, 0.0).astype(BF16)
@@ -104,25 +113,31 @@
     last_hit = key[:BLOCKS] == float(MAIN)
     order = last_slot_order(False)
 
-    def fill(value_ref, pick, last_pick, out_ref):
-        for j in range(COLS):
-            value = value_ref[:, j * LANES : (j + 1) * LANES]
-            rows = dot(pick, value).astype(BF16)
-            out_ref[:, j * MAIN : (j + 1) * MAIN, :] = rows.reshape(BLOCKS, MAIN, LANES)
-            last_ref[j * BLOCKS : (j + 1) * BLOCKS, :] = dot(last_pick, value).astype(BF16)
+    def fill(value_ref, pick, last_pick, out_ref, first, second):
+        for j in range(0, COLS, 2):
+            value = value_ref[:, j * LANES : (j + 2) * LANES]
+            last = dot(last_pick, value).astype(BF16)
+            for i in range(2):
+                last_ref[(j + i) * BLOCKS : (j + i + 1) * BLOCKS, :] = last[:, i * LANES : (i + 1) * LANES]
         tiles = dot(order, last_ref[...]).astype(BF16)
         out_ref[:, MAIN * COLS :, :] = tiles.reshape(BLOCKS, COLS, LANES)
+        for j in range(0, COLS, 2):
+            rows = dot(pick, value_ref[:, j * LANES : (j + 2) * LANES]).astype(BF16)
+            for i in range(2):
+                cut = rows[:, i * LANES : (i + 1) * LANES].reshape(BLOCKS, MAIN, LANES)
+                out_ref[:, (j + i) * MAIN : (j + i + 1) * MAIN, :] = cut
+            if j + 2 == COLS // 2:
+                first.start()
+        second.start()
 
     pick = jnp.where(hit, 1.0, 0.0).astype(BF16)
     last_pick = jnp.where(last_hit, 1.0, 0.0).astype(BF16)
     loads[0].wait()
-    fill(tokens_ref, pick, last_pick, x_ref)
-    stores[0].start()
+    fill(tokens_ref, pick, last_pick, x_ref, stores[0], stores[1])
     pick = jnp.where(hit, dot(spread, weight.astype(BF16)), 0.0).astype(BF16)
     last_pick = jnp.where(last_hit, weight[:BLOCKS], 0.0).astype(BF16)
     loads[1].wait()
-    fill(cotangent_ref, pick, last_pick, dy_ref)
-    stores[1].start()
+    fill(cotangent_ref, pick, last_pick, dy_ref, stores[2], stores[3])
     for store in stores:
         store.wait()
 
@@ -143,7 +158,7 @@
             pltpu.VMEM((BLOCKS, PACK, LANES), BF16),
             pltpu.VMEM((BLOCKS * COLS, LANES), BF16),
             pltpu.SemaphoreType.DMA((2,)),
-            pltpu.SemaphoreType.DMA((2,)),
+            pltpu.SemaphoreType.DMA((4,)),
         ],
         compiler_params=params(60 * 1024 * 1024),
         cost_estimate=cost(4 * ROWS * TOK * D, 4 * (ROWS + TOK) * D),
@@ -394,7 +409,7 @@
 def combine_kernel(plane_ref, routes_ref, packed_ref, *refs):
     out_ref = refs[-1]
     experts = BLOCKS // 2
-    key = slot_keys(routes_ref[...]).T + 1.0
+    key = slot_keys(place(routes_ref[...])).T + 1.0
     plane = plane_ref[0]
 
     def spread(shape, width):
@@ -411,10 +426,15 @@
     order = ((tile // COLS) == (row % experts)) & ((tile % COLS) == (row // experts))
     last = packed_ref[:, 0, MAIN * COLS :, :].reshape(count, LANES)
     last = dot(jnp.where(order, 1.0, 0.0).astype(BF16), last).astype(BF16)
-    for j in range(COLS):
-        rows = packed_ref[:, 0, j * MAIN : (j + 1) * MAIN, :].reshape(experts * MAIN, LANES)
-        total = dot(pick, rows) + dot(last_pick, last[j * experts : (j + 1) * experts])
-        out_ref[:, j * LANES : (j + 1) * LANES] = total.astype(out_ref.dtype)
+    for j in range(0, COLS, 2):
+        rows, ends = [], []
+        for at in (j, j + 1):
+            part = packed_ref[:, 0, at * MAIN : (at + 1) * MAIN, :]
+            rows.append(part.reshape(experts * MAIN, LANES))
+            ends.append(last[at * experts : (at + 1) * experts])
+        total = dot(pick, jnp.concatenate(rows, axis=1))
+        total += dot(last_pick, jnp.concatenate(ends, axis=1))
+        out_ref[:, j * LANES : (j + 2) * LANES] = total.astype(out_ref.dtype)
 
 
 def combine(plane, own, routes, packed, dtype, after):
@@ -477,8 +497,8 @@
     routes_ref, probs_ref, cotangent_ref, packed_ref, after_in, after_out,
     out_ref, grad_ref, same_routes_ref, rows_ref,
 ):
-    routes = routes_ref[...]
-    same_routes_ref[...] = routes
+    routes = place(routes_ref[...])
+    same_routes_ref[...] = routes_ref[...]
     unpack_rows(packed_ref, rows_ref)
     key = slot_keys(routes)
     pick, last_pick = combine_tables(key, expert_weights(routes, probs_ref[...]))
@@ -515,11 +535,13 @@
 
 
 def exchange(value):
-    return lax.all_to_all(value, "expert", split_axis=0, concat_axis=0, tiled=True)
+    return lax.all_to_all(
+        value, "expert", split_axis=0, concat_axis=0, tiled=True, axis_index_groups=[ORDER]
+    )
 
 
 def exchange_in_plane(value):
-    planes = [list(range(z, BLOCKS, 2)) for z in range(2)]
+    planes = [ORDER[z::2] for z in range(2)]
     value = value.reshape(BLOCKS // 2, 2 * PACK, LANES)
     return lax.all_to_all(
         value, "expert", split_axis=0, concat_axis=0, tiled=True, axis_index_groups=planes

time: 284 us -> 280 us (0.986)
  waiting for transfers between devices: 71.9 us -> 63.6 us
  starting transfers between devices: 28.3 us -> 32 us
    all_to_all x1, waiting for transfers between devices: 5.58 us -> 0.01 us  [exchange_in_plane(): lax.all_to_all(value, 'expert', split_axis=0, concat_axis=0, tiled=True,...]
  transfers between devices with their start and end apart: 9 -> 9, of which waited for: 5 -> 3; matrix products, arithmetic and copies ran while one was open for 2% -> 2% of each run, Pallas kernels for 36% -> 37%
where the time goes in v4:
time: 280 us; the launch traced here: 276 us
  Pallas kernels  109 us (39%)
  waiting for transfers between devices  63.6 us (23%)
  blocking collectives  60.5 us (22%)
  starting transfers between devices  32 us (11%)
  other arithmetic  6.99 us (2%)
  local copies, waits for them, and re-layouts  3.12 us (1%)
    all_to_all x1, blocking collectives, exchange(): lax.all_to_all(value, 'expert', split_axis=0, concat_axis=0, tiled=True,...  60.5 us
    ppermute x2, waiting for transfers between devices, between_planes(): return lax.ppermute(value, 'expert', [(e, e ^ 1) for e in range(BLOCKS)])  42.4 us
    all_to_all x2, waiting for transfers between devices, exchange(): lax.all_to_all(value, 'expert', split_axis=0, concat_axis=0, tiled=True,...  21.2 us
    pallas_call x2, Pallas kernels, weight_in_grads(): pl.pallas_call(weight_in_kernel, grid_spec=pltpu.PrefetchScalarGridSpec(n...  16.1 us
    all_to_all x2, starting transfers between devices, exchange(): lax.all_to_all(value, 'expert', split_axis=0, concat_axis=0, tiled=True,...  13.7 us
    pallas_call x1, Pallas kernels, gate_up(): pl.pallas_call(gate_up_kernel, grid=(wide,), out_shape=(jax.ShapeDtypeStr...  13 us
    pallas_call x1, Pallas kernels, input_grads(): pl.pallas_call(input_grad_kernel, grid=(D // 256,), out_shape=jax.ShapeDt...  12.2 us
    pallas_call x2, Pallas kernels, noisy(): pl.pallas_call(noisy_kernel, grid=(height // 256,), out_shape=jax.ShapeDt...  11.7 us
  transfers between devices with their start and end apart: 9, of which 3 were waited for; matrix products, arithmetic and copies ran while one was open for 2% of the time, Pallas kernels for 37%

profile of v4, /device:TPU:1, one launch (start us, length us, event | category | flops | bytes accessed | tf_op | source)
XLA Modules:
  0.0 276.3 jit_solution(6723644102970093775)
XLA Ops:
  0.6 6.8 %shard_map.119 = (bf16[32,528,128]{2,1,0:T(8,128)(2,1)}, bf16[32,528,128]{2,1,0:T(8,128)(2,1)}) custom-call(s32[8,128]{1,0:T(8,128)} %bitcast.38, bf16[8,128]{1,0:T(8,128)(2,1)} %bitcast.44, bf16[128,2048]{1,0:T(8,128)(2,1)} %bitcast.51, bf16[128,2048]{1,0:T(8,128)(2,1)} %bitcast.33), custom_call_target="tpu_custom_call" | custom-call | flops 1107296 | bytes 9699 | tf_op jit(solution)/shard_map/pallas_call | solution.py:148
  7.4 60.5 %all_to_all.20.after_ref.packed_ref = bf16[32,528,128]{2,1,0:T(8,128)(2,1)} all-to-all(bf16[32,528,128]{2,1,0:T(8,128)(2,1)} %get-tuple-element.17), channel_id=1, replica_groups={{0,1,26,27,20,21,14,15,8,9,2,3,28,29,22,23,16,17,10,11,4,5,30,31,24,25,..., dimensions={0} | all-to-all | bytes 8650752 | tf_op jit(solution)/shard_map/all_to_all | solution.py:538
  68.0 5.6 %all-to-all-start.2 = ((bf16[32,528,128]{2,1,0:T(8,128)(2,1)}), bf16[32,528,128]{2,1,0:T(8,128)(2,1)}, u32[]{:S(2)}, u32[]{:S(2)}) async-start(bf16[32,528,128]{2,1,0:T(8,128)(2,1)} %get-tuple-element.20), calls=%async_computation.2 | async-start | bytes 8650752 | tf_op jit(solution)/shard_map/all_to_all | solution.py:538
  73.7 3.3 %shard_map.122.weight_ref = bf16[768,2048]{1,0:T(8,128)(2,1)S(1)} custom-call(f32[3,8]{1,0:T(4,128)S(1)} %bitcast.41, bf16[768,2048]{1,0:T(8,128)(2,1)} %bitcast.48, bf16[32,528,128]{2,1,0:T(8,128)(2,1)} %all_to_all.20.after_ref.packed_ref), custom_call_target="tpu_custom_call" | custom-call | flops 1572 | bytes 6291 | tf_op jit(solution)/shard_map/pallas_call | solution.py:177
  77.0 8.4 %shard_map.120.gate_w_ref.up_w_ref.weight_ref = bf16[2048,1536]{1,0:T(8,128)(2,1)} custom-call(f32[8,6]{1,0:T(8,128)S(1)} %bitcast.35, bf16[2048,1536]{1,0:T(8,128)(2,1)} %bitcast.47, bf16[32,528,128]{2,1,0:T(8,128)(2,1)S(1)} %bitcast.32), custom_call_target="tpu_custom_call" | custom-call | flops 3145 | bytes 12582 | tf_op jit(solution)/shard_map/pallas_call | solution.py:177
  85.4 13.0 %shard_map.121 = (bf16[1056,2048]{1,0:T(8,128)(2,1)}, f32[1056,768]{1,0:T(8,128)S(1)}, f32[1056,768]{1,0:T(8,128)}, bf16[1056,768]{1,0:T(8,128)(2,1)S(1)}) custom-call(bf16[32,528,128]{2,1,0:T(8,128)(2,1)} %all_to_all.20.after_ref.packed_ref, bf16[2048,1536]{1,0:T(8,128)(2,1)} %shard_map.120.gate_w_ref.up_w_ref.weight_ref, ...), custom_call_target="tpu_custom_call" | custom-call | flops 6643777 | bytes 23052 | tf_op jit(solution)/shard_map/pallas_call | solution.py:228
  100.2 7.8 %shard_map.123.after_ref = bf16[32,528,128]{2,1,0:T(8,128)(2,1)} custom-call(bf16[1056,768]{1,0:T(8,128)(2,1)S(1)} %get-tuple-element.18.hidden_ref, bf16[768,2048]{1,0:T(8,128)(2,1)S(1)} %shard_map.122.weight_ref), custom_call_target="tpu_custom_call" | custom-call | flops 3321888 | bytes 9093 | tf_op jit(solution)/shard_map/pallas_call | solution.py:259
  109.1 21.2 %all-to-all-done.2.packed_ref = bf16[32,528,128]{2,1,0:T(8,128)(2,1)} async-done(((bf16[32,528,128]{2,1,0:T(8,128)(2,1)}), bf16[32,528,128]{2,1,0:T(8,128)(2,1)}, u32[]{:S(2)}, u32[]{:S(2)}) %all-to-all-start.2) | async-done | bytes 4325408 | tf_op jit(solution)/shard_map/all_to_all | solution.py:538
  130.3 8.0 %all-to-all-start.1 = ((bf16[32,528,128]{2,1,0:T(8,128)(2,1)}), bf16[32,528,128]{2,1,0:T(8,128)(2,1)}, u32[]{:S(2)}, u32[]{:S(2)}) async-start(bf16[32,528,128]{2,1,0:T(8,128)(2,1)} %shard_map.123.after_ref), calls=%async_computation.1 | async-start | bytes 8650752 | tf_op jit(solution)/shard_map/all_to_all | solution.py:538
  138.5 10.5 %shard_map.124 = (bf16[1056,2048]{1,0:T(8,128)(2,1)}, bf16[1056,768]{1,0:T(8,128)(2,1)S(1)}, bf16[1056,768]{1,0:T(8,128)(2,1)S(1)}) custom-call(bf16[32,528,128]{2,1,0:T(8,128)(2,1)} %all-to-all-done.2.packed_ref, bf16[768,2048]{1,0:T(8,128)(2,1)} %copy-done, f32[1056,768]{1,0:T(8,128)} %copy-done.8, f32[1056,768]{1,0:T(8,128)} %get-tuple-element.22.up_ref, ...), custom_call_target="tpu_custom_call" | custom-call | flops 3321888 | bytes 21528 | tf_op jit(solution)/shard_map/pallas_call | solution.py:289
  148.9 7.6 %shard_map.126 = bf16[2,512,1536]{2,1,0:T(8,128)(2,1)} custom-call(s32[2]{0:T(128)S(1)} %get-tuple-element.29.share_ref, f32[8,6]{1,0:T(8,128)S(1)} %bitcast.36, bf16[1056,2048]{1,0:T(8,128)(2,1)} %get-tuple-element.19.rows_ref, bf16[1056,768]{1,0:T(8,128)(2,1)S(1)} %get-tuple-element.23.gate_grad_ref, bf16[1056,768]{1,0:T(8,128)(2,1)S(1)} %get-tuple-element.24.up_grad_ref, ...), custom_call_target="tpu_custom_call" | custom-call | flops 3321888 | bytes 11698 | tf_op jit(solution)/shard_map/pallas_call | solution.py:347
  159.4 5.1 %shard_map.129 = bf16[2,768,512]{2,1,0:T(8,128)(2,1)S(1)} custom-call(s32[2]{0:T(128)S(1)} %get-tuple-element.29.share_ref, f32[3,8]{1,0:T(4,128)S(1)} %bitcast.42, bf16[1056,768]{1,0:T(8,128)(2,1)S(1)} %copy-done.3, bf16[1056,2048]{1,0:T(8,128)(2,1)} %get-tuple-element.25.rows_ref), custom_call_target="tpu_custom_call" | custom-call | flops 1660944 | bytes 6930 | tf_op jit(solution)/shard_map/pallas_call | solution.py:376
  164.5 5.2 %shard_map.128.kept_ref = f32[2,768,512]{2,1,0:T(8,128)S(1)} custom-call(s32[2]{0:T(128)S(1)} %get-tuple-element.30.share_ref, f32[3,8]{1,0:T(4,128)S(1)} %bitcast.43, bf16[1056,768]{1,0:T(8,128)(2,1)S(1)} %copy-done.3, bf16[1056,2048]{1,0:T(8,128)(2,1)} %get-tuple-element.25.rows_ref), custom_call_target="tpu_custom_call" | custom-call | flops 1660944 | bytes 6930 | tf_op jit(solution)/shard_map/pallas_call | solution.py:376
  169.7 8.5 %shard_map.125.kept_ref = f32[2,512,1536]{2,1,0:T(8,128)} custom-call(s32[2]{0:T(128)S(1)} %get-tuple-element.30.share_ref, f32[8,6]{1,0:T(8,128)S(1)} %bitcast.37, bf16[1056,2048]{1,0:T(8,128)(2,1)} %get-tuple-element.19.rows_ref, bf16[1056,768]{1,0:T(8,128)(2,1)S(1)} %get-tuple-element.23.gate_grad_ref, ...), custom_call_target="tpu_custom_call" | custom-call | flops 3321888 | bytes 11698 | tf_op jit(solution)/shard_map/pallas_call | solution.py:347
  179.6 4.6 %fusion.1.after_in = bf16[512,1536]{1,0:T(8,128)(2,1)} fusion(f32[2,512,1536]{2,1,0:T(8,128)} %shard_map.125.kept_ref, bf16[2,512,1536]{2,1,0:T(8,128)(2,1)S(1)} %collective-permute-done.got_ref), kind=kLoop, calls=%fused_computation.2 | loop fusion | flops 2359296 | bytes 6291456 | tf_op jit(solution)/shard_map/convert_element_type | solution.py:583
  184.2 12.2 %shard_map.132 = bf16[32,528,128]{2,1,0:T(8,128)(2,1)} custom-call(bf16[1056,768]{1,0:T(8,128)(2,1)S(1)} %get-tuple-element.23.gate_grad_ref, bf16[1056,768]{1,0:T(8,128)(2,1)S(1)} %get-tuple-element.24.up_grad_ref, bf16[2048,1536]{1,0:T(8,128)(2,1)} %shard_map.120.gate_w_ref.up_w_ref.weight_ref, bf16[512,1536]{1,0:T(8,128)(2,1)} %fusion.1.after_in, ...), custom_call_target="tpu_custom_call" | custom-call | flops 6643777 | bytes 13860 | tf_op jit(solution)/shard_map/pallas_call | solution.py:323
  196.4 6.7 %all-to-all-start.3 = ((bf16[16,1056,128]{2,1,0:T(8,128)(2,1)}), bf16[16,1056,128]{2,1,0:T(8,128)(2,1)}, u32[]{:S(2)}, u32[]{:S(2)}) async-start(bf16[16,1056,128]{2,1,0:T(8,128)(2,1)} %bitcast.46), calls=%async_computation.3 | async-start | bytes 8650752 | tf_op jit(solution)/shard_map/all_to_all | solution.py:546
  203.2 3.3 %collective-permute-start.4 = (bf16[512,1536]{1,0:T(8,128)(2,1)}, bf16[512,1536]{1,0:T(8,128)(2,1)}, u32[]{:S(2)}, u32[]{:S(2)}) collective-permute-start(bf16[512,1536]{1,0:T(8,128)(2,1)} %fusion.1.after_in), channel_id=1, source_target_pairs={{0,64},{1,65},{2,66},{3,67},{4,68},{5,69},{6,70},{7,71},{8,72},{9,... | collective-permute-start | bytes 4718600 | tf_op jit(solution)/shard_map/ppermute | solution.py:557
  208.0 3.1 %shard_map.127.after_in.near_ref = f32[512,1536]{1,0:T(8,128)S(1)} custom-call(f32[2,512,1536]{2,1,0:T(8,128)} %shard_map.125.kept_ref, bf16[2,512,1536]{2,1,0:T(8,128)(2,1)} %copy-done.12, bf16[32,528,128]{2,1,0:T(8,128)(2,1)} %all-to-all-done.1.after_ref.packed_ref), custom_call_target="tpu_custom_call" | custom-call | flops 786 | bytes 7864 | tf_op jit(solution)/shard_map/pallas_call | solution.py:485
  211.2 6.1 %shard_map.131 = (bf16[128,2048]{1,0:T(8,128)(2,1)}, f32[8,128]{1,0:T(8,128)}, s32[8,128]{1,0:T(8,128)S(1)}) custom-call(s32[8,128]{1,0:T(8,128)S(1)} %bitcast.39, bf16[8,128]{1,0:T(8,128)(2,1)S(1)} %bitcast.45, bf16[128,2048]{1,0:T(8,128)(2,1)S(1)} %bitcast.34, bf16[32,528,128]{2,1,0:T(8,128)(2,1)} %all-to-all-done.1.after_ref.packed_ref, ...), custom_call_target="tpu_custom_call" | custom-call | flops 1107296 | bytes 5373 | tf_op jit(solution)/shard_map/pallas_call | solution.py:523
  218.1 39.3 %collective-permute-done.2.routes_ref = s32[8,128]{1,0:T(8,128)S(1)} collective-permute-done((s32[8,128]{1,0:T(8,128)S(1)}, s32[8,128]{1,0:T(8,128)S(1)}, u32[]{:S(2)}, u32[]{:S(2)}) %collective-permute-start.2) | collective-permute-done | bytes 4128 | tf_op jit(solution)/shard_map/ppermute | solution.py:552
  260.0 4.4 %collective-permute-start.3 = (bf16[128,2048]{1,0:T(8,128)(2,1)S(1)}, bf16[128,2048]{1,0:T(8,128)(2,1)S(1)}, u32[]{:S(2)}, u32[]{:S(2)}) collective-permute-start(bf16[128,2048]{1,0:T(8,128)(2,1)S(1)} %shard_map.133.refs_0_.after_ref), channel_id=1, source_target_pairs={{0,1},{1,0},{2,3},{3,2},{4,5},{5,4},{6,7},{7,6},{8,9},{9,8},{10,11... | collective-permute-start | bytes 1572872 | tf_op jit(solution)/shard_map/ppermute | solution.py:552
  266.7 2.9 %shard_map.135 = f32[512,1536]{1,0:T(8,128)} custom-call(f32[512,1536]{1,0:T(8,128)S(1)} %shard_map.127.after_in.near_ref, bf16[512,1536]{1,0:T(8,128)(2,1)} %collective-permute-done.4.far_ref, bf16[128,2048]{1,0:T(8,128)(2,1)S(1)} %shard_map.133.refs_0_.after_ref), custom_call_target="tpu_custom_call" | custom-call | flops 1572 | bytes 7864 | tf_op jit(solution)/shard_map/pallas_call | solution.py:467
  272.2 3.2 %collective-permute-done.3 = bf16[128,2048]{1,0:T(8,128)(2,1)S(1)} collective-permute-done((bf16[128,2048]{1,0:T(8,128)(2,1)S(1)}, bf16[128,2048]{1,0:T(8,128)(2,1)S(1)}, u32[]{:S(2)}, u32[]{:S(2)}) %collective-permute-start.3) | collective-permute-done | bytes 524320 | tf_op jit(solution)/shard_map/ppermute | solution.py:552
  (54 shorter events, 18.4 us)
Async XLA Ops:
  68.0 5.6 %copy-start.13 = (f32[1,1,8,6]{2,1,3,0:T(1,128)S(1)}, f32[1,1,8,6]{2,1,3,0:T(1,128)}, u32[]{:S(2)}) copy-start(f32[1,1,8,6]{2,1,3,0:T(1,128)} %param.14) | copy-start | bytes 580
  68.0 5.7 %copy-start.14 = (f32[1,1,3,8]{3,1,2,0:T(1,128)S(1)}, f32[1,1,3,8]{3,1,2,0:T(1,128)}, u32[]{:S(2)}) copy-start(f32[1,1,3,8]{3,1,2,0:T(1,128)} %param.15) | copy-start | bytes 292
  68.0 9.0 %slice-start = ((s8[4325376]{0:T(1024)(128)(4,1)}), s8[131072]{0:T(1024)(128)(4,1)S(1)}, s32[]{:S(2)}) async-start(s8[4325376]{0:T(1024)(128)(4,1)} %bitcast.31), calls=%async_computation.4 | async-start | bytes 262144
  68.0 62.4 %all-to-all-start.2 = ((bf16[32,528,128]{2,1,0:T(8,128)(2,1)}), bf16[32,528,128]{2,1,0:T(8,128)(2,1)}, u32[]{:S(2)}, u32[]{:S(2)}) async-start(bf16[32,528,128]{2,1,0:T(8,128)(2,1)} %get-tuple-element.20), calls=%async_computation.2 | async-start | bytes 8650752 | tf_op jit(solution)/shard_map/all_to_all | solution.py:538
  73.7 3.3 %slice-start.1 = ((s8[4325376]{0:T(1024)(128)(4,1)}), s8[4194304]{0:T(1024)(128)(4,1)S(1)}, s32[]{:S(2)}) async-start(s8[4325376]{0:T(1024)(128)(4,1)} %bitcast.31), calls=%async_computation.5 | async-start | bytes 8388608
  77.0 23.3 %copy-start = (bf16[768,2048]{1,0:T(8,128)(2,1)}, bf16[768,2048]{1,0:T(8,128)(2,1)S(1)}, u32[]{:S(2)}) copy-start(bf16[768,2048]{1,0:T(8,128)(2,1)S(1)} %shard_map.122.weight_ref) | copy-start | bytes 9437188
  130.3 66.1 %all-to-all-start.1 = ((bf16[32,528,128]{2,1,0:T(8,128)(2,1)}), bf16[32,528,128]{2,1,0:T(8,128)(2,1)}, u32[]{:S(2)}, u32[]{:S(2)}) async-start(bf16[32,528,128]{2,1,0:T(8,128)(2,1)} %shard_map.123.after_ref), calls=%async_computation.1 | async-start | bytes 8650752 | tf_op jit(solution)/shard_map/all_to_all | solution.py:538
  148.9 10.4 %copy-start.3 = (bf16[1056,768]{1,0:T(8,128)(2,1)S(1)}, bf16[1056,768]{1,0:T(8,128)(2,1)}, u32[]{:S(2)}) copy-start(bf16[1056,768]{1,0:T(8,128)(2,1)} %copy-done.2) | copy-start | bytes 4866052
  156.5 23.1 %collective-permute-start = (bf16[2,512,1536]{2,1,0:T(8,128)(2,1)}, bf16[2,512,1536]{2,1,0:T(8,128)(2,1)S(1)}, u32[]{:S(2)}, u32[]{:S(2)}) collective-permute-start(bf16[2,512,1536]{2,1,0:T(8,128)(2,1)} %shard_map.126), channel_id=1, source_target_pairs={{0,32},{1,33},{2,34},{3,35},{4,36},{5,37},{6,38},{7,39},{8,40},{9,... | collective-permute-start | bytes 9437192 | tf_op jit(solution)/shard_map/ppermute | solution.py:557
  164.4 13.8 %collective-permute-start.1 = (bf16[2,768,512]{2,1,0:T(8,128)(2,1)S(1)}, bf16[2,768,512]{2,1,0:T(8,128)(2,1)S(1)}, u32[]{:S(2)}, u32[]{:S(2)}) collective-permute-start(bf16[2,768,512]{2,1,0:T(8,128)(2,1)S(1)} %shard_map.129), channel_id=1, source_target_pairs={{0,32},{1,33},{2,34},{3,35},{4,36},{5,37},{6,38},{7,39},{8,40},{9,... | collective-permute-start | bytes 4718600 | tf_op jit(solution)/shard_map/ppermute | solution.py:557
  169.7 8.5 %copy-start.1 = (f32[2,768,512]{2,1,0:T(8,128)}, f32[2,768,512]{2,1,0:T(8,128)S(1)}, u32[]{:S(2)}) copy-start(f32[2,768,512]{2,1,0:T(8,128)S(1)} %shard_map.128.kept_ref) | copy-start | bytes 9437188
  178.2 6.0 %copy-start.6 = (bf16[2,768,512]{2,1,0:T(8,128)(2,1)}, bf16[2,768,512]{2,1,0:T(8,128)(2,1)S(1)}, u32[]{:S(2)}) copy-start(bf16[2,768,512]{2,1,0:T(8,128)(2,1)S(1)} %collective-permute-done.1.got_ref) | copy-start | bytes 4718596
  179.6 4.6 %copy-start.12 = (bf16[2,512,1536]{2,1,0:T(8,128)(2,1)}, bf16[2,512,1536]{2,1,0:T(8,128)(2,1)S(1)}, u32[]{:S(2)}) copy-start(bf16[2,512,1536]{2,1,0:T(8,128)(2,1)S(1)} %collective-permute-done.got_ref) | copy-start | bytes 9437188
  196.4 10.1 %copy-start.7 = (bf16[2,768,512]{2,1,0:T(8,128)(2,1)S(1)}, bf16[2,768,512]{2,1,0:T(8,128)(2,1)}, u32[]{:S(2)}) copy-start(bf16[2,768,512]{2,1,0:T(8,128)(2,1)} %copy-done.6) | copy-start | bytes 4718596
  196.4 60.9 %all-to-all-start.3 = ((bf16[16,1056,128]{2,1,0:T(8,128)(2,1)}), bf16[16,1056,128]{2,1,0:T(8,128)(2,1)}, u32[]{:S(2)}, u32[]{:S(2)}) async-start(bf16[16,1056,128]{2,1,0:T(8,128)(2,1)} %bitcast.46), calls=%async_computation.3 | async-start | bytes 8650752 | tf_op jit(solution)/shard_map/all_to_all | solution.py:546
  203.2 63.5 %collective-permute-start.4 = (bf16[512,1536]{1,0:T(8,128)(2,1)}, bf16[512,1536]{1,0:T(8,128)(2,1)}, u32[]{:S(2)}, u32[]{:S(2)}) collective-permute-start(bf16[512,1536]{1,0:T(8,128)(2,1)} %fusion.1.after_in), channel_id=1, source_target_pairs={{0,64},{1,65},{2,66},{3,67},{4,68},{5,69},{6,70},{7,71},{8,72},{9,... | collective-permute-start | bytes 4718600 | tf_op jit(solution)/shard_map/ppermute | solution.py:557
  206.4 58.0 %collective-permute-start.5 = (bf16[768,512]{1,0:T(8,128)(2,1)}, bf16[768,512]{1,0:T(8,128)(2,1)}, u32[]{:S(2)}, u32[]{:S(2)}) collective-permute-start(bf16[768,512]{1,0:T(8,128)(2,1)} %fusion.3.after_out), channel_id=1, source_target_pairs={{0,64},{1,65},{2,66},{3,67},{4,68},{5,69},{6,70},{7,71},{8,72},{9,... | collective-permute-start | bytes 2359304 | tf_op jit(solution)/shard_map/ppermute | solution.py:557
  208.0 3.1 %copy-start.4 = (f32[768,512]{1,0:T(8,128)}, f32[768,512]{1,0:T(8,128)S(1)}, u32[]{:S(2)}) copy-start(f32[768,512]{1,0:T(8,128)S(1)} %shard_map.130.after_out.near_ref) | copy-start | bytes 4718596
  208.0 3.1 %copy-start.9 = (bf16[1,128,2048]{2,1,0:T(8,128)(2,1)S(1)}, bf16[1,128,2048]{2,1,0:T(8,128)(2,1)}, u32[]{:S(2)}) copy-start(bf16[1,128,2048]{2,1,0:T(8,128)(2,1)} %param.11) | copy-start | bytes 1572868
  208.0 3.1 %copy-start.10 = (s32[1,128,8]{1,2,0:T(8,128)S(1)}, s32[1,128,8]{1,2,0:T(8,128)}, u32[]{:S(2)}) copy-start(s32[1,128,8]{1,2,0:T(8,128)} %param.9) | copy-start | bytes 12292
  208.0 3.1 %copy-start.11 = (bf16[1,128,8]{1,2,0:T(8,128)(2,1)S(1)}, bf16[1,128,8]{1,2,0:T(8,128)(2,1)}, u32[]{:S(2)}) copy-start(bf16[1,128,8]{1,2,0:T(8,128)(2,1)} %param.10) | copy-start | bytes 6148
  217.2 40.1 %collective-permute-start.2 = (s32[8,128]{1,0:T(8,128)S(1)}, s32[8,128]{1,0:T(8,128)S(1)}, u32[]{:S(2)}, u32[]{:S(2)}) collective-permute-start(s32[8,128]{1,0:T(8,128)S(1)} %get-tuple-element.27), channel_id=1, source_target_pairs={{0,1},{1,0},{2,3},{3,2},{4,5},{5,4},{6,7},{7,6},{8,9},{9,8},{10,11... | collective-permute-start | bytes 12296 | tf_op jit(solution)/shard_map/ppermute | solution.py:552
  257.4 7.1 %copy-start.5 = (f32[768,512]{1,0:T(8,128)S(1)}, f32[768,512]{1,0:T(8,128)}, u32[]{:S(2)}) copy-start(f32[768,512]{1,0:T(8,128)} %copy-done.4) | copy-start | bytes 4718596
  260.0 15.3 %collective-permute-start.3 = (bf16[128,2048]{1,0:T(8,128)(2,1)S(1)}, bf16[128,2048]{1,0:T(8,128)(2,1)S(1)}, u32[]{:S(2)}, u32[]{:S(2)}) collective-permute-start(bf16[128,2048]{1,0:T(8,128)(2,1)S(1)} %shard_map.133.refs_0_.after_ref), channel_id=1, source_target_pairs={{0,1},{1,0},{2,3},{3,2},{4,5},{5,4},{6,7},{7,6},{8,9},{9,8},{10,11... | collective-permute-start | bytes 1572872 | tf_op jit(solution)/shard_map/ppermute | solution.py:552
  (2 other events, 3.0 us)

commit v5 on v4

--- a/solution.py
+++ b/solution.py
@@ -52,10 +52,16 @@
 
 
 def place(expert):
+    return ((((expert >> 3) + 2 * (expert >> 1)) & 3) << 3) | (expert & 7)
+
+
+def plane_place(expert):
     return ((((expert >> 3) + (expert >> 1)) & 3) << 3) | (expert & 7)
 
 
 ORDER = sorted(range(BLOCKS), key=place)
+PLANE_ORDER = sorted(range(BLOCKS), key=plane_place)
+PLANE_PAIRS = [plane_place(device) // 2 for device in ORDER[::2]]
 
 
 def slot_keys(routes):
@@ -197,17 +203,25 @@
         rows_ref[BIG:, cut] = last[j * BLOCKS : (j + 1) * BLOCKS]
 
 
-def pack_columns(values, first, out_ref, last_ref):
+def put_blocks(blocks, at, count, out_ref, pairs):
+    if pairs is None:
+        out_ref[:, pl.ds(at, count), :] = blocks
+    else:
+        for m, to in enumerate(pairs):
+            out_ref[2 * to : 2 * to + 2, pl.ds(at, count), :] = blocks[2 * m : 2 * m + 2]
+
+
+def pack_columns(values, first, out_ref, last_ref, pairs=None):
     for i in range(2):
         cut = values[:, i * LANES : (i + 1) * LANES]
         at = pl.multiple_of((first + i) * MAIN, MAIN)
-        out_ref[:, pl.ds(at, MAIN), :] = cut[:BIG].reshape(BLOCKS, MAIN, LANES)
+        put_blocks(cut[:BIG].reshape(BLOCKS, MAIN, LANES), at, MAIN, out_ref, pairs)
         last_ref[pl.ds(at, BLOCKS), :] = cut[BIG:]
 
 
-def pack_last(out_ref, last_ref):
+def pack_last(out_ref, last_ref, pairs=None):
     tiles = dot(last_slot_order(False), last_ref[...]).astype(BF16)
-    out_ref[:, MAIN * COLS :, :] = tiles.reshape(BLOCKS, COLS, LANES)
+    put_blocks(tiles.reshape(BLOCKS, COLS, LANES), MAIN * COLS, COLS, out_ref, pairs)
 
 
 def gate_up_kernel(packed_ref, gate_w_ref, up_w_ref, rows_ref, gate_ref, up_ref, hidden_ref):
@@ -311,11 +325,11 @@
     step = pl.program_id(0)
     values = dot_nt(gate_grad_ref[...], weight_ref[:, :FF])
     values = (values + dot_nt(up_grad_ref[...], weight_ref[:, FF:])).astype(BF16)
-    pack_columns(values, step * 2, out_ref, last_ref)
+    pack_columns(values, step * 2, out_ref, last_ref, PLANE_PAIRS)
 
     @pl.when(step == pl.num_programs(0) - 1)
     def _():
-        pack_last(out_ref, last_ref)
+        pack_last(out_ref, last_ref, PLANE_PAIRS)
 
 
 def input_grads(gate_grad, up_grad, weight_in, after):
@@ -409,7 +423,7 @@
 def combine_kernel(plane_ref, routes_ref, packed_ref, *refs):
     out_ref = refs[-1]
     experts = BLOCKS // 2
-    key = slot_keys(place(routes_ref[...])).T + 1.0
+    key = slot_keys(plane_place(routes_ref[...])).T + 1.0
     plane = plane_ref[0]
 
     def spread(shape, width):
@@ -541,7 +555,7 @@
 
 
 def exchange_in_plane(value):
-    planes = [ORDER[z::2] for z in range(2)]
+    planes = [PLANE_ORDER[z::2] for z in range(2)]
     value = value.reshape(BLOCKS // 2, 2 * PACK, LANES)
     return lax.all_to_all(
         value, "expert", split_axis=0, concat_axis=0, tiled=True, axis_index_groups=planes

time: 280 us -> 279 us (level)
  starting transfers between devices: 32 us -> 26 us
  waiting for transfers between devices: 63.6 us -> 67.6 us
    ppermute x2, starting transfers between devices: 5.3 us -> 1.44 us  [between_planes(): return lax.ppermute(value, 'expert', [(e, e ^ 1) for e in range(BLOCKS)])]
    all_to_all x1, waiting for transfers between devices: 0.01 us -> 2.81 us  [exchange_in_plane(): lax.all_to_all(value, 'expert', split_axis=0, concat_axis=0, tiled=True,...]
  transfers between devices with their start and end apart: 9 -> 9, of which waited for: 3 -> 4; matrix products, arithmetic and copies ran while one was open for 2% -> 2% of each run, Pallas kernels for 37% -> 37%
where the time goes in v5:
time: 279 us; the launch traced here: 275 us
  Pallas kernels  109 us (39%)
  waiting for transfers between devices  67.6 us (24%)
  blocking collectives  61.1 us (22%)
  starting transfers between devices  26 us (9%)
  other arithmetic  6.99 us (3%)
  local copies, waits for them, and re-layouts  3.12 us (1%)
    all_to_all x1, blocking collectives, exchange(): lax.all_to_all(value, 'expert', split_axis=0, concat_axis=0, tiled=True,...  61.1 us
    ppermute x2, waiting for transfers between devices, between_planes(): return lax.ppermute(value, 'expert', [(e, e ^ 1) for e in range(BLOCKS)])  43.6 us
    all_to_all x2, waiting for transfers between devices, exchange(): lax.all_to_all(value, 'expert', split_axis=0, concat_axis=0, tiled=True,...  21.2 us
    pallas_call x2, Pallas kernels, weight_in_grads(): pl.pallas_call(weight_in_kernel, grid_spec=pltpu.PrefetchScalarGridSpec(n...  16.1 us
    pallas_call x1, Pallas kernels, gate_up(): pl.pallas_call(gate_up_kernel, grid=(wide,), out_shape=(jax.ShapeDtypeStr...  13 us
    pallas_call x1, Pallas kernels, input_grads(): pl.pallas_call(input_grad_kernel, grid=(D // 256,), out_shape=jax.ShapeDt...  12.2 us
    all_to_all x2, starting transfers between devices, exchange(): lax.all_to_all(value, 'expert', split_axis=0, concat_axis=0, tiled=True,...  12 us
    pallas_call x2, Pallas kernels, noisy(): pl.pallas_call(noisy_kernel, grid=(height // 256,), out_shape=jax.ShapeDt...  11.7 us
  transfers between devices with their start and end apart: 9, of which 4 were waited for; matrix products, arithmetic and copies ran while one was open for 2% of the time, Pallas kernels for 37%

profile of v5, /device:TPU:1, one launch (start us, length us, event | category | flops | bytes accessed | tf_op | source)
XLA Modules:
  0.0 274.8 jit_solution(5521330910331214179)
XLA Ops:
  0.6 6.8 %shard_map.119 = (bf16[32,528,128]{2,1,0:T(8,128)(2,1)}, bf16[32,528,128]{2,1,0:T(8,128)(2,1)}) custom-call(s32[8,128]{1,0:T(8,128)} %bitcast.38, bf16[8,128]{1,0:T(8,128)(2,1)} %bitcast.44, bf16[128,2048]{1,0:T(8,128)(2,1)} %bitcast.51, bf16[128,2048]{1,0:T(8,128)(2,1)} %bitcast.33), custom_call_target="tpu_custom_call" | custom-call | flops 1107296 | bytes 9699 | tf_op jit(solution)/shard_map/pallas_call | solution.py:154
  7.4 61.1 %all_to_all.20.after_ref.packed_ref = bf16[32,528,128]{2,1,0:T(8,128)(2,1)} all-to-all(bf16[32,528,128]{2,1,0:T(8,128)(2,1)} %get-tuple-element.17), channel_id=1, replica_groups={{0,1,18,19,4,5,22,23,8,9,26,27,12,13,30,31,16,17,2,3,20,21,6,7,24,25,10..., dimensions={0} | all-to-all | bytes 8650752 | tf_op jit(solution)/shard_map/all_to_all | solution.py:552
  68.5 5.0 %all-to-all-start.2 = ((bf16[32,528,128]{2,1,0:T(8,128)(2,1)}), bf16[32,528,128]{2,1,0:T(8,128)(2,1)}, u32[]{:S(2)}, u32[]{:S(2)}) async-start(bf16[32,528,128]{2,1,0:T(8,128)(2,1)} %get-tuple-element.20), calls=%async_computation.2 | async-start | bytes 8650752 | tf_op jit(solution)/shard_map/all_to_all | solution.py:552
  73.6 3.3 %shard_map.122.weight_ref = bf16[768,2048]{1,0:T(8,128)(2,1)S(1)} custom-call(f32[3,8]{1,0:T(4,128)S(1)} %bitcast.41, bf16[768,2048]{1,0:T(8,128)(2,1)} %bitcast.48, bf16[32,528,128]{2,1,0:T(8,128)(2,1)} %all_to_all.20.after_ref.packed_ref), custom_call_target="tpu_custom_call" | custom-call | flops 1572 | bytes 6291 | tf_op jit(solution)/shard_map/pallas_call | solution.py:183
  76.9 8.4 %shard_map.120.gate_w_ref.up_w_ref.weight_ref = bf16[2048,1536]{1,0:T(8,128)(2,1)} custom-call(f32[8,6]{1,0:T(8,128)S(1)} %bitcast.35, bf16[2048,1536]{1,0:T(8,128)(2,1)} %bitcast.47, bf16[32,528,128]{2,1,0:T(8,128)(2,1)S(1)} %bitcast.32), custom_call_target="tpu_custom_call" | custom-call | flops 3145 | bytes 12582 | tf_op jit(solution)/shard_map/pallas_call | solution.py:183
  85.3 13.0 %shard_map.121 = (bf16[1056,2048]{1,0:T(8,128)(2,1)}, f32[1056,768]{1,0:T(8,128)S(1)}, f32[1056,768]{1,0:T(8,128)}, bf16[1056,768]{1,0:T(8,128)(2,1)S(1)}) custom-call(bf16[32,528,128]{2,1,0:T(8,128)(2,1)} %all_to_all.20.after_ref.packed_ref, bf16[2048,1536]{1,0:T(8,128)(2,1)} %shard_map.120.gate_w_ref.up_w_ref.weight_ref, ...), custom_call_target="tpu_custom_call" | custom-call | flops 6643777 | bytes 23052 | tf_op jit(solution)/shard_map/pallas_call | solution.py:242
  100.2 7.8 %shard_map.123.after_ref = bf16[32,528,128]{2,1,0:T(8,128)(2,1)} custom-call(bf16[1056,768]{1,0:T(8,128)(2,1)S(1)} %get-tuple-element.18.hidden_ref, bf16[768,2048]{1,0:T(8,128)(2,1)S(1)} %shard_map.122.weight_ref), custom_call_target="tpu_custom_call" | custom-call | flops 3321888 | bytes 9093 | tf_op jit(solution)/shard_map/pallas_call | solution.py:273
  109.1 21.2 %all-to-all-done.2.packed_ref = bf16[32,528,128]{2,1,0:T(8,128)(2,1)} async-done(((bf16[32,528,128]{2,1,0:T(8,128)(2,1)}), bf16[32,528,128]{2,1,0:T(8,128)(2,1)}, u32[]{:S(2)}, u32[]{:S(2)}) %all-to-all-start.2) | async-done | bytes 4325408 | tf_op jit(solution)/shard_map/all_to_all | solution.py:552
  130.3 7.0 %all-to-all-start.1 = ((bf16[32,528,128]{2,1,0:T(8,128)(2,1)}), bf16[32,528,128]{2,1,0:T(8,128)(2,1)}, u32[]{:S(2)}, u32[]{:S(2)}) async-start(bf16[32,528,128]{2,1,0:T(8,128)(2,1)} %shard_map.123.after_ref), calls=%async_computation.1 | async-start | bytes 8650752 | tf_op jit(solution)/shard_map/all_to_all | solution.py:552
  137.4 10.5 %shard_map.124 = (bf16[1056,2048]{1,0:T(8,128)(2,1)}, bf16[1056,768]{1,0:T(8,128)(2,1)S(1)}, bf16[1056,768]{1,0:T(8,128)(2,1)S(1)}) custom-call(bf16[32,528,128]{2,1,0:T(8,128)(2,1)} %all-to-all-done.2.packed_ref, bf16[768,2048]{1,0:T(8,128)(2,1)} %copy-done, f32[1056,768]{1,0:T(8,128)} %copy-done.8, f32[1056,768]{1,0:T(8,128)} %get-tuple-element.22.up_ref, ...), custom_call_target="tpu_custom_call" | custom-call | flops 3321888 | bytes 21528 | tf_op jit(solution)/shard_map/pallas_call | solution.py:303
  147.9 7.6 %shard_map.126 = bf16[2,512,1536]{2,1,0:T(8,128)(2,1)} custom-call(s32[2]{0:T(128)S(1)} %get-tuple-element.29.share_ref, f32[8,6]{1,0:T(8,128)S(1)} %bitcast.36, bf16[1056,2048]{1,0:T(8,128)(2,1)} %get-tuple-element.19.rows_ref, bf16[1056,768]{1,0:T(8,128)(2,1)S(1)} %get-tuple-element.23.gate_grad_ref, bf16[1056,768]{1,0:T(8,128)(2,1)S(1)} %get-tuple-element.24.up_grad_ref, ...), custom_call_target="tpu_custom_call" | custom-call | flops 3321888 | bytes 11698 | tf_op jit(solution)/shard_map/pallas_call | solution.py:361
  157.8 5.1 %shard_map.129 = bf16[2,768,512]{2,1,0:T(8,128)(2,1)S(1)} custom-call(s32[2]{0:T(128)S(1)} %get-tuple-element.29.share_ref, f32[3,8]{1,0:T(4,128)S(1)} %bitcast.42, bf16[1056,768]{1,0:T(8,128)(2,1)S(1)} %copy-done.3, bf16[1056,2048]{1,0:T(8,128)(2,1)} %get-tuple-element.25.rows_ref), custom_call_target="tpu_custom_call" | custom-call | flops 1660944 | bytes 6930 | tf_op jit(solution)/shard_map/pallas_call | solution.py:390
  163.0 5.2 %shard_map.128.kept_ref = f32[2,768,512]{2,1,0:T(8,128)S(1)} custom-call(s32[2]{0:T(128)S(1)} %get-tuple-element.30.share_ref, f32[3,8]{1,0:T(4,128)S(1)} %bitcast.43, bf16[1056,768]{1,0:T(8,128)(2,1)S(1)} %copy-done.3, bf16[1056,2048]{1,0:T(8,128)(2,1)} %get-tuple-element.25.rows_ref), custom_call_target="tpu_custom_call" | custom-call | flops 1660944 | bytes 6930 | tf_op jit(solution)/shard_map/pallas_call | solution.py:390
  168.2 8.5 %shard_map.125.kept_ref = f32[2,512,1536]{2,1,0:T(8,128)} custom-call(s32[2]{0:T(128)S(1)} %get-tuple-element.30.share_ref, f32[8,6]{1,0:T(8,128)S(1)} %bitcast.37, bf16[1056,2048]{1,0:T(8,128)(2,1)} %get-tuple-element.19.rows_ref, bf16[1056,768]{1,0:T(8,128)(2,1)S(1)} %get-tuple-element.23.gate_grad_ref, ...), custom_call_target="tpu_custom_call" | custom-call | flops 3321888 | bytes 11698 | tf_op jit(solution)/shard_map/pallas_call | solution.py:361
  178.1 4.6 %fusion.1.after_in = bf16[512,1536]{1,0:T(8,128)(2,1)} fusion(f32[2,512,1536]{2,1,0:T(8,128)} %shard_map.125.kept_ref, bf16[2,512,1536]{2,1,0:T(8,128)(2,1)S(1)} %collective-permute-done.got_ref), kind=kLoop, calls=%fused_computation.2 | loop fusion | flops 2359296 | bytes 6291456 | tf_op jit(solution)/shard_map/convert_element_type | solution.py:597
  182.7 12.2 %shard_map.132 = bf16[32,528,128]{2,1,0:T(8,128)(2,1)} custom-call(bf16[1056,768]{1,0:T(8,128)(2,1)S(1)} %get-tuple-element.23.gate_grad_ref, bf16[1056,768]{1,0:T(8,128)(2,1)S(1)} %get-tuple-element.24.up_grad_ref, bf16[2048,1536]{1,0:T(8,128)(2,1)} %shard_map.120.gate_w_ref.up_w_ref.weight_ref, bf16[512,1536]{1,0:T(8,128)(2,1)} %fusion.1.after_in, ...), custom_call_target="tpu_custom_call" | custom-call | flops 6643777 | bytes 13860 | tf_op jit(solution)/shard_map/pallas_call | solution.py:337
  194.9 6.8 %all-to-all-start.3 = ((bf16[16,1056,128]{2,1,0:T(8,128)(2,1)}), bf16[16,1056,128]{2,1,0:T(8,128)(2,1)}, u32[]{:S(2)}, u32[]{:S(2)}) async-start(bf16[16,1056,128]{2,1,0:T(8,128)(2,1)} %bitcast.46), calls=%async_computation.3 | async-start | bytes 8650752 | tf_op jit(solution)/shard_map/all_to_all | solution.py:560
  201.7 3.1 %collective-permute-start.4 = (bf16[512,1536]{1,0:T(8,128)(2,1)}, bf16[512,1536]{1,0:T(8,128)(2,1)}, u32[]{:S(2)}, u32[]{:S(2)}) collective-permute-start(bf16[512,1536]{1,0:T(8,128)(2,1)} %fusion.1.after_in), channel_id=1, source_target_pairs={{0,64},{1,65},{2,66},{3,67},{4,68},{5,69},{6,70},{7,71},{8,72},{9,... | collective-permute-start | bytes 4718600 | tf_op jit(solution)/shard_map/ppermute | solution.py:571
  206.4 3.1 %shard_map.127.after_in.near_ref = f32[512,1536]{1,0:T(8,128)S(1)} custom-call(f32[2,512,1536]{2,1,0:T(8,128)} %shard_map.125.kept_ref, bf16[2,512,1536]{2,1,0:T(8,128)(2,1)} %copy-done.12, bf16[32,528,128]{2,1,0:T(8,128)(2,1)} %all-to-all-done.1.after_ref.packed_ref), custom_call_target="tpu_custom_call" | custom-call | flops 786 | bytes 7864 | tf_op jit(solution)/shard_map/pallas_call | solution.py:499
  209.5 6.1 %shard_map.131 = (bf16[128,2048]{1,0:T(8,128)(2,1)}, f32[8,128]{1,0:T(8,128)}, s32[8,128]{1,0:T(8,128)S(1)}) custom-call(s32[8,128]{1,0:T(8,128)S(1)} %bitcast.39, bf16[8,128]{1,0:T(8,128)(2,1)S(1)} %bitcast.45, bf16[128,2048]{1,0:T(8,128)(2,1)S(1)} %bitcast.34, bf16[32,528,128]{2,1,0:T(8,128)(2,1)} %all-to-all-done.1.after_ref.packed_ref, ...), custom_call_target="tpu_custom_call" | custom-call | flops 1107296 | bytes 5373 | tf_op jit(solution)/shard_map/pallas_call | solution.py:537
  216.6 39.6 %collective-permute-done.2.routes_ref = s32[8,128]{1,0:T(8,128)S(1)} collective-permute-done((s32[8,128]{1,0:T(8,128)S(1)}, s32[8,128]{1,0:T(8,128)S(1)}, u32[]{:S(2)}, u32[]{:S(2)}) %collective-permute-start.2) | collective-permute-done | bytes 4128 | tf_op jit(solution)/shard_map/ppermute | solution.py:566
  256.2 2.8 %all-to-all-done.3 = bf16[16,1056,128]{2,1,0:T(8,128)(2,1)} async-done(((bf16[16,1056,128]{2,1,0:T(8,128)(2,1)}), bf16[16,1056,128]{2,1,0:T(8,128)(2,1)}, u32[]{:S(2)}, u32[]{:S(2)}) %all-to-all-start.3) | async-done | bytes 4325408 | tf_op jit(solution)/shard_map/all_to_all | solution.py:560
  264.4 2.9 %shard_map.135 = f32[512,1536]{1,0:T(8,128)} custom-call(f32[512,1536]{1,0:T(8,128)S(1)} %shard_map.127.after_in.near_ref, bf16[512,1536]{1,0:T(8,128)(2,1)} %collective-permute-done.4.far_ref, bf16[128,2048]{1,0:T(8,128)(2,1)S(1)} %shard_map.133.refs_0_.after_ref), custom_call_target="tpu_custom_call" | custom-call | flops 1572 | bytes 7864 | tf_op jit(solution)/shard_map/pallas_call | solution.py:481
  269.9 4.0 %collective-permute-done.3 = bf16[128,2048]{1,0:T(8,128)(2,1)S(1)} collective-permute-done((bf16[128,2048]{1,0:T(8,128)(2,1)S(1)}, bf16[128,2048]{1,0:T(8,128)(2,1)S(1)}, u32[]{:S(2)}, u32[]{:S(2)}) %collective-permute-start.3) | collective-permute-done | bytes 524320 | tf_op jit(solution)/shard_map/ppermute | solution.py:566
  (54 shorter events, 18.5 us)
Async XLA Ops:
  68.5 5.0 %copy-start.13 = (f32[1,1,8,6]{2,1,3,0:T(1,128)S(1)}, f32[1,1,8,6]{2,1,3,0:T(1,128)}, u32[]{:S(2)}) copy-start(f32[1,1,8,6]{2,1,3,0:T(1,128)} %param.14) | copy-start | bytes 580
  68.5 5.1 %copy-start.14 = (f32[1,1,3,8]{3,1,2,0:T(1,128)S(1)}, f32[1,1,3,8]{3,1,2,0:T(1,128)}, u32[]{:S(2)}) copy-start(f32[1,1,3,8]{3,1,2,0:T(1,128)} %param.15) | copy-start | bytes 292
  68.5 8.4 %slice-start = ((s8[4325376]{0:T(1024)(128)(4,1)}), s8[131072]{0:T(1024)(128)(4,1)S(1)}, s32[]{:S(2)}) async-start(s8[4325376]{0:T(1024)(128)(4,1)} %bitcast.31), calls=%async_computation.4 | async-start | bytes 262144
  68.5 61.8 %all-to-all-start.2 = ((bf16[32,528,128]{2,1,0:T(8,128)(2,1)}), bf16[32,528,128]{2,1,0:T(8,128)(2,1)}, u32[]{:S(2)}, u32[]{:S(2)}) async-start(bf16[32,528,128]{2,1,0:T(8,128)(2,1)} %get-tuple-element.20), calls=%async_computation.2 | async-start | bytes 8650752 | tf_op jit(solution)/shard_map/all_to_all | solution.py:552
  73.6 3.3 %slice-start.1 = ((s8[4325376]{0:T(1024)(128)(4,1)}), s8[4194304]{0:T(1024)(128)(4,1)S(1)}, s32[]{:S(2)}) async-start(s8[4325376]{0:T(1024)(128)(4,1)} %bitcast.31), calls=%async_computation.5 | async-start | bytes 8388608
  76.9 23.3 %copy-start = (bf16[768,2048]{1,0:T(8,128)(2,1)}, bf16[768,2048]{1,0:T(8,128)(2,1)S(1)}, u32[]{:S(2)}) copy-start(bf16[768,2048]{1,0:T(8,128)(2,1)S(1)} %shard_map.122.weight_ref) | copy-start | bytes 9437188
  130.3 64.6 %all-to-all-start.1 = ((bf16[32,528,128]{2,1,0:T(8,128)(2,1)}), bf16[32,528,128]{2,1,0:T(8,128)(2,1)}, u32[]{:S(2)}, u32[]{:S(2)}) async-start(bf16[32,528,128]{2,1,0:T(8,128)(2,1)} %shard_map.123.after_ref), calls=%async_computation.1 | async-start | bytes 8650752 | tf_op jit(solution)/shard_map/all_to_all | solution.py:552
  147.9 10.0 %copy-start.3 = (bf16[1056,768]{1,0:T(8,128)(2,1)S(1)}, bf16[1056,768]{1,0:T(8,128)(2,1)}, u32[]{:S(2)}) copy-start(bf16[1056,768]{1,0:T(8,128)(2,1)} %copy-done.2) | copy-start | bytes 4866052
  155.4 22.7 %collective-permute-start = (bf16[2,512,1536]{2,1,0:T(8,128)(2,1)}, bf16[2,512,1536]{2,1,0:T(8,128)(2,1)S(1)}, u32[]{:S(2)}, u32[]{:S(2)}) collective-permute-start(bf16[2,512,1536]{2,1,0:T(8,128)(2,1)} %shard_map.126), channel_id=1, source_target_pairs={{0,32},{1,33},{2,34},{3,35},{4,36},{5,37},{6,38},{7,39},{8,40},{9,... | collective-permute-start | bytes 9437192 | tf_op jit(solution)/shard_map/ppermute | solution.py:571
  162.9 13.8 %collective-permute-start.1 = (bf16[2,768,512]{2,1,0:T(8,128)(2,1)S(1)}, bf16[2,768,512]{2,1,0:T(8,128)(2,1)S(1)}, u32[]{:S(2)}, u32[]{:S(2)}) collective-permute-start(bf16[2,768,512]{2,1,0:T(8,128)(2,1)S(1)} %shard_map.129), channel_id=1, source_target_pairs={{0,32},{1,33},{2,34},{3,35},{4,36},{5,37},{6,38},{7,39},{8,40},{9,... | collective-permute-start | bytes 4718600 | tf_op jit(solution)/shard_map/ppermute | solution.py:571
  168.2 8.5 %copy-start.1 = (f32[2,768,512]{2,1,0:T(8,128)}, f32[2,768,512]{2,1,0:T(8,128)S(1)}, u32[]{:S(2)}) copy-start(f32[2,768,512]{2,1,0:T(8,128)S(1)} %shard_map.128.kept_ref) | copy-start | bytes 9437188
  176.7 6.0 %copy-start.6 = (bf16[2,768,512]{2,1,0:T(8,128)(2,1)}, bf16[2,768,512]{2,1,0:T(8,128)(2,1)S(1)}, u32[]{:S(2)}) copy-start(bf16[2,768,512]{2,1,0:T(8,128)(2,1)S(1)} %collective-permute-done.1.got_ref) | copy-start | bytes 4718596
  178.1 4.6 %copy-start.12 = (bf16[2,512,1536]{2,1,0:T(8,128)(2,1)}, bf16[2,512,1536]{2,1,0:T(8,128)(2,1)S(1)}, u32[]{:S(2)}) copy-start(bf16[2,512,1536]{2,1,0:T(8,128)(2,1)S(1)} %collective-permute-done.got_ref) | copy-start | bytes 9437188
  194.9 10.0 %copy-start.7 = (bf16[2,768,512]{2,1,0:T(8,128)(2,1)S(1)}, bf16[2,768,512]{2,1,0:T(8,128)(2,1)}, u32[]{:S(2)}) copy-start(bf16[2,768,512]{2,1,0:T(8,128)(2,1)} %copy-done.6) | copy-start | bytes 4718596
  194.9 64.1 %all-to-all-start.3 = ((bf16[16,1056,128]{2,1,0:T(8,128)(2,1)}), bf16[16,1056,128]{2,1,0:T(8,128)(2,1)}, u32[]{:S(2)}, u32[]{:S(2)}) async-start(bf16[16,1056,128]{2,1,0:T(8,128)(2,1)} %bitcast.46), calls=%async_computation.3 | async-start | bytes 8650752 | tf_op jit(solution)/shard_map/all_to_all | solution.py:560
  201.7 62.7 %collective-permute-start.4 = (bf16[512,1536]{1,0:T(8,128)(2,1)}, bf16[512,1536]{1,0:T(8,128)(2,1)}, u32[]{:S(2)}, u32[]{:S(2)}) collective-permute-start(bf16[512,1536]{1,0:T(8,128)(2,1)} %fusion.1.after_in), channel_id=1, source_target_pairs={{0,64},{1,65},{2,66},{3,67},{4,68},{5,69},{6,70},{7,71},{8,72},{9,... | collective-permute-start | bytes 4718600 | tf_op jit(solution)/shard_map/ppermute | solution.py:571
  204.8 57.3 %collective-permute-start.5 = (bf16[768,512]{1,0:T(8,128)(2,1)}, bf16[768,512]{1,0:T(8,128)(2,1)}, u32[]{:S(2)}, u32[]{:S(2)}) collective-permute-start(bf16[768,512]{1,0:T(8,128)(2,1)} %fusion.3.after_out), channel_id=1, source_target_pairs={{0,64},{1,65},{2,66},{3,67},{4,68},{5,69},{6,70},{7,71},{8,72},{9,... | collective-permute-start | bytes 2359304 | tf_op jit(solution)/shard_map/ppermute | solution.py:571
  206.4 3.1 %copy-start.4 = (f32[768,512]{1,0:T(8,128)}, f32[768,512]{1,0:T(8,128)S(1)}, u32[]{:S(2)}) copy-start(f32[768,512]{1,0:T(8,128)S(1)} %shard_map.130.after_out.near_ref) | copy-start | bytes 4718596
  206.4 3.1 %copy-start.9 = (bf16[1,128,2048]{2,1,0:T(8,128)(2,1)S(1)}, bf16[1,128,2048]{2,1,0:T(8,128)(2,1)}, u32[]{:S(2)}) copy-start(bf16[1,128,2048]{2,1,0:T(8,128)(2,1)} %param.11) | copy-start | bytes 1572868
  206.4 3.1 %copy-start.10 = (s32[1,128,8]{1,2,0:T(8,128)S(1)}, s32[1,128,8]{1,2,0:T(8,128)}, u32[]{:S(2)}) copy-start(s32[1,128,8]{1,2,0:T(8,128)} %param.9) | copy-start | bytes 12292
  206.4 3.1 %copy-start.11 = (bf16[1,128,8]{1,2,0:T(8,128)(2,1)S(1)}, bf16[1,128,8]{1,2,0:T(8,128)(2,1)}, u32[]{:S(2)}) copy-start(bf16[1,128,8]{1,2,0:T(8,128)(2,1)} %param.10) | copy-start | bytes 6148
  215.6 40.6 %collective-permute-start.2 = (s32[8,128]{1,0:T(8,128)S(1)}, s32[8,128]{1,0:T(8,128)S(1)}, u32[]{:S(2)}, u32[]{:S(2)}) collective-permute-start(s32[8,128]{1,0:T(8,128)S(1)} %get-tuple-element.27), channel_id=1, source_target_pairs={{0,1},{1,0},{2,3},{3,2},{4,5},{5,4},{6,7},{7,6},{8,9},{9,8},{10,11... | collective-permute-start | bytes 12296 | tf_op jit(solution)/shard_map/ppermute | solution.py:566
  259.0 3.1 %copy-start.5 = (f32[768,512]{1,0:T(8,128)S(1)}, f32[768,512]{1,0:T(8,128)}, u32[]{:S(2)}) copy-start(f32[768,512]{1,0:T(8,128)} %copy-done.4) | copy-start | bytes 4718596
  261.7 12.2 %collective-permute-start.3 = (bf16[128,2048]{1,0:T(8,128)(2,1)S(1)}, bf16[128,2048]{1,0:T(8,128)(2,1)S(1)}, u32[]{:S(2)}, u32[]{:S(2)}) collective-permute-start(bf16[128,2048]{1,0:T(8,128)(2,1)S(1)} %shard_map.133.refs_0_.after_ref), channel_id=1, source_target_pairs={{0,1},{1,0},{2,3},{3,2},{4,5},{5,4},{6,7},{7,6},{8,9},{9,8},{10,11... | collective-permute-start | bytes 1572872 | tf_op jit(solution)/shard_map/ppermute | solution.py:566
  (2 other events, 3.0 us)

commit v6 on v5

--- a/solution.py
+++ b/solution.py
@@ -52,7 +52,7 @@
 
 
 def place(expert):
-    return ((((expert >> 3) + 2 * (expert >> 1)) & 3) << 3) | (expert & 7)
+    return ((((expert >> 1) + 2 * (expert >> 3)) & 3) << 3) | ((expert >> 3) << 1) | (expert & 1)
 
 
 def plane_place(expert):

time: 279 us -> 279 us (level)
  no operation moved by 1% of the time
where the time goes in v6:
time: 279 us; the launch traced here: 275 us
  Pallas kernels  109 us (39%)
  waiting for transfers between devices  68 us (24%)
  blocking collectives  61.7 us (22%)
  starting transfers between devices  25.5 us (9%)
  other arithmetic  6.99 us (3%)
  local copies, waits for them, and re-layouts  3.12 us (1%)
    all_to_all x1, blocking collectives, exchange(): lax.all_to_all(value, 'expert', split_axis=0, concat_axis=0, tiled=True,...  61.7 us
    ppermute x2, waiting for transfers between devices, between_planes(): return lax.ppermute(value, 'expert', [(e, e ^ 1) for e in range(BLOCKS)])  43.1 us
    all_to_all x2, waiting for transfers between devices, exchange(): lax.all_to_all(value, 'expert', split_axis=0, concat_axis=0, tiled=True,...  22.4 us
    pallas_call x2, Pallas kernels, weight_in_grads(): pl.pallas_call(weight_in_kernel, grid_spec=pltpu.PrefetchScalarGridSpec(n...  16 us
    pallas_call x1, Pallas kernels, gate_up(): pl.pallas_call(gate_up_kernel, grid=(wide,), out_shape=(jax.ShapeDtypeStr...  13 us
    pallas_call x1, Pallas kernels, input_grads(): pl.pallas_call(input_grad_kernel, grid=(D // 256,), out_shape=jax.ShapeDt...  12.2 us
    pallas_call x2, Pallas kernels, noisy(): pl.pallas_call(noisy_kernel, grid=(height // 256,), out_shape=jax.ShapeDt...  11.7 us
    all_to_all x2, starting transfers between devices, exchange(): lax.all_to_all(value, 'expert', split_axis=0, concat_axis=0, tiled=True,...  10.5 us
  transfers between devices with their start and end apart: 9, of which 4 were waited for; matrix products, arithmetic and copies ran while one was open for 2% of the time, Pallas kernels for 37%

profile of v6, /device:TPU:1, one launch (start us, length us, event | category | flops | bytes accessed | tf_op | source)
XLA Modules:
  0.0 275.2 jit_solution(18343381822994166541)
XLA Ops:
  0.6 6.8 %shard_map.119 = (bf16[32,528,128]{2,1,0:T(8,128)(2,1)}, bf16[32,528,128]{2,1,0:T(8,128)(2,1)}) custom-call(s32[8,128]{1,0:T(8,128)} %bitcast.38, bf16[8,128]{1,0:T(8,128)(2,1)} %bitcast.44, bf16[128,2048]{1,0:T(8,128)(2,1)} %bitcast.51, bf16[128,2048]{1,0:T(8,128)(2,1)} %bitcast.33), custom_call_target="tpu_custom_call" | custom-call | flops 1107296 | bytes 9699 | tf_op jit(solution)/shard_map/pallas_call | solution.py:154
  7.4 61.7 %all_to_all.20.after_ref.packed_ref = bf16[32,528,128]{2,1,0:T(8,128)(2,1)} all-to-all(bf16[32,528,128]{2,1,0:T(8,128)(2,1)} %get-tuple-element.17), channel_id=1, replica_groups={{0,1,12,13,16,17,28,29,2,3,14,15,18,19,30,31,4,5,8,9,20,21,24,25,6,7,10..., dimensions={0} | all-to-all | bytes 8650752 | tf_op jit(solution)/shard_map/all_to_all | solution.py:552
  69.1 5.0 %all-to-all-start.2 = ((bf16[32,528,128]{2,1,0:T(8,128)(2,1)}), bf16[32,528,128]{2,1,0:T(8,128)(2,1)}, u32[]{:S(2)}, u32[]{:S(2)}) async-start(bf16[32,528,128]{2,1,0:T(8,128)(2,1)} %get-tuple-element.20), calls=%async_computation.2 | async-start | bytes 8650752 | tf_op jit(solution)/shard_map/all_to_all | solution.py:552
  74.2 3.3 %shard_map.122.weight_ref = bf16[768,2048]{1,0:T(8,128)(2,1)S(1)} custom-call(f32[3,8]{1,0:T(4,128)S(1)} %bitcast.41, bf16[768,2048]{1,0:T(8,128)(2,1)} %bitcast.48, bf16[32,528,128]{2,1,0:T(8,128)(2,1)} %all_to_all.20.after_ref.packed_ref), custom_call_target="tpu_custom_call" | custom-call | flops 1572 | bytes 6291 | tf_op jit(solution)/shard_map/pallas_call | solution.py:183
  77.5 8.4 %shard_map.120.gate_w_ref.up_w_ref.weight_ref = bf16[2048,1536]{1,0:T(8,128)(2,1)} custom-call(f32[8,6]{1,0:T(8,128)S(1)} %bitcast.35, bf16[2048,1536]{1,0:T(8,128)(2,1)} %bitcast.47, bf16[32,528,128]{2,1,0:T(8,128)(2,1)S(1)} %bitcast.32), custom_call_target="tpu_custom_call" | custom-call | flops 3145 | bytes 12582 | tf_op jit(solution)/shard_map/pallas_call | solution.py:183
  85.9 13.0 %shard_map.121 = (bf16[1056,2048]{1,0:T(8,128)(2,1)}, f32[1056,768]{1,0:T(8,128)S(1)}, f32[1056,768]{1,0:T(8,128)}, bf16[1056,768]{1,0:T(8,128)(2,1)S(1)}) custom-call(bf16[32,528,128]{2,1,0:T(8,128)(2,1)} %all_to_all.20.after_ref.packed_ref, bf16[2048,1536]{1,0:T(8,128)(2,1)} %shard_map.120.gate_w_ref.up_w_ref.weight_ref, ...), custom_call_target="tpu_custom_call" | custom-call | flops 6643777 | bytes 23052 | tf_op jit(solution)/shard_map/pallas_call | solution.py:242
  100.7 7.8 %shard_map.123.after_ref = bf16[32,528,128]{2,1,0:T(8,128)(2,1)} custom-call(bf16[1056,768]{1,0:T(8,128)(2,1)S(1)} %get-tuple-element.18.hidden_ref, bf16[768,2048]{1,0:T(8,128)(2,1)S(1)} %shard_map.122.weight_ref), custom_call_target="tpu_custom_call" | custom-call | flops 3321888 | bytes 9093 | tf_op jit(solution)/shard_map/pallas_call | solution.py:273
  109.7 22.4 %all-to-all-done.2.packed_ref = bf16[32,528,128]{2,1,0:T(8,128)(2,1)} async-done(((bf16[32,528,128]{2,1,0:T(8,128)(2,1)}), bf16[32,528,128]{2,1,0:T(8,128)(2,1)}, u32[]{:S(2)}, u32[]{:S(2)}) %all-to-all-start.2) | async-done | bytes 4325408 | tf_op jit(solution)/shard_map/all_to_all | solution.py:552
  132.1 5.5 %all-to-all-start.1 = ((bf16[32,528,128]{2,1,0:T(8,128)(2,1)}), bf16[32,528,128]{2,1,0:T(8,128)(2,1)}, u32[]{:S(2)}, u32[]{:S(2)}) async-start(bf16[32,528,128]{2,1,0:T(8,128)(2,1)} %shard_map.123.after_ref), calls=%async_computation.1 | async-start | bytes 8650752 | tf_op jit(solution)/shard_map/all_to_all | solution.py:552
  137.7 10.5 %shard_map.124 = (bf16[1056,2048]{1,0:T(8,128)(2,1)}, bf16[1056,768]{1,0:T(8,128)(2,1)S(1)}, bf16[1056,768]{1,0:T(8,128)(2,1)S(1)}) custom-call(bf16[32,528,128]{2,1,0:T(8,128)(2,1)} %all-to-all-done.2.packed_ref, bf16[768,2048]{1,0:T(8,128)(2,1)} %copy-done, f32[1056,768]{1,0:T(8,128)} %copy-done.8, f32[1056,768]{1,0:T(8,128)} %get-tuple-element.22.up_ref, ...), custom_call_target="tpu_custom_call" | custom-call | flops 3321888 | bytes 21528 | tf_op jit(solution)/shard_map/pallas_call | solution.py:303
  148.2 7.5 %shard_map.126 = bf16[2,512,1536]{2,1,0:T(8,128)(2,1)} custom-call(s32[2]{0:T(128)S(1)} %get-tuple-element.29.share_ref, f32[8,6]{1,0:T(8,128)S(1)} %bitcast.36, bf16[1056,2048]{1,0:T(8,128)(2,1)} %get-tuple-element.19.rows_ref, bf16[1056,768]{1,0:T(8,128)(2,1)S(1)} %get-tuple-element.23.gate_grad_ref, bf16[1056,768]{1,0:T(8,128)(2,1)S(1)} %get-tuple-element.24.up_grad_ref, ...), custom_call_target="tpu_custom_call" | custom-call | flops 3321888 | bytes 11698 | tf_op jit(solution)/shard_map/pallas_call | solution.py:361
  158.3 5.1 %shard_map.129 = bf16[2,768,512]{2,1,0:T(8,128)(2,1)S(1)} custom-call(s32[2]{0:T(128)S(1)} %get-tuple-element.29.share_ref, f32[3,8]{1,0:T(4,128)S(1)} %bitcast.42, bf16[1056,768]{1,0:T(8,128)(2,1)S(1)} %copy-done.3, bf16[1056,2048]{1,0:T(8,128)(2,1)} %get-tuple-element.25.rows_ref), custom_call_target="tpu_custom_call" | custom-call | flops 1660944 | bytes 6930 | tf_op jit(solution)/shard_map/pallas_call | solution.py:390
  163.5 5.2 %shard_map.128.kept_ref = f32[2,768,512]{2,1,0:T(8,128)S(1)} custom-call(s32[2]{0:T(128)S(1)} %get-tuple-element.30.share_ref, f32[3,8]{1,0:T(4,128)S(1)} %bitcast.43, bf16[1056,768]{1,0:T(8,128)(2,1)S(1)} %copy-done.3, bf16[1056,2048]{1,0:T(8,128)(2,1)} %get-tuple-element.25.rows_ref), custom_call_target="tpu_custom_call" | custom-call | flops 1660944 | bytes 6930 | tf_op jit(solution)/shard_map/pallas_call | solution.py:390
  168.7 8.5 %shard_map.125.kept_ref = f32[2,512,1536]{2,1,0:T(8,128)} custom-call(s32[2]{0:T(128)S(1)} %get-tuple-element.30.share_ref, f32[8,6]{1,0:T(8,128)S(1)} %bitcast.37, bf16[1056,2048]{1,0:T(8,128)(2,1)} %get-tuple-element.19.rows_ref, bf16[1056,768]{1,0:T(8,128)(2,1)S(1)} %get-tuple-element.23.gate_grad_ref, ...), custom_call_target="tpu_custom_call" | custom-call | flops 3321888 | bytes 11698 | tf_op jit(solution)/shard_map/pallas_call | solution.py:361
  178.6 4.6 %fusion.1.after_in = bf16[512,1536]{1,0:T(8,128)(2,1)} fusion(f32[2,512,1536]{2,1,0:T(8,128)} %shard_map.125.kept_ref, bf16[2,512,1536]{2,1,0:T(8,128)(2,1)S(1)} %collective-permute-done.got_ref), kind=kLoop, calls=%fused_computation.2 | loop fusion | flops 2359296 | bytes 6291456 | tf_op jit(solution)/shard_map/convert_element_type | solution.py:597
  183.2 12.2 %shard_map.132 = bf16[32,528,128]{2,1,0:T(8,128)(2,1)} custom-call(bf16[1056,768]{1,0:T(8,128)(2,1)S(1)} %get-tuple-element.23.gate_grad_ref, bf16[1056,768]{1,0:T(8,128)(2,1)S(1)} %get-tuple-element.24.up_grad_ref, bf16[2048,1536]{1,0:T(8,128)(2,1)} %shard_map.120.gate_w_ref.up_w_ref.weight_ref, bf16[512,1536]{1,0:T(8,128)(2,1)} %fusion.1.after_in, ...), custom_call_target="tpu_custom_call" | custom-call | flops 6643777 | bytes 13860 | tf_op jit(solution)/shard_map/pallas_call | solution.py:337
  195.4 6.8 %all-to-all-start.3 = ((bf16[16,1056,128]{2,1,0:T(8,128)(2,1)}), bf16[16,1056,128]{2,1,0:T(8,128)(2,1)}, u32[]{:S(2)}, u32[]{:S(2)}) async-start(bf16[16,1056,128]{2,1,0:T(8,128)(2,1)} %bitcast.46), calls=%async_computation.3 | async-start | bytes 8650752 | tf_op jit(solution)/shard_map/all_to_all | solution.py:560
  202.2 3.3 %collective-permute-start.4 = (bf16[512,1536]{1,0:T(8,128)(2,1)}, bf16[512,1536]{1,0:T(8,128)(2,1)}, u32[]{:S(2)}, u32[]{:S(2)}) collective-permute-start(bf16[512,1536]{1,0:T(8,128)(2,1)} %fusion.1.after_in), channel_id=1, source_target_pairs={{0,64},{1,65},{2,66},{3,67},{4,68},{5,69},{6,70},{7,71},{8,72},{9,... | collective-permute-start | bytes 4718600 | tf_op jit(solution)/shard_map/ppermute | solution.py:571
  207.0 3.1 %shard_map.127.after_in.near_ref = f32[512,1536]{1,0:T(8,128)S(1)} custom-call(f32[2,512,1536]{2,1,0:T(8,128)} %shard_map.125.kept_ref, bf16[2,512,1536]{2,1,0:T(8,128)(2,1)} %copy-done.12, bf16[32,528,128]{2,1,0:T(8,128)(2,1)} %all-to-all-done.1.after_ref.packed_ref), custom_call_target="tpu_custom_call" | custom-call | flops 786 | bytes 7864 | tf_op jit(solution)/shard_map/pallas_call | solution.py:499
  210.2 6.1 %shard_map.131 = (bf16[128,2048]{1,0:T(8,128)(2,1)}, f32[8,128]{1,0:T(8,128)}, s32[8,128]{1,0:T(8,128)S(1)}) custom-call(s32[8,128]{1,0:T(8,128)S(1)} %bitcast.39, bf16[8,128]{1,0:T(8,128)(2,1)S(1)} %bitcast.45, bf16[128,2048]{1,0:T(8,128)(2,1)S(1)} %bitcast.34, bf16[32,528,128]{2,1,0:T(8,128)(2,1)} %all-to-all-done.1.after_ref.packed_ref, ...), custom_call_target="tpu_custom_call" | custom-call | flops 1107296 | bytes 5373 | tf_op jit(solution)/shard_map/pallas_call | solution.py:537
  217.1 39.9 %collective-permute-done.2.routes_ref = s32[8,128]{1,0:T(8,128)S(1)} collective-permute-done((s32[8,128]{1,0:T(8,128)S(1)}, s32[8,128]{1,0:T(8,128)S(1)}, u32[]{:S(2)}, u32[]{:S(2)}) %collective-permute-start.2) | collective-permute-done | bytes 4128 | tf_op jit(solution)/shard_map/ppermute | solution.py:566
  259.5 2.7 shard_map.133.refs_0_.after_ref
  265.6 2.9 %shard_map.135 = f32[512,1536]{1,0:T(8,128)} custom-call(f32[512,1536]{1,0:T(8,128)S(1)} %shard_map.127.after_in.near_ref, bf16[512,1536]{1,0:T(8,128)(2,1)} %collective-permute-done.4.far_ref, bf16[128,2048]{1,0:T(8,128)(2,1)S(1)} %shard_map.133.refs_0_.after_ref), custom_call_target="tpu_custom_call" | custom-call | flops 1572 | bytes 7864 | tf_op jit(solution)/shard_map/pallas_call | solution.py:481
  271.1 3.2 %collective-permute-done.3 = bf16[128,2048]{1,0:T(8,128)(2,1)S(1)} collective-permute-done((bf16[128,2048]{1,0:T(8,128)(2,1)S(1)}, bf16[128,2048]{1,0:T(8,128)(2,1)S(1)}, u32[]{:S(2)}, u32[]{:S(2)}) %collective-permute-start.3) | collective-permute-done | bytes 524320 | tf_op jit(solution)/shard_map/ppermute | solution.py:566
  (54 shorter events, 19.1 us)
Async XLA Ops:
  69.1 5.0 %copy-start.13 = (f32[1,1,8,6]{2,1,3,0:T(1,128)S(1)}, f32[1,1,8,6]{2,1,3,0:T(1,128)}, u32[]{:S(2)}) copy-start(f32[1,1,8,6]{2,1,3,0:T(1,128)} %param.14) | copy-start | bytes 580
  69.1 5.1 %copy-start.14 = (f32[1,1,3,8]{3,1,2,0:T(1,128)S(1)}, f32[1,1,3,8]{3,1,2,0:T(1,128)}, u32[]{:S(2)}) copy-start(f32[1,1,3,8]{3,1,2,0:T(1,128)} %param.15) | copy-start | bytes 292
  69.1 8.4 %slice-start = ((s8[4325376]{0:T(1024)(128)(4,1)}), s8[131072]{0:T(1024)(128)(4,1)S(1)}, s32[]{:S(2)}) async-start(s8[4325376]{0:T(1024)(128)(4,1)} %bitcast.31), calls=%async_computation.4 | async-start | bytes 262144
  69.1 63.0 %all-to-all-start.2 = ((bf16[32,528,128]{2,1,0:T(8,128)(2,1)}), bf16[32,528,128]{2,1,0:T(8,128)(2,1)}, u32[]{:S(2)}, u32[]{:S(2)}) async-start(bf16[32,528,128]{2,1,0:T(8,128)(2,1)} %get-tuple-element.20), calls=%async_computation.2 | async-start | bytes 8650752 | tf_op jit(solution)/shard_map/all_to_all | solution.py:552
  74.2 3.3 %slice-start.1 = ((s8[4325376]{0:T(1024)(128)(4,1)}), s8[4194304]{0:T(1024)(128)(4,1)S(1)}, s32[]{:S(2)}) async-start(s8[4325376]{0:T(1024)(128)(4,1)} %bitcast.31), calls=%async_computation.5 | async-start | bytes 8388608
  77.5 23.3 %copy-start = (bf16[768,2048]{1,0:T(8,128)(2,1)}, bf16[768,2048]{1,0:T(8,128)(2,1)S(1)}, u32[]{:S(2)}) copy-start(bf16[768,2048]{1,0:T(8,128)(2,1)S(1)} %shard_map.122.weight_ref) | copy-start | bytes 9437188
  132.1 63.3 %all-to-all-start.1 = ((bf16[32,528,128]{2,1,0:T(8,128)(2,1)}), bf16[32,528,128]{2,1,0:T(8,128)(2,1)}, u32[]{:S(2)}, u32[]{:S(2)}) async-start(bf16[32,528,128]{2,1,0:T(8,128)(2,1)} %shard_map.123.after_ref), calls=%async_computation.1 | async-start | bytes 8650752 | tf_op jit(solution)/shard_map/all_to_all | solution.py:552
  148.2 10.2 %copy-start.3 = (bf16[1056,768]{1,0:T(8,128)(2,1)S(1)}, bf16[1056,768]{1,0:T(8,128)(2,1)}, u32[]{:S(2)}) copy-start(bf16[1056,768]{1,0:T(8,128)(2,1)} %copy-done.2) | copy-start | bytes 4866052
  155.7 22.8 %collective-permute-start = (bf16[2,512,1536]{2,1,0:T(8,128)(2,1)}, bf16[2,512,1536]{2,1,0:T(8,128)(2,1)S(1)}, u32[]{:S(2)}, u32[]{:S(2)}) collective-permute-start(bf16[2,512,1536]{2,1,0:T(8,128)(2,1)} %shard_map.126), channel_id=1, source_target_pairs={{0,32},{1,33},{2,34},{3,35},{4,36},{5,37},{6,38},{7,39},{8,40},{9,... | collective-permute-start | bytes 9437192 | tf_op jit(solution)/shard_map/ppermute | solution.py:571
  163.4 13.8 %collective-permute-start.1 = (bf16[2,768,512]{2,1,0:T(8,128)(2,1)S(1)}, bf16[2,768,512]{2,1,0:T(8,128)(2,1)S(1)}, u32[]{:S(2)}, u32[]{:S(2)}) collective-permute-start(bf16[2,768,512]{2,1,0:T(8,128)(2,1)S(1)} %shard_map.129), channel_id=1, source_target_pairs={{0,32},{1,33},{2,34},{3,35},{4,36},{5,37},{6,38},{7,39},{8,40},{9,... | collective-permute-start | bytes 4718600 | tf_op jit(solution)/shard_map/ppermute | solution.py:571
  168.6 8.5 %copy-start.1 = (f32[2,768,512]{2,1,0:T(8,128)}, f32[2,768,512]{2,1,0:T(8,128)S(1)}, u32[]{:S(2)}) copy-start(f32[2,768,512]{2,1,0:T(8,128)S(1)} %shard_map.128.kept_ref) | copy-start | bytes 9437188
  177.2 6.0 %copy-start.6 = (bf16[2,768,512]{2,1,0:T(8,128)(2,1)}, bf16[2,768,512]{2,1,0:T(8,128)(2,1)S(1)}, u32[]{:S(2)}) copy-start(bf16[2,768,512]{2,1,0:T(8,128)(2,1)S(1)} %collective-permute-done.1.got_ref) | copy-start | bytes 4718596
  178.6 4.6 %copy-start.12 = (bf16[2,512,1536]{2,1,0:T(8,128)(2,1)}, bf16[2,512,1536]{2,1,0:T(8,128)(2,1)S(1)}, u32[]{:S(2)}) copy-start(bf16[2,512,1536]{2,1,0:T(8,128)(2,1)S(1)} %collective-permute-done.got_ref) | copy-start | bytes 9437188
  195.4 10.2 %copy-start.7 = (bf16[2,768,512]{2,1,0:T(8,128)(2,1)S(1)}, bf16[2,768,512]{2,1,0:T(8,128)(2,1)}, u32[]{:S(2)}) copy-start(bf16[2,768,512]{2,1,0:T(8,128)(2,1)} %copy-done.6) | copy-start | bytes 4718596
  195.4 64.1 %all-to-all-start.3 = ((bf16[16,1056,128]{2,1,0:T(8,128)(2,1)}), bf16[16,1056,128]{2,1,0:T(8,128)(2,1)}, u32[]{:S(2)}, u32[]{:S(2)}) async-start(bf16[16,1056,128]{2,1,0:T(8,128)(2,1)} %bitcast.46), calls=%async_computation.3 | async-start | bytes 8650752 | tf_op jit(solution)/shard_map/all_to_all | solution.py:560
  202.2 63.5 %collective-permute-start.4 = (bf16[512,1536]{1,0:T(8,128)(2,1)}, bf16[512,1536]{1,0:T(8,128)(2,1)}, u32[]{:S(2)}, u32[]{:S(2)}) collective-permute-start(bf16[512,1536]{1,0:T(8,128)(2,1)} %fusion.1.after_in), channel_id=1, source_target_pairs={{0,64},{1,65},{2,66},{3,67},{4,68},{5,69},{6,70},{7,71},{8,72},{9,... | collective-permute-start | bytes 4718600 | tf_op jit(solution)/shard_map/ppermute | solution.py:571
  205.4 58.0 %collective-permute-start.5 = (bf16[768,512]{1,0:T(8,128)(2,1)}, bf16[768,512]{1,0:T(8,128)(2,1)}, u32[]{:S(2)}, u32[]{:S(2)}) collective-permute-start(bf16[768,512]{1,0:T(8,128)(2,1)} %fusion.3.after_out), channel_id=1, source_target_pairs={{0,64},{1,65},{2,66},{3,67},{4,68},{5,69},{6,70},{7,71},{8,72},{9,... | collective-permute-start | bytes 2359304 | tf_op jit(solution)/shard_map/ppermute | solution.py:571
  207.0 3.1 %copy-start.4 = (f32[768,512]{1,0:T(8,128)}, f32[768,512]{1,0:T(8,128)S(1)}, u32[]{:S(2)}) copy-start(f32[768,512]{1,0:T(8,128)S(1)} %shard_map.130.after_out.near_ref) | copy-start | bytes 4718596
  207.0 3.1 %copy-start.9 = (bf16[1,128,2048]{2,1,0:T(8,128)(2,1)S(1)}, bf16[1,128,2048]{2,1,0:T(8,128)(2,1)}, u32[]{:S(2)}) copy-start(bf16[1,128,2048]{2,1,0:T(8,128)(2,1)} %param.11) | copy-start | bytes 1572868
  207.0 3.1 %copy-start.10 = (s32[1,128,8]{1,2,0:T(8,128)S(1)}, s32[1,128,8]{1,2,0:T(8,128)}, u32[]{:S(2)}) copy-start(s32[1,128,8]{1,2,0:T(8,128)} %param.9) | copy-start | bytes 12292
  207.0 3.1 %copy-start.11 = (bf16[1,128,8]{1,2,0:T(8,128)(2,1)S(1)}, bf16[1,128,8]{1,2,0:T(8,128)(2,1)}, u32[]{:S(2)}) copy-start(bf16[1,128,8]{1,2,0:T(8,128)(2,1)} %param.10) | copy-start | bytes 6148
  216.2 40.8 %collective-permute-start.2 = (s32[8,128]{1,0:T(8,128)S(1)}, s32[8,128]{1,0:T(8,128)S(1)}, u32[]{:S(2)}, u32[]{:S(2)}) collective-permute-start(s32[8,128]{1,0:T(8,128)S(1)} %get-tuple-element.27), channel_id=1, source_target_pairs={{0,1},{1,0},{2,3},{3,2},{4,5},{5,4},{6,7},{7,6},{8,9},{9,8},{10,11... | collective-permute-start | bytes 12296 | tf_op jit(solution)/shard_map/ppermute | solution.py:566
  259.5 4.0 %copy-start.5 = (f32[768,512]{1,0:T(8,128)S(1)}, f32[768,512]{1,0:T(8,128)}, u32[]{:S(2)}) copy-start(f32[768,512]{1,0:T(8,128)} %copy-done.4) | copy-start | bytes 4718596
  262.1 12.2 %collective-permute-start.3 = (bf16[128,2048]{1,0:T(8,128)(2,1)S(1)}, bf16[128,2048]{1,0:T(8,128)(2,1)S(1)}, u32[]{:S(2)}, u32[]{:S(2)}) collective-permute-start(bf16[128,2048]{1,0:T(8,128)(2,1)S(1)} %shard_map.133.refs_0_.after_ref), channel_id=1, source_target_pairs={{0,1},{1,0},{2,3},{3,2},{4,5},{5,4},{6,7},{7,6},{8,9},{9,8},{10,11... | collective-permute-start | bytes 1572872 | tf_op jit(solution)/shard_map/ppermute | solution.py:566
  (2 other events, 3.0 us)
